TPU v7x, 32 devices: a whole 2x2x4 slice. The times are simulated.
32 devices in a mesh: bank: 4 (over y, x), seg: 8 (over z, core).
Axes of the slice: x: 2, y: 2, z: 4, core: 2. Of those that a mesh axis runs over, the one named last changes fastest.
Arguments:
- strain: bfloat16 [1024, 2, 4096], P(('bank', 'seg')), may hold values from -6 to 6
- templates: float32 [12, 2, 4096], P('bank'), may hold values from -2 to 2
- inv_psd: float32 [2, 2048], replicated, may hold values from 0.2 to 5
- seg_blocks: int32 [4, 8], P('bank'), may hold values from 1 to 32, 128 in all within a row
- dest_order: int32 [4, 8], P('bank'), may hold values from 0 to 7, each once within a row
- bin_edges: int32 [12, 9], replicated, may hold values from 0 to 2048, as said below
Outputs:
- peak_snr: float32 [512, 12], P(('bank', 'seg'))
- chisq_mean: float32 [512, 12], P(('bank', 'seg'))
Inputs may be any that keep to these rules, and one draw needn't show every extreme that they name: `seg_blocks`: each row sums to 128. `dest_order`: each row holds every seg index once. `bin_edges`: each row rises strictly from 0 to 2048.
All inputs are finite; a program needn't handle non-finite values.
Results may differ from a plain program's by a relative error of at most 0.0014.
Values may be sent and summed in bfloat16 or wider, within the bound.
No kernel may reach another device: no remote copies, remote signals or barrier semaphores. Data moves between devices by JAX's collectives and lax.ppermute only.
A program may use at most 64 MiB of HBM per device.

v0:
```python
import math

import jax
import jax.numpy as jnp
from jax import lax
from jax.sharding import PartitionSpec as P

TIME_LAGS = 64
BLK_DEV = 16


def dft_table(freq_count, lag_count):
    frequency = jnp.arange(freq_count, dtype=jnp.int32)
    lag_ids = jnp.arange(lag_count, dtype=jnp.int32)
    turns = frequency[:, None] * lag_ids[None, :] % (2 * freq_count)
    angle = turns.astype(jnp.float32) * (math.pi / freq_count)
    cosine = jnp.cos(angle)
    sine = jnp.sin(angle)
    upper = jnp.concatenate([cosine, sine], axis=1)
    lower = jnp.concatenate([-sine, cosine], axis=1)
    return jnp.concatenate([upper, lower], axis=0).astype(jnp.bfloat16)


def filter_core(blocks, templates, edge_rows, inv_psd, dft_rows):
    freq_count = inv_psd.shape[1]
    lag_count = dft_rows.shape[1] // 2
    bin_count = edge_rows.shape[1] - 1
    block_count = blocks.shape[0]
    tmpl_count = templates.shape[0]
    detectors = inv_psd.shape[0]
    spectra = blocks.astype(jnp.float32)
    strain_re = spectra[:, None, :, :freq_count]
    strain_im = spectra[:, None, :, freq_count:]
    tmpl_re = templates[None, :, :, :freq_count]
    tmpl_im = templates[None, :, :, freq_count:]
    weights = inv_psd[None, None]
    prod_re = (tmpl_re * strain_re + tmpl_im * strain_im) * weights
    prod_im = (tmpl_re * strain_im - tmpl_im * strain_re) * weights
    frequency = jnp.arange(freq_count, dtype=jnp.int32)
    member = (
        (frequency[None, None, :] >= edge_rows[:, :-1, None])
        & (frequency[None, None, :] < edge_rows[:, 1:, None])
    ).astype(jnp.float32)
    bin_mask = member[None, :, None]
    masked = jnp.concatenate(
        [prod_re[:, :, :, None, :] * bin_mask, prod_im[:, :, :, None, :] * bin_mask], axis=-1
    ).astype(jnp.bfloat16)
    flattened = masked.reshape(-1, 2 * freq_count)
    bin_series = lax.dot_general(
        dft_rows, flattened, (((0,), (1,)), ((), ())), preferred_element_type=jnp.float32
    )
    bin_series = bin_series.reshape(2 * lag_count, block_count, tmpl_count, detectors, bin_count)
    part_re = bin_series[:lag_count]
    part_im = bin_series[lag_count:]
    tmpl_power = (templates[..., :freq_count] ** 2 + templates[..., freq_count:] ** 2) * inv_psd[
        None
    ]
    sigma_part = jnp.einsum("tdf,tpf->tdp", tmpl_power, member, precision=lax.Precision.HIGHEST)
    sigma_total = jnp.sum(sigma_part, axis=-1)
    whole_re = jnp.sum(part_re, axis=-1)
    whole_im = jnp.sum(part_im, axis=-1)
    snr_power = jnp.sum((whole_re**2 + whole_im**2) / sigma_total, axis=-1)
    peak_rows = jnp.sqrt(jnp.max(snr_power, axis=0))
    fraction = sigma_part / sigma_total[..., None]
    dev_re = part_re - fraction * whole_re[..., None]
    dev_im = part_im - fraction * whole_im[..., None]
    chi_terms = jnp.sum((dev_re**2 + dev_im**2) / sigma_part, axis=(-2, -1))
    chi_sums = jnp.mean(chi_terms, axis=0) / (2.0 * detectors * (bin_count - 1))
    return (peak_rows, chi_sums)


def routing(seg_blocks, dest_order, capacity, per_device):
    seg_count = lax.axis_size("seg")
    seg_here = lax.axis_index("seg")
    seg_counts = seg_blocks[0]
    starts = jnp.cumsum(seg_counts) - seg_counts
    seg_ids = jnp.arange(seg_count, dtype=jnp.int32)
    residue = jnp.sum(
        jnp.where(dest_order[0][:, None] == seg_ids[None, :], seg_ids[:, None], 0), axis=0
    )
    pair_slots = -(-capacity // seg_count)
    pair_ids = jnp.arange(pair_slots, dtype=jnp.int32)
    offsets = (residue - starts[seg_here]) % seg_count
    send_slot = pair_ids[None, :] * seg_count + offsets[:, None]
    live_mask = send_slot < seg_counts[seg_here]
    send_slot = jnp.minimum(send_slot, capacity - 1).reshape(-1)
    global_ids = residue[seg_here] + jnp.arange(per_device, dtype=jnp.int32) * seg_count
    anchor = jnp.sum((starts[None, :] <= global_ids[:, None]).astype(jnp.int32), axis=1) - 1
    pick_index = anchor * pair_slots + (global_ids - starts[anchor]) // seg_count
    return (send_slot, live_mask.reshape(-1), pick_index, pair_slots)


def filter_all(blocks, templates, inv_psd, bin_edges, dft_rows):
    block_count = blocks.shape[0]
    block_group = math.gcd(block_count, 16)
    grouped = blocks.reshape((block_count // block_group, block_group) + blocks.shape[1:])
    piece = lax.all_gather(templates, "bank", axis=0, tiled=True)
    piece_count = piece.shape[0]
    tmpl_group = math.gcd(piece_count, 4)
    tmpl_sets = piece.reshape((piece_count // tmpl_group, tmpl_group) + piece.shape[1:])
    edge_sets = bin_edges.reshape(piece_count // tmpl_group, tmpl_group, bin_edges.shape[1])

    def per_templates(tmpl_pair):

        def per_blocks(block_set):
            return filter_core(block_set, tmpl_pair[0], tmpl_pair[1], inv_psd, dft_rows)

        peak_rows, chi_sums = lax.map(per_blocks, grouped)
        return (
            peak_rows.reshape(block_count, tmpl_group),
            chi_sums.reshape(block_count, tmpl_group),
        )

    peak_rows, chi_sums = lax.map(per_templates, (tmpl_sets, edge_sets))
    peak_rows = jnp.transpose(peak_rows, (1, 0, 2)).reshape(block_count, piece_count)
    chi_sums = jnp.transpose(chi_sums, (1, 0, 2)).reshape(block_count, piece_count)
    return (peak_rows, chi_sums)


def body(strain, templates, inv_psd, seg_blocks, dest_order, bin_edges):
    capacity = strain.shape[0]
    seg_count = lax.axis_size("seg")
    tmpl_total = bin_edges.shape[0]
    send_slot, live_mask, pick_index, pair_slots = routing(
        seg_blocks, dest_order, capacity, BLK_DEV
    )
    dft_rows = dft_table(inv_psd.shape[1], TIME_LAGS)
    peak_all, chisq_all = filter_all(strain, templates, inv_psd, bin_edges, dft_rows)
    peak_out = jnp.where(live_mask[:, None], peak_all[send_slot], 0.0).reshape(
        seg_count, pair_slots, tmpl_total
    )
    chisq_out = jnp.where(live_mask[:, None], chisq_all[send_slot], 0.0).reshape(
        seg_count, pair_slots, tmpl_total
    )
    peak_in, chisq_in = (
        lax.all_to_all(peak_out, "seg", split_axis=0, concat_axis=0, tiled=True),
        lax.all_to_all(chisq_out, "seg", split_axis=0, concat_axis=0, tiled=True),
    )
    peak_snr = peak_in.reshape(seg_count * pair_slots, tmpl_total)[pick_index]
    chisq_mean = chisq_in.reshape(seg_count * pair_slots, tmpl_total)[pick_index]
    return (peak_snr, chisq_mean)


def solution(mesh):
    return jax.shard_map(
        body,
        mesh=mesh,
        in_specs=(
            P(("bank", "seg"), None, None),
            P("bank", None, None),
            P(),
            P("bank", None),
            P("bank", None),
            P(),
        ),
        out_specs=(P(("bank", "seg"), None), P(("bank", "seg"), None)),
        check_vma=False,
    )
```

profile of v0, /device:TPU:0, one launch (start us, length us, event | category | flops | bytes accessed | tf_op | source)
XLA Modules:
  0.0 116.1 jit_solution(12982432212267981192)
XLA Ops:
  0.7 4.4 %negate_convert_fusion = (bf16[2048,64]{1,0:T(8,128)(2,1)S(1)}, bf16[2048,64]{1,0:T(8,128)(2,1)S(1)}) fusion(), kind=kLoop, calls=%fused_computation.50 | loop fusion | flops 2228224 | bytes 524288 | tf_op jit(solution)/shard_map/convert.7
  5.1 4.0 %fusion.28 = bf16[2048,64]{1,0:T(8,128)(2,1)S(1)} fusion(), kind=kLoop, calls=%fused_computation.56 | loop fusion | flops 1966080 | bytes 262144 | tf_op jit(solution)/shard_map/convert.10
  9.0 0.5 iota_multiply_fusion
  9.6 11.3 %all_gather.3 = f32[12,2,4096]{2,1,0:T(2,128)S(1)} all-gather(f32[3,2,4096]{2,1,0:T(2,128)} %param.11), channel_id=1, replica_groups=mesh['bank'=4,'seg'=8] {'bank'}, dimensions={0}, use_global_device_ids=true | all-gather | bytes 491520 | tf_op jit(solution)/shard_map/all_gather | solution.py:97
  20.8 0.7 reshape.356
  21.6 1.6 %maximum_maximum_fusion = bf16[4096,128]{1,0:T(8,128)(2,1)} fusion(bf16[2048,64]{1,0:T(8,128)(2,1)S(1)} %get-tuple-element.381, bf16[2048,64]{1,0:T(8,128)(2,1)S(1)} %get-tuple-element.380, bf16[2048,64]{1,0:T(8,128)(2,1)S(1)} %fusion.28), kind=kLoop, calls=%fused_computation.49 | loop fusion | flops 4194304 | bytes 1835008 | tf_op jit(solution)/shard_map/concatenate | solution.py:21
  23.1 67.2 %while.41 = (s32[]{:T(128)}, f32[3,32,4]{1,2,0:T(4,128)S(1)}, f32[3,32,4]{1,2,0:T(4,128)S(1)}, f32[3,4,2,4096]{3,2,1,0:T(2,128)S(1)}, s32[3,4,9]{2,1,0:T(4,128)S...) while((s32[]{:T(128)}, f32[3,32,4]{1,2,0:T(4,128)S(1)}, ...), condition=%wide.region_12.13_spmd, body=%wide.region_2.12_spmd.sunk | while | flops 1103978496 | bytes 31786048 | solution.py:114
  23.3 0.6 fusion.55
  23.8 21.6 %while.42 = (s32[]{:T(128)}, f32[2,16,4]{1,0,2:T(2,128)S(1)}, f32[2,16,4]{1,0,2:T(2,128)S(1)}, f32[4,2,4096]{2,1,0:T(2,128)S(1)}, bf16[2,16,2,4096]{3,2,1,0:T(2,...) while((s32[]{:T(128)}, f32[2,16,4]{1,0,2:T(2,128)S(1)}, ...), condition=%wide.region_11.11_spmd, body=%wide.region_4.10_spmd.sunk | while | flops 1102143488 | bytes 31364576 | solution.py:108
  24.0 0.2 bitcast_convert_fusion.2
  24.3 1.2 %add_multiply_fusion.2 = (f32[16,4,2,2048]{3,2,1,0:T(2,128)S(1)}, f32[16,4,2,2048]{3,2,1,0:T(2,128)S(1)}) fusion(f32[2,2048]{1,0:T(2,128)S(1)} %get-tuple-element.590, f32[16,2,2048]{2,1,0:T(2,128)S(1)} %get-tuple-element.545, f32[4,2,2048]{2,1,0:T(2,128)S(1)} %get-tuple-element.546, f32[16,2,2048]{2,1,0:T(2,128)S(1)} %get-tuple-element.547, ...), kind=kLoop, calls=%fused_computation.13.clone.1 | loop fusion | flops 2097152 | bytes 2768896 | tf_op jit(solution)/shard_map/while/body/eval_jaxpr/while/body/eval_jaxpr/mul | solution.py:37
  25.5 2.2 %multiply_convert_fusion.3 = (bf16[16,4,2,8,2048]{4,3,2,1,0:T(8,128)(2,1)S(1)}, bf16[16,4,2,8,2048]{4,3,2,1,0:T(8,128)(2,1)S(1)}) fusion(f32[4,8,2048]{2,1,0:T(8,128)S(1)} %fusion.59, f32[16,4,2,2048]{3,2,1,0:T(2,128)S(1)} %get-tuple-element.549, f32[16,4,2,2048]{3,2,1,0:T(2,128)S(1)} %get-tuple-element.550), kind=kLoop, calls=%fused_computation.10.clone.1 | loop fusion | flops 8388608 | bytes 10747904 | tf_op jit(solution)/shard_map/convert.4
  27.8 4.1 %fusion.62 = f32[128,1024]{1,0:T(8,128)S(1)} fusion(bf16[4096,128]{1,0:T(8,128)(2,1)} %get-tuple-element.592, bf16[1024,2048]{1,0:T(8,128)(2,1)S(1)} %bitcast.99, bf16[1024,2048]{1,0:T(8,128)(2,1)S(1)} %bitcast.98), kind=kOutput, calls=%fused_computation.11.clone.1 | convolution fusion | flops 1090519040 | bytes 9961472 | tf_op jit(solution)/shard_map/while/body/eval_jaxpr/while/body/eval_jaxpr/dot_general | solution.py:49
  32.2 0.2 copy.73
  32.4 0.4 bitcast_reduce_fusion.3
  34.8 0.2 bitcast_convert_fusion.2
  35.1 1.2 %add_multiply_fusion.2 = (f32[16,4,2,2048]{3,2,1,0:T(2,128)S(1)}, f32[16,4,2,2048]{3,2,1,0:T(2,128)S(1)}) fusion(f32[2,2048]{1,0:T(2,128)S(1)} %get-tuple-element.590, f32[16,2,2048]{2,1,0:T(2,128)S(1)} %get-tuple-element.545, f32[4,2,2048]{2,1,0:T(2,128)S(1)} %get-tuple-element.546, f32[16,2,2048]{2,1,0:T(2,128)S(1)} %get-tuple-element.547, ...), kind=kLoop, calls=%fused_computation.13.clone.1 | loop fusion | flops 2097152 | bytes 2768896 | tf_op jit(solution)/shard_map/while/body/eval_jaxpr/while/body/eval_jaxpr/mul | solution.py:37
  36.3 2.2 %multiply_convert_fusion.3 = (bf16[16,4,2,8,2048]{4,3,2,1,0:T(8,128)(2,1)S(1)}, bf16[16,4,2,8,2048]{4,3,2,1,0:T(8,128)(2,1)S(1)}) fusion(f32[4,8,2048]{2,1,0:T(8,128)S(1)} %fusion.59, f32[16,4,2,2048]{3,2,1,0:T(2,128)S(1)} %get-tuple-element.549, f32[16,4,2,2048]{3,2,1,0:T(2,128)S(1)} %get-tuple-element.550), kind=kLoop, calls=%fused_computation.10.clone.1 | loop fusion | flops 8388608 | bytes 10747904 | tf_op jit(solution)/shard_map/convert.4
  38.6 4.1 %fusion.62 = f32[128,1024]{1,0:T(8,128)S(1)} fusion(bf16[4096,128]{1,0:T(8,128)(2,1)} %get-tuple-element.592, bf16[1024,2048]{1,0:T(8,128)(2,1)S(1)} %bitcast.99, bf16[1024,2048]{1,0:T(8,128)(2,1)S(1)} %bitcast.98), kind=kOutput, calls=%fused_computation.11.clone.1 | convolution fusion | flops 1090519040 | bytes 9961472 | tf_op jit(solution)/shard_map/while/body/eval_jaxpr/while/body/eval_jaxpr/dot_general | solution.py:49
  43.0 0.2 copy.73
  43.2 0.4 bitcast_reduce_fusion.3
  45.7 0.6 fusion.55
  46.2 21.6 %while.42 = (s32[]{:T(128)}, f32[2,16,4]{1,0,2:T(2,128)S(1)}, f32[2,16,4]{1,0,2:T(2,128)S(1)}, f32[4,2,4096]{2,1,0:T(2,128)S(1)}, bf16[2,16,2,4096]{3,2,1,0:T(2,...) while((s32[]{:T(128)}, f32[2,16,4]{1,0,2:T(2,128)S(1)}, ...), condition=%wide.region_11.11_spmd, body=%wide.region_4.10_spmd.sunk | while | flops 1102143488 | bytes 31364576 | solution.py:108
  46.4 0.2 bitcast_convert_fusion.2
  46.7 1.2 %add_multiply_fusion.2 = (f32[16,4,2,2048]{3,2,1,0:T(2,128)S(1)}, f32[16,4,2,2048]{3,2,1,0:T(2,128)S(1)}) fusion(f32[2,2048]{1,0:T(2,128)S(1)} %get-tuple-element.590, f32[16,2,2048]{2,1,0:T(2,128)S(1)} %get-tuple-element.545, f32[4,2,2048]{2,1,0:T(2,128)S(1)} %get-tuple-element.546, f32[16,2,2048]{2,1,0:T(2,128)S(1)} %get-tuple-element.547, ...), kind=kLoop, calls=%fused_computation.13.clone.1 | loop fusion | flops 2097152 | bytes 2768896 | tf_op jit(solution)/shard_map/while/body/eval_jaxpr/while/body/eval_jaxpr/mul | solution.py:37
  47.9 2.2 %multiply_convert_fusion.3 = (bf16[16,4,2,8,2048]{4,3,2,1,0:T(8,128)(2,1)S(1)}, bf16[16,4,2,8,2048]{4,3,2,1,0:T(8,128)(2,1)S(1)}) fusion(f32[4,8,2048]{2,1,0:T(8,128)S(1)} %fusion.59, f32[16,4,2,2048]{3,2,1,0:T(2,128)S(1)} %get-tuple-element.549, f32[16,4,2,2048]{3,2,1,0:T(2,128)S(1)} %get-tuple-element.550), kind=kLoop, calls=%fused_computation.10.clone.1 | loop fusion | flops 8388608 | bytes 10747904 | tf_op jit(solution)/shard_map/convert.4
  50.2 4.1 %fusion.62 = f32[128,1024]{1,0:T(8,128)S(1)} fusion(bf16[4096,128]{1,0:T(8,128)(2,1)} %get-tuple-element.592, bf16[1024,2048]{1,0:T(8,128)(2,1)S(1)} %bitcast.99, bf16[1024,2048]{1,0:T(8,128)(2,1)S(1)} %bitcast.98), kind=kOutput, calls=%fused_computation.11.clone.1 | convolution fusion | flops 1090519040 | bytes 9961472 | tf_op jit(solution)/shard_map/while/body/eval_jaxpr/while/body/eval_jaxpr/dot_general | solution.py:49
  54.8 0.4 bitcast_reduce_fusion.3
  57.2 0.2 bitcast_convert_fusion.2
  57.5 1.2 %add_multiply_fusion.2 = (f32[16,4,2,2048]{3,2,1,0:T(2,128)S(1)}, f32[16,4,2,2048]{3,2,1,0:T(2,128)S(1)}) fusion(f32[2,2048]{1,0:T(2,128)S(1)} %get-tuple-element.590, f32[16,2,2048]{2,1,0:T(2,128)S(1)} %get-tuple-element.545, f32[4,2,2048]{2,1,0:T(2,128)S(1)} %get-tuple-element.546, f32[16,2,2048]{2,1,0:T(2,128)S(1)} %get-tuple-element.547, ...), kind=kLoop, calls=%fused_computation.13.clone.1 | loop fusion | flops 2097152 | bytes 2768896 | tf_op jit(solution)/shard_map/while/body/eval_jaxpr/while/body/eval_jaxpr/mul | solution.py:37
  58.7 2.2 %multiply_convert_fusion.3 = (bf16[16,4,2,8,2048]{4,3,2,1,0:T(8,128)(2,1)S(1)}, bf16[16,4,2,8,2048]{4,3,2,1,0:T(8,128)(2,1)S(1)}) fusion(f32[4,8,2048]{2,1,0:T(8,128)S(1)} %fusion.59, f32[16,4,2,2048]{3,2,1,0:T(2,128)S(1)} %get-tuple-element.549, f32[16,4,2,2048]{3,2,1,0:T(2,128)S(1)} %get-tuple-element.550), kind=kLoop, calls=%fused_computation.10.clone.1 | loop fusion | flops 8388608 | bytes 10747904 | tf_op jit(solution)/shard_map/convert.4
  61.0 4.1 %fusion.62 = f32[128,1024]{1,0:T(8,128)S(1)} fusion(bf16[4096,128]{1,0:T(8,128)(2,1)} %get-tuple-element.592, bf16[1024,2048]{1,0:T(8,128)(2,1)S(1)} %bitcast.99, bf16[1024,2048]{1,0:T(8,128)(2,1)S(1)} %bitcast.98), kind=kOutput, calls=%fused_computation.11.clone.1 | convolution fusion | flops 1090519040 | bytes 9961472 | tf_op jit(solution)/shard_map/while/body/eval_jaxpr/while/body/eval_jaxpr/dot_general | solution.py:49
  65.4 0.2 copy.73
  65.6 0.4 bitcast_reduce_fusion.3
  68.1 0.6 fusion.55
  68.6 21.6 %while.42 = (s32[]{:T(128)}, f32[2,16,4]{1,0,2:T(2,128)S(1)}, f32[2,16,4]{1,0,2:T(2,128)S(1)}, f32[4,2,4096]{2,1,0:T(2,128)S(1)}, bf16[2,16,2,4096]{3,2,1,0:T(2,...) while((s32[]{:T(128)}, f32[2,16,4]{1,0,2:T(2,128)S(1)}, ...), condition=%wide.region_11.11_spmd, body=%wide.region_4.10_spmd.sunk | while | flops 1102143488 | bytes 31364576 | solution.py:108
  68.8 0.2 bitcast_convert_fusion.2
  69.1 1.2 %add_multiply_fusion.2 = (f32[16,4,2,2048]{3,2,1,0:T(2,128)S(1)}, f32[16,4,2,2048]{3,2,1,0:T(2,128)S(1)}) fusion(f32[2,2048]{1,0:T(2,128)S(1)} %get-tuple-element.590, f32[16,2,2048]{2,1,0:T(2,128)S(1)} %get-tuple-element.545, f32[4,2,2048]{2,1,0:T(2,128)S(1)} %get-tuple-element.546, f32[16,2,2048]{2,1,0:T(2,128)S(1)} %get-tuple-element.547, ...), kind=kLoop, calls=%fused_computation.13.clone.1 | loop fusion | flops 2097152 | bytes 2768896 | tf_op jit(solution)/shard_map/while/body/eval_jaxpr/while/body/eval_jaxpr/mul | solution.py:37
  70.3 2.2 %multiply_convert_fusion.3 = (bf16[16,4,2,8,2048]{4,3,2,1,0:T(8,128)(2,1)S(1)}, bf16[16,4,2,8,2048]{4,3,2,1,0:T(8,128)(2,1)S(1)}) fusion(f32[4,8,2048]{2,1,0:T(8,128)S(1)} %fusion.59, f32[16,4,2,2048]{3,2,1,0:T(2,128)S(1)} %get-tuple-element.549, f32[16,4,2,2048]{3,2,1,0:T(2,128)S(1)} %get-tuple-element.550), kind=kLoop, calls=%fused_computation.10.clone.1 | loop fusion | flops 8388608 | bytes 10747904 | tf_op jit(solution)/shard_map/convert.4
  72.6 4.1 %fusion.62 = f32[128,1024]{1,0:T(8,128)S(1)} fusion(bf16[4096,128]{1,0:T(8,128)(2,1)} %get-tuple-element.592, bf16[1024,2048]{1,0:T(8,128)(2,1)S(1)} %bitcast.99, bf16[1024,2048]{1,0:T(8,128)(2,1)S(1)} %bitcast.98), kind=kOutput, calls=%fused_computation.11.clone.1 | convolution fusion | flops 1090519040 | bytes 9961472 | tf_op jit(solution)/shard_map/while/body/eval_jaxpr/while/body/eval_jaxpr/dot_general | solution.py:49
  77.2 0.4 bitcast_reduce_fusion.3
  79.6 0.2 bitcast_convert_fusion.2
  79.9 1.2 %add_multiply_fusion.2 = (f32[16,4,2,2048]{3,2,1,0:T(2,128)S(1)}, f32[16,4,2,2048]{3,2,1,0:T(2,128)S(1)}) fusion(f32[2,2048]{1,0:T(2,128)S(1)} %get-tuple-element.590, f32[16,2,2048]{2,1,0:T(2,128)S(1)} %get-tuple-element.545, f32[4,2,2048]{2,1,0:T(2,128)S(1)} %get-tuple-element.546, f32[16,2,2048]{2,1,0:T(2,128)S(1)} %get-tuple-element.547, ...), kind=kLoop, calls=%fused_computation.13.clone.1 | loop fusion | flops 2097152 | bytes 2768896 | tf_op jit(solution)/shard_map/while/body/eval_jaxpr/while/body/eval_jaxpr/mul | solution.py:37
  81.1 2.2 %multiply_convert_fusion.3 = (bf16[16,4,2,8,2048]{4,3,2,1,0:T(8,128)(2,1)S(1)}, bf16[16,4,2,8,2048]{4,3,2,1,0:T(8,128)(2,1)S(1)}) fusion(f32[4,8,2048]{2,1,0:T(8,128)S(1)} %fusion.59, f32[16,4,2,2048]{3,2,1,0:T(2,128)S(1)} %get-tuple-element.549, f32[16,4,2,2048]{3,2,1,0:T(2,128)S(1)} %get-tuple-element.550), kind=kLoop, calls=%fused_computation.10.clone.1 | loop fusion | flops 8388608 | bytes 10747904 | tf_op jit(solution)/shard_map/convert.4
  83.4 4.1 %fusion.62 = f32[128,1024]{1,0:T(8,128)S(1)} fusion(bf16[4096,128]{1,0:T(8,128)(2,1)} %get-tuple-element.592, bf16[1024,2048]{1,0:T(8,128)(2,1)S(1)} %bitcast.99, bf16[1024,2048]{1,0:T(8,128)(2,1)S(1)} %bitcast.98), kind=kOutput, calls=%fused_computation.11.clone.1 | convolution fusion | flops 1090519040 | bytes 9961472 | tf_op jit(solution)/shard_map/while/body/eval_jaxpr/while/body/eval_jaxpr/dot_general | solution.py:49
  87.8 0.2 copy.73
  88.0 0.4 bitcast_reduce_fusion.3
  90.8 0.7 constant_dynamic-slice_fusion
  91.4 0.6 dynamic_slice.32
  92.0 0.7 and_select_fusion.1
  92.8 0.8 add_compare_fusion
  93.7 0.6 gather_fusion.3
  94.3 0.6 gather_fusion
  94.8 0.7 broadcast_select_fusion
  95.5 4.9 %all-to-all-start = ((f32[8,4,12]{2,1,0:T(4,128)}), f32[8,4,12]{2,1,0:T(4,128)S(1)}, u32[]{:S(2)}, u32[]{:S(2)}) async-start(f32[8,4,12]{2,1,0:T(4,128)} %get-tuple-element.379), calls=%async_computation | async-start | bytes 32768 | tf_op jit(solution)/shard_map/all_to_all | solution.py:136
  100.4 0.6 dynamic_slice.34
  101.0 0.6 multiply_add_fusion
  101.8 0.7 gather_fusion.1
  102.4 0.7 fusion.32
  103.1 3.0 %all-to-all-done = f32[8,4,12]{2,1,0:T(4,128)S(1)} async-done(((f32[8,4,12]{2,1,0:T(4,128)}), f32[8,4,12]{2,1,0:T(4,128)S(1)}, u32[]{:S(2)}, u32[]{:S(2)}) %all-to-all-start) | async-done | bytes 1568 | tf_op jit(solution)/shard_map/all_to_all | solution.py:136
  106.1 3.3 %all-to-all-start.1 = ((f32[8,4,12]{2,1,0:T(4,128)}), f32[8,4,12]{2,1,0:T(4,128)S(1)}, u32[]{:S(2)}, u32[]{:S(2)}) async-start(f32[8,4,12]{2,1,0:T(4,128)} %get-tuple-element.378), calls=%async_computation.1 | async-start | bytes 32768 | tf_op jit(solution)/shard_map/all_to_all | solution.py:137
  109.4 1.2 gather_fusion.2
  110.6 4.4 %all-to-all-done.1 = f32[8,4,12]{2,1,0:T(4,128)S(1)} async-done(((f32[8,4,12]{2,1,0:T(4,128)}), f32[8,4,12]{2,1,0:T(4,128)S(1)}, u32[]{:S(2)}, u32[]{:S(2)}) %all-to-all-start.1) | async-done | bytes 1568 | tf_op jit(solution)/shard_map/all_to_all | solution.py:137
  115.0 1.2 gather_fusion.4
  (210 shorter events, 15.4 us)
Async XLA Ops:
  0.6 22.5 %copy-start.1 = (f32[2,2048]{1,0:T(2,128)S(1)}, f32[2,2048]{1,0:T(2,128)}, u32[]{:S(2)}) copy-start(f32[2,2048]{1,0:T(2,128)} %param.12) | copy-start | bytes 49156
  0.6 22.5 %copy-start = (bf16[32,2,4096]{2,1,0:T(2,128)(2,1)S(1)}, bf16[32,2,4096]{2,1,0:T(2,128)(2,1)}, u32[]{:S(2)}) copy-start(bf16[32,2,4096]{2,1,0:T(2,128)(2,1)} %param.10) | copy-start | bytes 1572868
  23.1 67.4 %copy-start.3 = (s32[1,8]{1,0:T(1,128)S(1)}, s32[1,8]{1,0:T(1,128)}, u32[]{:S(2)}) copy-start(s32[1,8]{1,0:T(1,128)} %param.14) | copy-start | bytes 100
  23.1 67.4 %copy-start.4 = (s32[1,8]{1,0:T(1,128)S(1)}, s32[1,8]{1,0:T(1,128)}, u32[]{:S(2)}) copy-start(s32[1,8]{1,0:T(1,128)} %param.13) | copy-start | bytes 100
  23.1 69.5 %copy-start.2 = (s32[4]{0:T(128)S(1)}, s32[4]{0:T(128)}, u32[]{:S(2)}) copy-start(s32[4]{0:T(128)} %iota_multiply_fusion) | copy-start | bytes 52
  95.5 10.5 %all-to-all-start = ((f32[8,4,12]{2,1,0:T(4,128)}), f32[8,4,12]{2,1,0:T(4,128)S(1)}, u32[]{:S(2)}, u32[]{:S(2)}) async-start(f32[8,4,12]{2,1,0:T(4,128)} %get-tuple-element.379), calls=%async_computation | async-start | bytes 32768 | tf_op jit(solution)/shard_map/all_to_all | solution.py:136
  106.1 8.9 %all-to-all-start.1 = ((f32[8,4,12]{2,1,0:T(4,128)}), f32[8,4,12]{2,1,0:T(4,128)S(1)}, u32[]{:S(2)}, u32[]{:S(2)}) async-start(f32[8,4,12]{2,1,0:T(4,128)} %get-tuple-element.378), calls=%async_computation.1 | async-start | bytes 32768 | tf_op jit(solution)/shard_map/all_to_all | solution.py:137
where the time goes:
time: 117 us; the launch traced here: 116 us
  other arithmetic  43.1 us (37%)
  matrix products  26.5 us (23%)
  local copies, waits for them, and re-layouts  17.8 us (15%)
  blocking collectives  11.3 us (10%)
  starting transfers between devices  8.22 us (7%)
  waiting for transfers between devices  7.4 us (6%)
    dot_general x6, matrix products, filter_core(): lax.dot_general(dft_rows, flattened, (((0,), (1,)), ((), ())), preferred_...  24.8 us
    another operation x17, other arithmetic  22 us
    all_gather x1, blocking collectives, filter_all(): piece = lax.all_gather(templates, 'bank', axis=0, tiled=True)  11.3 us
    mul x6, other arithmetic, filter_core(): prod_re = (tmpl_re * strain_re + tmpl_im * strain_im) * weights  7.17 us
    all_to_all x1, starting transfers between devices, body(): lax.all_to_all(peak_out, 'seg', split_axis=0, concat_axis=0, tiled=True)  4.88 us
    all_to_all x1, waiting for transfers between devices, body(): lax.all_to_all(chisq_out, 'seg', split_axis=0, concat_axis=0, tiled=True)  4.42 us
    all_to_all x1, starting transfers between devices, body(): lax.all_to_all(chisq_out, 'seg', split_axis=0, concat_axis=0, tiled=True)  3.33 us
    all_to_all x1, waiting for transfers between devices, body(): lax.all_to_all(peak_out, 'seg', split_axis=0, concat_axis=0, tiled=True)  2.98 us
  transfers between devices with their start and end apart: 2, of which 2 were waited for; matrix products, arithmetic and copies ran while one was open for 3% of the time, Pallas kernels for 0%

commit v1 on v0

v1 whole, which is shorter than its diff:
```python
import functools

import jax
import jax.numpy as jnp
import ml_dtypes
import numpy as np
from jax import lax
from jax.experimental import pallas as pl
from jax.experimental.pallas import tpu as pltpu
from jax.sharding import PartitionSpec as P

TIME_LAGS = 64
BLK_DEV = 16
CHUNK = 128
LANES = 128
VMEM = pl.BlockSpec(memory_space=pltpu.VMEM)
SMEM = pl.BlockSpec(memory_space=pltpu.SMEM)


def dft_chunks(freq_count):
    turns = np.arange(freq_count)[:, None] * np.arange(TIME_LAGS)[None, :] % (2 * freq_count)
    angle = turns * (np.pi / freq_count)
    cosine, sine = np.cos(angle), np.sin(angle)
    upper = np.concatenate([cosine, sine], axis=1).reshape(-1, CHUNK, 2 * TIME_LAGS)
    lower = np.concatenate([-sine, cosine], axis=1).reshape(-1, CHUNK, 2 * TIME_LAGS)
    return np.concatenate([upper, lower], axis=1).astype(np.float32).astype(ml_dtypes.bfloat16)


def seg_starts(seg_ref, start_ref, seg_count):
    total = jnp.int32(0)
    for s in range(seg_count):
        start_ref[s] = total
        total = total + seg_ref[0, s]


def inverse_order(order_ref, residue_ref, seg_count):
    for r in range(seg_count):
        residue_ref[order_ref[0, r]] = jnp.int32(r)


def arrange_strain(own_ref, other_ref, order_ref, seg_ref, spectra_ref, start_ref, residue_ref, seg_count):
    seg_here = lax.axis_index("seg")
    core = seg_here % 2
    chip = seg_here // 2
    chip_count = seg_count // 2
    pair_slots = own_ref.shape[0] // seg_count
    slots = own_ref.shape[0]
    seg_starts(seg_ref, start_ref, seg_count)
    inverse_order(order_ref, residue_ref, seg_count)
    for m in range(chip_count):
        residue = residue_ref[(chip ^ m) * 2 + core]
        for side, ref in ((0, own_ref), (1, other_ref)):
            first = (residue - start_ref[chip * 2 + (core ^ side)] + 32 * seg_count) % seg_count
            for j in range(pair_slots):
                row = (m * 2 + side) * pair_slots + j
                block = ref[first + j * seg_count].astype(jnp.float32)
                spectra_ref[row : row + 1, :] = block[0:1]
                spectra_ref[slots + row : slots + row + 1, :] = block[1:2]


def weigh(tmpl_ref, psd_ref, edge_ref, first, weighted_ref, sigma_ref, frac_ref, held_ref):
    tmpl_count, detectors, width = tmpl_ref.shape
    freq_count = width // 2
    bins = edge_ref.shape[1] - 1
    psd = psd_ref[...]
    both = jnp.concatenate([psd, psd], axis=1)
    for t in range(tmpl_count):
        rows = pl.ds(t * detectors, detectors)
        held_ref[rows, :] = tmpl_ref[t]
        weighted_ref[rows, :] = tmpl_ref[t] * both
    row_ids = lax.broadcasted_iota(jnp.int32, (8, LANES), 0) // detectors
    lane_ids = lax.broadcasted_iota(jnp.int32, (8, LANES), 1)
    edges = []
    for p in range(bins + 1):
        edge = jnp.zeros((8, LANES), jnp.int32)
        for t in range(tmpl_count):
            edge = jnp.where(row_ids == t, edge_ref[first + t, p], edge)
        edges.append(edge)
    sums = [jnp.zeros((8, LANES), jnp.float32) for _ in range(bins)]
    for c in range(freq_count // LANES):
        re, im = pl.ds(c * LANES, LANES), pl.ds(freq_count + c * LANES, LANES)
        power = held_ref[:, re] * weighted_ref[:, re] + held_ref[:, im] * weighted_ref[:, im]
        below = [lane_ids + c * LANES < edges[p] for p in range(bins + 1)]
        for p in range(bins):
            sums[p] = sums[p] + jnp.where(below[p + 1] & ~below[p], power, 0.0)
    parts = [jnp.broadcast_to(jnp.sum(s, axis=1, keepdims=True), (8, LANES)) for s in sums]
    total = functools.reduce(jnp.add, parts)
    for p in range(bins):
        sigma_ref[p] = 1.0 / parts[p]
        frac_ref[p] = parts[p] / total
    sigma_ref[bins] = 1.0 / total


def filter_templates(
    spectra_ref, weighted_ref, inv_ref, frac_ref, edge_ref, first, dft_ref, series_ref, tmpl_count, out_ref, lane_step
):
    rows, width = spectra_ref.shape
    slots = rows // 2
    freq_count = width // 2
    bins = edge_ref.shape[1] - 1
    chunk_count = freq_count // CHUNK
    lane_ids = lax.broadcasted_iota(jnp.int32, (16, LANES), 1)

    def product(t, re, im, strain_re, strain_im):
        def rows_of(lanes):
            return jnp.concatenate(
                [jnp.broadcast_to(weighted_ref[2 * t + d : 2 * t + d + 1, lanes], (slots, CHUNK)) for d in range(2)],
                axis=0,
            )

        tmpl_re, tmpl_im = rows_of(re), rows_of(im)
        prod_re = tmpl_re * strain_re + tmpl_im * strain_im
        prod_im = tmpl_re * strain_im - tmpl_im * strain_re
        return jnp.concatenate([prod_re, prod_im], axis=1).astype(jnp.bfloat16)

    def masked(prod, low, high):
        member = jnp.where((lane_ids >= low) & (lane_ids < high), 1.0, 0.0).astype(jnp.bfloat16)
        member = jnp.concatenate([member] * (rows // 16), axis=0)
        return prod * jnp.concatenate([member, member], axis=1)

    def bin_before(t, bound):
        count = jnp.int32(0)
        for j in range(1, bins):
            count = count + (edge_ref[first + t, j] < bound).astype(jnp.int32)
        return count

    running = [jnp.zeros((rows, 2 * TIME_LAGS), jnp.float32) for _ in range(tmpl_count)]
    before = [jnp.int32(0) for _ in range(tmpl_count)]
    for c in range(chunk_count):
        re, im = pl.ds(c * CHUNK, CHUNK), pl.ds(freq_count + c * CHUNK, CHUNK)
        strain_re, strain_im = spectra_ref[:, re], spectra_ref[:, im]
        stack, crosses = [], []
        after = []
        for t in range(tmpl_count):
            prod = product(t, re, im, strain_re, strain_im)
            last = jnp.int32(bins - 1) if c == chunk_count - 1 else bin_before(t, (c + 1) * CHUNK)
            after.append(last)
            cross = last > before[t]
            crosses.append(cross)
            stack.append(masked(prod, 0, edge_ref[first + t, before[t] + 1] - c * CHUNK))
            stack.append(masked(prod, jnp.where(cross, edge_ref[first + t, last] - c * CHUNK, CHUNK), CHUNK))
        got = jnp.dot(jnp.concatenate(stack, axis=0), dft_ref[c], preferred_element_type=jnp.float32)
        for t in range(tmpl_count):
            ended = running[t] + got[2 * t * rows : (2 * t + 1) * rows]
            series_ref[t, before[t]] = ended
            running[t] = jnp.where(crosses[t], got[(2 * t + 1) * rows : (2 * t + 2) * rows], ended)
            before[t] = after[t]
    for t in range(tmpl_count):
        series_ref[t, bins - 1] = running[t]

    for t in range(tmpl_count):
        for p in range(1, bins - 1):
            low, high = edge_ref[first + t, p], edge_ref[first + t, p + 1]
            c = low // CHUNK

            @pl.when(high < (c + 1) * CHUNK)
            def _(t=t, p=p, low=low, high=high, c=c):
                start = pl.multiple_of(c * CHUNK, CHUNK)
                re, im = pl.ds(start, CHUNK), pl.ds(freq_count + start, CHUNK)
                prod = product(t, re, im, spectra_ref[:, re], spectra_ref[:, im])
                prod = masked(prod, low - start, high - start)
                series_ref[t, p] = jnp.dot(prod, dft_ref[c], preferred_element_type=jnp.float32)

    out_ids = lax.broadcasted_iota(jnp.int32, (slots, LANES), 1)
    out = out_ref[...]
    for t in range(tmpl_count):
        whole = series_ref[t, 0]
        for p in range(1, bins):
            whole = whole + series_ref[t, p]

        def spread(ref, p):
            return jnp.concatenate(
                [jnp.broadcast_to(ref[p, 2 * t + d : 2 * t + d + 1, :], (slots, LANES)) for d in range(2)], axis=0
            )

        chi = jnp.zeros((rows, LANES), jnp.float32)
        for p in range(bins):
            dev = series_ref[t, p] - spread(frac_ref, p) * whole
            chi = chi + dev * dev * spread(inv_ref, p)
        chi = jnp.sum(chi[:slots] + chi[slots:], axis=1, keepdims=True) / (TIME_LAGS * 2.0 * 2 * (bins - 1))
        power = whole * whole * spread(inv_ref, bins)
        power = power[:slots] + power[slots:]
        power = power + pltpu.roll(power, TIME_LAGS, 1)
        peak = jnp.sqrt(jnp.max(power, axis=1, keepdims=True))
        out = jnp.where(out_ids == first + t, peak, out)
        out = jnp.where(out_ids == first + t + lane_step, chi, out)
    out_ref[...] = out


def own_kernel(
    seg_count,
    own_ref, other_ref, tmpl_ref, psd_ref, dft_ref, order_ref, seg_ref, edge_ref,
    spectra_ref, out_ref,
    start_ref, residue_ref, held_ref, weighted_ref, sigma_ref, frac_ref, series_ref,
):
    tmpl_count = tmpl_ref.shape[0]
    first = lax.axis_index("bank") * tmpl_count
    arrange_strain(own_ref, other_ref, order_ref, seg_ref, spectra_ref, start_ref, residue_ref, seg_count)
    out_ref[...] = jnp.zeros_like(out_ref)
    weigh(tmpl_ref, psd_ref, edge_ref, first, weighted_ref, sigma_ref, frac_ref, held_ref)
    filter_templates(
        spectra_ref, weighted_ref, sigma_ref, frac_ref, edge_ref, first, dft_ref, series_ref,
        tmpl_count, out_ref, edge_ref.shape[0],
    )


def rest_kernel(group_count, part_count, *refs):
    tmpl_refs = refs[: group_count - 1]
    spectra_ref, part_ref, psd_ref, dft_ref, edge_ref = refs[group_count - 1 : group_count + 4]
    out_refs = refs[group_count + 4 : group_count + 4 + part_count]
    held_ref, weighted_ref, sigma_ref, frac_ref, series_ref, all_ref = refs[group_count + 4 + part_count :]
    tmpl_count = tmpl_refs[0].shape[0]
    bank = lax.axis_index("bank")
    all_ref[...] = part_ref[...]
    for s in range(1, group_count):
        first = (bank ^ s) * tmpl_count
        weigh(
            tmpl_refs[s - 1], psd_ref, edge_ref, first,
            weighted_ref.at[s - 1], sigma_ref.at[s - 1], frac_ref.at[s - 1], held_ref,
        )

    def one(s, _):
        first = (bank ^ (s + 1)) * tmpl_count
        filter_templates(
            spectra_ref, weighted_ref.at[s], sigma_ref.at[s], frac_ref.at[s], edge_ref, first, dft_ref, series_ref,
            tmpl_count, all_ref, edge_ref.shape[0],
        )
        return 0

    lax.fori_loop(0, group_count - 1, one, 0)
    size = out_refs[0].shape[0]
    for m in range(part_count):
        out_refs[m][...] = all_ref[m * size : (m + 1) * size, :]


def pick_kernel(seg_count, *refs):
    chip_count = seg_count // 2
    part_refs = refs[:chip_count]
    order_ref, seg_ref, peak_ref, chi_ref, start_ref, residue_ref, held_ref, rows_ref = refs[chip_count:]
    seg_here = lax.axis_index("seg")
    core, chip = seg_here % 2, seg_here // 2
    size = part_refs[0].shape[0]
    pair_slots = size // 2
    seg_starts(seg_ref, start_ref, seg_count)
    inverse_order(order_ref, residue_ref, seg_count)
    for m in range(chip_count):
        held_ref[m] = part_refs[m][...]
    for n in range(BLK_DEV):
        block = residue_ref[seg_here] + n * seg_count
        source = jnp.int32(-1)
        for s in range(seg_count):
            source = source + (start_ref[s] <= block).astype(jnp.int32)
        slot = block - start_ref[source]
        row = ((source % 2) ^ core) * pair_slots + slot // seg_count
        rows_ref[n : n + 1, :] = held_ref[(source // 2) ^ chip, pl.ds(row, 1), :]
    tmpl_total = peak_ref.shape[1]
    rows = rows_ref[...]
    peak_ref[...] = rows[:, :tmpl_total]
    chi_ref[...] = rows[:, tmpl_total : 2 * tmpl_total]


def swap(x, axis, step):
    return lax.ppermute(x, axis, [(i, i ^ step) for i in range(lax.axis_size(axis))])


def body(strain, templates, inv_psd, seg_blocks, dest_order, bin_edges):
    seg_count, bank_count = lax.axis_size("seg"), lax.axis_size("bank")
    chip_count = seg_count // 2
    slots, detectors, width = strain.shape
    freq_count = width // 2
    tmpl_total, bins = bin_edges.shape[0], bin_edges.shape[1] - 1
    tmpl_count = templates.shape[0]
    rows = detectors * slots
    dft = jnp.asarray(dft_chunks(freq_count))
    f32 = jnp.float32

    other = swap(strain, "seg", 1)
    remote = [swap(templates, "bank", s) for s in range(1, bank_count)]

    def scratch(lead):
        return [
            pltpu.VMEM((8, width), f32),
            pltpu.VMEM(lead + (8, width), f32),
            pltpu.VMEM(lead + (bins + 1, 8, LANES), f32),
            pltpu.VMEM(lead + (bins + 1, 8, LANES), f32),
            pltpu.VMEM((tmpl_count, bins, rows, 2 * TIME_LAGS), f32),
        ]

    tables = [pltpu.SMEM((seg_count,), jnp.int32), pltpu.SMEM((seg_count,), jnp.int32)]
    params = pltpu.CompilerParams(vmem_limit_bytes=40 * 1024 * 1024)
    spectra, part = pl.pallas_call(
        functools.partial(own_kernel, seg_count),
        out_shape=(jax.ShapeDtypeStruct((rows, width), f32), jax.ShapeDtypeStruct((slots, LANES), f32)),
        in_specs=[VMEM] * 5 + [SMEM] * 3,
        out_specs=(VMEM, VMEM),
        scratch_shapes=tables + scratch(()),
        compiler_params=params,
        cost_estimate=pl.CostEstimate(flops=10**9, bytes_accessed=4 * 10**6, transcendentals=0),
        name="own_templates",
    )(strain, other, templates, inv_psd, dft, dest_order, seg_blocks, bin_edges)

    size = 2 * (slots // seg_count)
    parts = pl.pallas_call(
        functools.partial(rest_kernel, bank_count, chip_count),
        out_shape=tuple(jax.ShapeDtypeStruct((size, LANES), f32) for _ in range(chip_count)),
        in_specs=[VMEM] * (bank_count - 1 + 4) + [SMEM],
        out_specs=(VMEM,) * chip_count,
        scratch_shapes=scratch((bank_count - 1,)) + [pltpu.VMEM((slots, LANES), f32)],
        compiler_params=params,
        cost_estimate=pl.CostEstimate(flops=3 * 10**9, bytes_accessed=4 * 10**6, transcendentals=0),
        name="other_templates",
    )(*remote, spectra, part, inv_psd, dft, bin_edges)

    got = [parts[0]] + [swap(parts[m], "seg", 2 * m) for m in range(1, chip_count)]
    return pl.pallas_call(
        functools.partial(pick_kernel, seg_count),
        out_shape=tuple(jax.ShapeDtypeStruct((BLK_DEV, tmpl_total), f32) for _ in range(2)),
        in_specs=[VMEM] * chip_count + [SMEM] * 2,
        out_specs=(VMEM, VMEM),
        scratch_shapes=tables + [pltpu.VMEM((chip_count, size, LANES), f32), pltpu.VMEM((BLK_DEV, LANES), f32)],
        compiler_params=params,
        name="pick_rows",
    )(*got, dest_order, seg_blocks)


def solution(mesh):
    return jax.shard_map(
        body,
        mesh=mesh,
        in_specs=(
            P(("bank", "seg"), None, None),
            P("bank", None, None),
            P(),
            P("bank", None),
            P("bank", None),
            P(),
        ),
        out_specs=(P(("bank", "seg"), None), P(("bank", "seg"), None)),
        check_vma=False,
    )
```

time: 117 us -> 31.9 us (0.27)
  other arithmetic: 43.1 us -> 0 us
  matrix products: 26.5 us -> 0 us
  local copies, waits for them, and re-layouts: 17.8 us -> 5.9 us
  blocking collectives: 11.3 us -> 0 us
  Pallas kernels: 0 us -> 10.3 us
  waiting for transfers between devices: 7.4 us -> 5.41 us
    dot_general x9 -> x0, matrix products: 26.5 us -> none  [the longest x6 24.8 us: filter_core(): lax.dot_general(dft_rows, flattened, (((0,), (1,)), ((), ())), preferred_...]
    another operation x17 -> x0, other arithmetic: 22 us -> none
    all_gather x1 -> x0, blocking collectives: 11.3 us -> none  [filter_all(): piece = lax.all_gather(templates, 'bank', axis=0, tiled=True)]
    pallas_call x0 -> x3, Pallas kernels: none -> 10.3 us  [the longest x1 6.05 us: body(): pl.pallas_call(functools.partial(rest_kernel, bank_count, chip_count), ou...]
    ppermute x0 -> x7, starting transfers between devices: none -> 9.3 us  [swap(): lax.ppermute(x, axis, [(i, i ^ step) for i in range(lax.axis_size(axis))])]
    all_to_all x2 -> x0, starting transfers between devices: 8.22 us -> none  [the longest x1 4.88 us: body(): lax.all_to_all(peak_out, 'seg', split_axis=0, concat_axis=0, tiled=True)]
    mul x7 -> x0, other arithmetic: 7.68 us -> none  [the longest x6 7.17 us: filter_core(): prod_re = (tmpl_re * strain_re + tmpl_im * strain_im) * weights]
    all_to_all x2 -> x0, waiting for transfers between devices: 7.4 us -> none  [the longest x1 4.42 us: body(): lax.all_to_all(chisq_out, 'seg', split_axis=0, concat_axis=0, tiled=True)]
  transfers between devices with their start and end apart: 2 -> 7, of which waited for: 2 -> 2; matrix products, arithmetic and copies ran while one was open for 3% -> 0% of each run, Pallas kernels for 0% -> 8%
where the time goes in v1:
time: 31.9 us; the launch traced here: 31.6 us
  Pallas kernels  10.3 us (32%)
  starting transfers between devices  9.3 us (29%)
  local copies, waits for them, and re-layouts  5.9 us (18%)
  waiting for transfers between devices  5.41 us (17%)
  between operations  0.68 us (2%)
    ppermute x7, starting transfers between devices, swap(): lax.ppermute(x, axis, [(i, i ^ step) for i in range(lax.axis_size(axis))])  9.3 us
    pallas_call x1, Pallas kernels, body(): pl.pallas_call(functools.partial(rest_kernel, bank_count, chip_count), ou...  6.05 us
    unnamed x22, local copies, waits for them, and re-layouts  5.9 us
    ppermute x7, waiting for transfers between devices, swap(): lax.ppermute(x, axis, [(i, i ^ step) for i in range(lax.axis_size(axis))])  5.41 us
    pallas_call x1, Pallas kernels, body(): pl.pallas_call(functools.partial(own_kernel, seg_count), out_shape=(jax.S...  2.64 us
    pallas_call x1, Pallas kernels, body(): pl.pallas_call(functools.partial(pick_kernel, seg_count), out_shape=tuple...  1.58 us
  transfers between devices with their start and end apart: 7, of which 2 were waited for; matrix products, arithmetic and copies ran while one was open for 0% of the time, Pallas kernels for 8%

profile of v1, /device:TPU:0, one launch (start us, length us, event | category | flops | bytes accessed | tf_op | source)
XLA Modules:
  0.0 31.6 jit_solution(13967629573824592575)
XLA Ops:
  0.6 0.5 %collective-permute-start.3 = (bf16[32,2,4096]{2,1,0:T(2,128)(2,1)}, bf16[32,2,4096]{2,1,0:T(2,128)(2,1)S(1)}, u32[]{:S(2)}, u32[]{:S(2)}) collective-permute-start(bf16[32,2,4096]{2,1,0:T(2,128)(2,1)} %own_ref.1), channel_id=1, source_target_pairs={{0,1},{1,0},{2,3},{3,2},{4,5},{5,4},{6,7},{7,6},{8,9},{9,8},{10,11... | collective-permute-start | bytes 1572872 | tf_op jit(solution)/shard_map/ppermute | solution.py:263
  1.1 2.6 %collective-permute-start = (f32[3,2,4096]{2,1,0:T(2,128)}, f32[3,2,4096]{2,1,0:T(2,128)S(1)}, u32[]{:S(2)}, u32[]{:S(2)}) collective-permute-start(f32[3,2,4096]{2,1,0:T(2,128)} %tmpl_ref.1), channel_id=1, source_target_pairs={{0,8},{8,0},{16,24},{24,16},{1,9},{9,1},{17,25},{25,17},{2,10},{10... | collective-permute-start | bytes 294920 | tf_op jit(solution)/shard_map/ppermute | solution.py:263
  3.7 1.5 %collective-permute-start.1 = (f32[3,2,4096]{2,1,0:T(2,128)}, f32[3,2,4096]{2,1,0:T(2,128)S(1)}, u32[]{:S(2)}, u32[]{:S(2)}) collective-permute-start(f32[3,2,4096]{2,1,0:T(2,128)} %tmpl_ref.1), channel_id=1, source_target_pairs={{0,16},{8,24},{16,0},{24,8},{1,17},{9,25},{17,1},{25,9},{2,18},{10... | collective-permute-start | bytes 294920 | tf_op jit(solution)/shard_map/ppermute | solution.py:263
  5.2 0.0 collective-permute-start.2
  5.3 0.0 collective-permute-done.3.other_ref
  5.3 0.0 copy-start
  5.3 0.7 %copy-done = s32[1,8]{1,0:T(1,128)S(1)} copy-done((s32[1,8]{1,0:T(1,128)S(1)}, s32[1,8]{1,0:T(1,128)}, u32[]{:S(2)}) %copy-start) | copy-done | bytes 56
  5.9 0.0 copy-start.2
  5.9 0.7 %copy-done.2 = s32[1,8]{1,0:T(1,128)S(1)} copy-done((s32[1,8]{1,0:T(1,128)S(1)}, s32[1,8]{1,0:T(1,128)}, u32[]{:S(2)}) %copy-start.2) | copy-done | bytes 56
  6.6 0.0 copy-start.4
  6.6 1.0 %copy-done.4 = bf16[32,2,4096]{2,1,0:T(2,128)(2,1)S(1)} copy-done((bf16[32,2,4096]{2,1,0:T(2,128)(2,1)S(1)}, bf16[32,2,4096]{2,1,0:T(2,128)(2,1)}, u32[]{:S(2)}) %copy-start.4) | copy-done | bytes 524312
  7.6 0.0 copy-start.5
  7.6 0.9 %copy-done.5 = f32[3,2,4096]{2,1,0:T(2,128)S(1)} copy-done((f32[3,2,4096]{2,1,0:T(2,128)S(1)}, f32[3,2,4096]{2,1,0:T(2,128)}, u32[]{:S(2)}) %copy-start.5) | copy-done | bytes 98328
  8.5 0.0 copy-start.6
  8.5 0.7 %copy-done.6 = f32[2,2048]{1,0:T(2,128)S(1)} copy-done((f32[2,2048]{1,0:T(2,128)S(1)}, f32[2,2048]{1,0:T(2,128)}, u32[]{:S(2)}) %copy-start.6) | copy-done | bytes 16408
  9.2 0.0 copy-start.8
  9.2 0.7 %copy-done.8 = s32[12,9]{1,0:T(8,128)S(1)} copy-done((s32[12,9]{1,0:T(8,128)S(1)}, s32[12,9]{1,0:T(8,128)}, u32[]{:S(2)}) %copy-start.8) | copy-done | bytes 456
  9.9 0.0 copy-start.9
  9.9 1.2 %copy-done.9 = bf16[16,256,128]{2,1,0:T(8,128)(2,1)S(1)} copy-done((bf16[16,256,128]{2,1,0:T(8,128)(2,1)S(1)}, bf16[16,256,128]{2,1,0:T(8,128)(2,1)}, u32[]{:S(2)}) %copy-start.9) | copy-done | bytes 1048600
  11.2 0.0 copy-start.7
  11.2 0.0 copy-start.10
  11.2 2.6 %own_templates.1 = (f32[64,4096]{1,0:T(8,128)S(1)}, f32[32,128]{1,0:T(8,128)S(1)}) custom-call(bf16[32,2,4096]{2,1,0:T(2,128)(2,1)S(1)} %copy-done.4, bf16[32,2,4096]{2,1,0:T(2,128)(2,1)S(1)} %collective-permute-done.3.other_ref, f32[3,2,4096]{2,1,0:T(2,128)S(1)} %copy-done.5, f32[2,2048]{1,0:T(2,128)S(1)} %copy-done.6, bf16[16,256,128]{2,1,0:T(8,128)(2,1)S(1)} %copy-done.9, ...), custom_call_target="tpu_custom_call" | custom-call | flops 1000000000 | bytes 4000000 | tf_op jit(solution)/shard_map/own_templates/pallas_call | solution.py:291
  13.8 0.0 collective-permute-done.refs_0_
  13.8 0.0 collective-permute-done.1.refs_1_
  13.8 0.0 collective-permute-done.2.refs_2_
  13.8 0.0 copy-done.7
  13.8 0.0 copy-done.10
  13.8 6.1 %other_templates.1 = (f32[8,128]{1,0:T(8,128)S(1)}, f32[8,128]{1,0:T(8,128)S(1)}, f32[8,128]{1,0:T(8,128)S(1)}, f32[8,128]{1,0:T(8,128)S(1)}) custom-call(f32[3,2,4096]{2,1,0:T(2,128)S(1)} %collective-permute-done.refs_0_, f32[3,2,4096]{2,1,0:T(2,128)S(1)} %collective-permute-done.1.refs_1_, f32[3,2,4096]{2,1,0:T(2,128)S(1)} %collective-permute-done.2.refs_2_, ...), custom_call_target="tpu_custom_call" | custom-call | flops 3000000000 | bytes 4000000 | tf_op jit(solution)/shard_map/other_templates/pallas_call | solution.py:303
  19.9 2.1 %collective-permute-start.4 = (f32[8,128]{1,0:T(8,128)S(1)}, f32[8,128]{1,0:T(8,128)S(1)}, u32[]{:S(2)}, u32[]{:S(2)}) collective-permute-start(f32[8,128]{1,0:T(8,128)S(1)} %get-tuple-element.11), channel_id=1, source_target_pairs={{0,2},{1,3},{2,0},{3,1},{4,6},{5,7},{6,4},{7,5},{8,10},{9,11},{10,... | collective-permute-start | bytes 12296 | tf_op jit(solution)/shard_map/ppermute | solution.py:263
  22.0 2.6 %collective-permute-start.5 = (f32[8,128]{1,0:T(8,128)S(1)}, f32[8,128]{1,0:T(8,128)S(1)}, u32[]{:S(2)}, u32[]{:S(2)}) collective-permute-start(f32[8,128]{1,0:T(8,128)S(1)} %get-tuple-element.12), channel_id=1, source_target_pairs={{0,4},{1,5},{2,6},{3,7},{4,0},{5,1},{6,2},{7,3},{8,12},{9,13},{10,... | collective-permute-start | bytes 12296 | tf_op jit(solution)/shard_map/ppermute | solution.py:263
  24.6 0.0 copy-start.1
  24.6 0.0 copy-start.3
  24.6 0.0 collective-permute-start.6
  24.6 0.0 collective-permute-done.4.refs_1_
  24.6 1.9 %collective-permute-done.5.refs_2_ = f32[8,128]{1,0:T(8,128)S(1)} collective-permute-done((f32[8,128]{1,0:T(8,128)S(1)}, f32[8,128]{1,0:T(8,128)S(1)}, u32[]{:S(2)}, u32[]{:S(2)}) %collective-permute-start.5) | collective-permute-done | bytes 4128 | tf_op jit(solution)/shard_map/ppermute | solution.py:263
  26.5 3.5 %collective-permute-done.6.refs_3_ = f32[8,128]{1,0:T(8,128)S(1)} collective-permute-done((f32[8,128]{1,0:T(8,128)S(1)}, f32[8,128]{1,0:T(8,128)S(1)}, u32[]{:S(2)}, u32[]{:S(2)}) %collective-permute-start.6) | collective-permute-done | bytes 4128 | tf_op jit(solution)/shard_map/ppermute | solution.py:263
  30.0 0.0 copy-done.1
  30.0 0.0 copy-done.3
  30.0 1.6 %pick_rows.1 = (f32[16,12]{1,0:T(8,128)}, f32[16,12]{1,0:T(8,128)}) custom-call(f32[8,128]{1,0:T(8,128)S(1)} %get-tuple-element.10.refs_0_, f32[8,128]{1,0:T(8,128)S(1)} %collective-permute-done.4.refs_1_, f32[8,128]{1,0:T(8,128)S(1)} %collective-permute-done.5.refs_2_, f32[8,128]{1,0:T(8,128)S(1)} %collective-permute-done.6.refs_3_, s32[1,8]{1,0:T(1,128)S(1)} %copy-done.1, ...), custom_call_target="tpu_custom_call" | custom-call | tf_op jit(solution)/shard_map/pick_rows/pallas_call | solution.py:315
Async XLA Ops:
  0.6 4.6 %collective-permute-start.3 = (bf16[32,2,4096]{2,1,0:T(2,128)(2,1)}, bf16[32,2,4096]{2,1,0:T(2,128)(2,1)S(1)}, u32[]{:S(2)}, u32[]{:S(2)}) collective-permute-start(bf16[32,2,4096]{2,1,0:T(2,128)(2,1)} %own_ref.1), channel_id=1, source_target_pairs={{0,1},{1,0},{2,3},{3,2},{4,5},{5,4},{6,7},{7,6},{8,9},{9,8},{10,11... | collective-permute-start | bytes 1572872 | tf_op jit(solution)/shard_map/ppermute | solution.py:263
  1.1 12.7 %collective-permute-start = (f32[3,2,4096]{2,1,0:T(2,128)}, f32[3,2,4096]{2,1,0:T(2,128)S(1)}, u32[]{:S(2)}, u32[]{:S(2)}) collective-permute-start(f32[3,2,4096]{2,1,0:T(2,128)} %tmpl_ref.1), channel_id=1, source_target_pairs={{0,8},{8,0},{16,24},{24,16},{1,9},{9,1},{17,25},{25,17},{2,10},{10... | collective-permute-start | bytes 294920 | tf_op jit(solution)/shard_map/ppermute | solution.py:263
  3.7 10.1 %collective-permute-start.1 = (f32[3,2,4096]{2,1,0:T(2,128)}, f32[3,2,4096]{2,1,0:T(2,128)S(1)}, u32[]{:S(2)}, u32[]{:S(2)}) collective-permute-start(f32[3,2,4096]{2,1,0:T(2,128)} %tmpl_ref.1), channel_id=1, source_target_pairs={{0,16},{8,24},{16,0},{24,8},{1,17},{9,25},{17,1},{25,9},{2,18},{10... | collective-permute-start | bytes 294920 | tf_op jit(solution)/shard_map/ppermute | solution.py:263
  5.2 8.6 %collective-permute-start.2 = (f32[3,2,4096]{2,1,0:T(2,128)}, f32[3,2,4096]{2,1,0:T(2,128)S(1)}, u32[]{:S(2)}, u32[]{:S(2)}) collective-permute-start(f32[3,2,4096]{2,1,0:T(2,128)} %tmpl_ref.1), channel_id=1, source_target_pairs={{0,24},{8,16},{16,8},{24,0},{1,25},{9,17},{17,9},{25,1},{2,26},{10... | collective-permute-start | bytes 294920 | tf_op jit(solution)/shard_map/ppermute | solution.py:263
  5.3 0.7 %copy-start = (s32[1,8]{1,0:T(1,128)S(1)}, s32[1,8]{1,0:T(1,128)}, u32[]{:S(2)}) copy-start(s32[1,8]{1,0:T(1,128)} %refs_4_.1) | copy-start | bytes 100
  5.9 0.7 %copy-start.2 = (s32[1,8]{1,0:T(1,128)S(1)}, s32[1,8]{1,0:T(1,128)}, u32[]{:S(2)}) copy-start(s32[1,8]{1,0:T(1,128)} %refs_5_.3) | copy-start | bytes 100
  6.6 1.0 %copy-start.4 = (bf16[32,2,4096]{2,1,0:T(2,128)(2,1)S(1)}, bf16[32,2,4096]{2,1,0:T(2,128)(2,1)}, u32[]{:S(2)}) copy-start(bf16[32,2,4096]{2,1,0:T(2,128)(2,1)} %own_ref.1) | copy-start | bytes 1572868
  7.6 0.9 %copy-start.5 = (f32[3,2,4096]{2,1,0:T(2,128)S(1)}, f32[3,2,4096]{2,1,0:T(2,128)}, u32[]{:S(2)}) copy-start(f32[3,2,4096]{2,1,0:T(2,128)} %tmpl_ref.1) | copy-start | bytes 294916
  8.5 0.7 %copy-start.6 = (f32[2,2048]{1,0:T(2,128)S(1)}, f32[2,2048]{1,0:T(2,128)}, u32[]{:S(2)}) copy-start(f32[2,2048]{1,0:T(2,128)} %refs_5_.2) | copy-start | bytes 49156
  9.2 0.7 %copy-start.8 = (s32[12,9]{1,0:T(8,128)S(1)}, s32[12,9]{1,0:T(8,128)}, u32[]{:S(2)}) copy-start(s32[12,9]{1,0:T(8,128)} %refs_7_.1) | copy-start | bytes 1300
  9.9 1.2 %copy-start.9 = (bf16[16,256,128]{2,1,0:T(8,128)(2,1)S(1)}, bf16[16,256,128]{2,1,0:T(8,128)(2,1)}, u32[]{:S(2)}) copy-start(bf16[16,256,128]{2,1,0:T(8,128)(2,1)} %constant.2.clone.dft_ref.refs_6_) | copy-start | bytes 3145732
  11.2 2.7 %copy-start.7 = (f32[2,2048]{1,0:T(2,128)S(1)}, f32[2,2048]{1,0:T(2,128)}, u32[]{:S(2)}) copy-start(f32[2,2048]{1,0:T(2,128)} %refs_5_.2) | copy-start | bytes 49156
  11.2 2.7 %copy-start.10 = (bf16[16,256,128]{2,1,0:T(8,128)(2,1)S(1)}, bf16[16,256,128]{2,1,0:T(8,128)(2,1)}, u32[]{:S(2)}) copy-start(bf16[16,256,128]{2,1,0:T(8,128)(2,1)} %constant.2.clone.dft_ref.refs_6_) | copy-start | bytes 3145732
  19.9 4.7 %collective-permute-start.4 = (f32[8,128]{1,0:T(8,128)S(1)}, f32[8,128]{1,0:T(8,128)S(1)}, u32[]{:S(2)}, u32[]{:S(2)}) collective-permute-start(f32[8,128]{1,0:T(8,128)S(1)} %get-tuple-element.11), channel_id=1, source_target_pairs={{0,2},{1,3},{2,0},{3,1},{4,6},{5,7},{6,4},{7,5},{8,10},{9,11},{10,... | collective-permute-start | bytes 12296 | tf_op jit(solution)/shard_map/ppermute | solution.py:263
  22.0 4.5 %collective-permute-start.5 = (f32[8,128]{1,0:T(8,128)S(1)}, f32[8,128]{1,0:T(8,128)S(1)}, u32[]{:S(2)}, u32[]{:S(2)}) collective-permute-start(f32[8,128]{1,0:T(8,128)S(1)} %get-tuple-element.12), channel_id=1, source_target_pairs={{0,4},{1,5},{2,6},{3,7},{4,0},{5,1},{6,2},{7,3},{8,12},{9,13},{10,... | collective-permute-start | bytes 12296 | tf_op jit(solution)/shard_map/ppermute | solution.py:263
  24.6 5.4 %copy-start.1 = (s32[1,8]{1,0:T(1,128)S(1)}, s32[1,8]{1,0:T(1,128)}, u32[]{:S(2)}) copy-start(s32[1,8]{1,0:T(1,128)} %refs_4_.1) | copy-start | bytes 100
  24.6 5.4 %copy-start.3 = (s32[1,8]{1,0:T(1,128)S(1)}, s32[1,8]{1,0:T(1,128)}, u32[]{:S(2)}) copy-start(s32[1,8]{1,0:T(1,128)} %refs_5_.3) | copy-start | bytes 100
  24.6 5.4 %collective-permute-start.6 = (f32[8,128]{1,0:T(8,128)S(1)}, f32[8,128]{1,0:T(8,128)S(1)}, u32[]{:S(2)}, u32[]{:S(2)}) collective-permute-start(f32[8,128]{1,0:T(8,128)S(1)} %get-tuple-element.13), channel_id=1, source_target_pairs={{0,6},{1,7},{2,4},{3,5},{4,2},{5,3},{6,0},{7,1},{8,14},{9,15},{10,... | collective-permute-start | bytes 12296 | tf_op jit(solution)/shard_map/ppermute | solution.py:263

commit v2 on v0

v2 whole, which is shorter than its diff:
```python
import functools

import jax
import jax.numpy as jnp
import ml_dtypes
import numpy as np
from jax import lax
from jax.experimental import pallas as pl
from jax.experimental.pallas import tpu as pltpu
from jax.sharding import PartitionSpec as P

TIME_LAGS = 64
BLK_DEV = 16
CHUNK = 128
LANES = 128
VMEM = pl.BlockSpec(memory_space=pltpu.VMEM)
SMEM = pl.BlockSpec(memory_space=pltpu.SMEM)


def dft_chunks(freq_count):
    turns = np.arange(freq_count)[:, None] * np.arange(TIME_LAGS)[None, :] % (2 * freq_count)
    angle = turns * (np.pi / freq_count)
    cosine, sine = np.cos(angle), np.sin(angle)
    upper = np.concatenate([cosine, sine], axis=1).reshape(-1, CHUNK, 2 * TIME_LAGS)
    lower = np.concatenate([-sine, cosine], axis=1).reshape(-1, CHUNK, 2 * TIME_LAGS)
    return np.concatenate([upper, lower], axis=1).astype(np.float32).astype(ml_dtypes.bfloat16)


def tile_rows(x):
    lead, (detectors, width) = x.shape[:-2], x.shape[-2:]
    tiles = jnp.swapaxes(x.reshape(lead + (detectors, width // LANES, LANES)), -3, -2)
    return tiles.reshape(lead + (detectors * width // LANES, LANES))


def seg_starts(seg_ref, start_ref, seg_count):
    total = jnp.int32(0)
    for s in range(seg_count):
        start_ref[s] = total
        total = total + seg_ref[0, s]


def inverse_order(order_ref, residue_ref, seg_count):
    for r in range(seg_count):
        residue_ref[order_ref[0, r]] = jnp.int32(r)


def first_slot(start_ref, residue_ref, seg_count, m, side):
    seg_here = lax.axis_index("seg")
    core, chip = seg_here % 2, seg_here // 2
    start = start_ref[chip * 2 + (core ^ side)]
    residue = residue_ref[(chip ^ m) * 2 + core]
    return start, (residue - start % seg_count + seg_count) % seg_count


def arrange_strain(side, src_ref, psd_ref, spectra_ref, start_ref, residue_ref, seg_count):
    slots, tiles = src_ref.shape[0], src_ref.shape[1]
    pair_slots = slots // seg_count
    psd = psd_ref[...]
    both = jnp.concatenate([psd, psd], axis=0)
    for m in range(seg_count // 2):
        _, first = first_slot(start_ref, residue_ref, seg_count, m, side)
        for j in range(pair_slots):
            row = (m * 2 + side) * pair_slots + j
            spectra_ref[pl.ds(row, tiles, stride=slots + 1), :] = src_ref[first + j * seg_count].astype(jnp.float32) * both


def chunk_masks(group):
    shape = (group.chunks, LANES)
    lanes = lax.broadcasted_iota(jnp.int32, shape, 1)
    starts = lax.broadcasted_iota(jnp.int32, shape, 0) * CHUNK
    for t in range(group.count):
        low = high = jnp.full(shape, CHUNK, jnp.int32)
        past = [group.edge[group.first + t, p] - starts for p in range(1, group.bins)]
        here = [(q >= 0) & (q < CHUNK) for q in past]
        for q, inside in zip(past, here):
            high = jnp.where(inside, q, high)
        for q, inside in zip(reversed(past), reversed(here)):
            low = jnp.where(inside, q, low)
        group.mask[t, 0] = jnp.where(lanes < low, 1.0, 0.0)
        group.mask[t, 1] = jnp.where(lanes >= high, 1.0, 0.0)
        group.mask[t, 2] = jnp.where(high < CHUNK, 1.0, 0.0)


def sigma_rows(group, t, psd_ref):
    bins = group.bins
    tmpl = group.tmpl[t]
    half = tmpl.shape[0] // 2
    power = (tmpl[:half] * tmpl[:half] + tmpl[half:] * tmpl[half:]) * psd_ref[...]
    shape = power.shape
    ids = lax.broadcasted_iota(jnp.int32, shape, 0) // 2 * LANES + lax.broadcasted_iota(jnp.int32, shape, 1)
    below = [ids < group.edge[group.first + t, p] for p in range(1, bins)]
    parts = []
    for p in range(bins):
        if p == 0:
            member = below[0]
        elif p == bins - 1:
            member = ~below[p - 1]
        else:
            member = below[p] & ~below[p - 1]
        part = jnp.where(member, power, 0.0)
        part = functools.reduce(jnp.add, [part[i : i + 8] for i in range(0, half, 8)])
        part = part + pltpu.roll(part, 4, 0)
        part = part + pltpu.roll(part, 2, 0)
        parts.append(jnp.broadcast_to(jnp.sum(part, axis=1, keepdims=True), (8, LANES)))
    total = functools.reduce(jnp.add, parts)
    for p in range(bins):
        group.inv[t, p] = 1.0 / parts[p]
        group.frac[t, p] = parts[p] / total
    group.inv[t, bins] = 1.0 / total


class Group:
    def __init__(self, tmpl_ref, first, edge_ref, series_ref, inv_ref, frac_ref, mask_ref=None):
        self.tmpl, self.first, self.edge = tmpl_ref, first, edge_ref
        self.series, self.inv, self.frac, self.mask = series_ref, inv_ref, frac_ref, mask_ref
        self.count, self.rows, self.bins = series_ref.shape[0], series_ref.shape[2], edge_ref.shape[1] - 1
        self.chunks = series_ref.shape[1] - (self.bins - 1)

    def chunk_of(self, t, p):
        return lax.shift_right_logical(self.edge[self.first + t, p], CHUNK.bit_length() - 1)

    def inside(self, t, p):
        return self.chunk_of(t, p) == self.chunk_of(t, p + 1)


def product(group, spectra_ref, t, chunk):
    slots = group.rows // 2

    def rows_of(ref, start, step, count):
        parts = [ref[pl.ds(start + d * step, count), :] for d in range(2)]
        return jnp.concatenate([jnp.broadcast_to(part, (slots, LANES)) for part in parts], axis=0)

    tiles = (chunk, group.chunks + chunk)
    tmpl_re, tmpl_im = (rows_of(group.tmpl.at[t], tile * 2, 1, 1) for tile in tiles)
    strain_re, strain_im = (rows_of(spectra_ref, tile * 2 * (slots + 1), slots + 1, slots) for tile in tiles)
    prod_re = tmpl_re * strain_re + tmpl_im * strain_im
    prod_im = tmpl_re * strain_im - tmpl_im * strain_re
    return jnp.concatenate([prod_re, prod_im], axis=1).astype(jnp.bfloat16)


def masked(prod, member):
    member = jnp.broadcast_to(member, (16, LANES)).astype(jnp.bfloat16)
    member = jnp.concatenate([member] * (prod.shape[0] // 16), axis=0)
    return prod * jnp.concatenate([member, member], axis=1)


def add_up(group, spectra_ref, psd_ref, dft_ref, beside=()):
    chunk_masks(group)
    for t in range(group.count):
        sigma_rows(group, t, psd_ref)
    rows = group.rows
    beside = list(beside)
    gap = group.chunks // (len(beside) + 1)
    running = [jnp.zeros((rows, 2 * TIME_LAGS), jnp.float32) for _ in range(group.count)]
    for c in range(group.chunks):
        stack = []
        for t in range(group.count):
            prod = product(group, spectra_ref, t, c)
            stack.append(masked(prod, group.mask[t, 0, c : c + 1, :]))
            stack.append(masked(prod, group.mask[t, 1, c : c + 1, :]))
        got = jnp.dot(jnp.concatenate(stack, axis=0), dft_ref[c], preferred_element_type=jnp.float32)
        for t in range(group.count):
            ended = running[t] + got[2 * t * rows : (2 * t + 1) * rows]
            group.series[t, c] = ended
            cross = jnp.broadcast_to(group.mask[t, 2, c : c + 1, :], (rows, LANES)) > 0.5
            running[t] = jnp.where(cross, got[(2 * t + 1) * rows : (2 * t + 2) * rows], ended)
        if beside and c % gap == gap - 1:
            beside.pop(0)()
    for t in range(group.count):
        group.series[t, group.chunks] = running[t]
    for write in beside:
        write()

    picks = [(t, p) for t in range(group.count) for p in range(1, group.bins - 1)]
    any_inside = functools.reduce(jnp.logical_or, [group.inside(t, p) for t, p in picks])

    @pl.when(any_inside)
    def _():
        def one(i, _):
            t, p = i // (group.bins - 2), i % (group.bins - 2) + 1

            @pl.when(group.inside(t, p))
            def _():
                c, row = group.chunk_of(t, p), group.first + t
                ids = lax.broadcasted_iota(jnp.int32, (1, LANES), 1) + c * CHUNK
                member = jnp.where((ids >= group.edge[row, p]) & (ids < group.edge[row, p + 1]), 1.0, 0.0)
                prod = masked(product(group, spectra_ref, t, c), member)
                group.series[t, group.chunks + p] = jnp.dot(prod, dft_ref[c], preferred_element_type=jnp.float32)

            return 0

        lax.fori_loop(0, len(picks), one, 0)


def test_values(group, t, out_ref):
    slots, bins = group.rows // 2, group.bins
    row = group.first + t

    def spread(ref, p):
        return jnp.concatenate(
            [jnp.broadcast_to(ref[t, p, d : d + 1, :], (slots, LANES)) for d in range(2)], axis=0
        )

    series = [group.series[t, group.chunk_of(t, 1)]]
    for p in range(1, bins - 1):
        at = jnp.where(group.inside(t, p), group.chunks + p, group.chunk_of(t, p + 1))
        series.append(group.series[t, at])
    series.append(group.series[t, group.chunks])
    whole = functools.reduce(jnp.add, series)
    chi = jnp.zeros((group.rows, LANES), jnp.float32)
    for p in range(bins):
        dev = series[p] - spread(group.frac, p) * whole
        chi = chi + dev * dev * spread(group.inv, p)
    chi = jnp.sum(chi[:slots] + chi[slots:], axis=1, keepdims=True) / (TIME_LAGS * 2.0 * 2 * (bins - 1))
    power = whole * whole * spread(group.inv, bins)
    power = power[:slots] + power[slots:]
    power = power + pltpu.roll(power, TIME_LAGS, 1)
    peak = jnp.sqrt(jnp.max(power, axis=1, keepdims=True))
    out_ids = lax.broadcasted_iota(jnp.int32, (slots, LANES), 1)
    out = jnp.where(out_ids == row, peak, out_ref[...])
    out_ref[...] = jnp.where(out_ids == row + group.edge.shape[0], chi, out)


def values_of(group, out_ref):
    return [functools.partial(test_values, group, t, out_ref) for t in range(group.count)]


def own_kernel(
    seg_count,
    other_ref, own_any, tmpl_any, psd_any, dft_any, order_any, seg_any, edge_any,
    spectra_ref, dft_ref, psd_ref, series_ref, inv_ref, frac_ref,
    own_ref, tmpl_ref, order_ref, seg_ref, edge_ref, start_ref, residue_ref, mask_ref, sems,
):
    pairs = [
        (order_any, order_ref), (seg_any, seg_ref), (edge_any, edge_ref), (psd_any, psd_ref),
        (own_any, own_ref), (tmpl_any, tmpl_ref), (dft_any, dft_ref),
    ]
    copies = [pltpu.make_async_copy(src, dst, sems.at[i]) for i, (src, dst) in enumerate(pairs)]
    for copy in copies:
        copy.start()
    for copy in copies[:4]:
        copy.wait()
    seg_starts(seg_ref, start_ref, seg_count)
    inverse_order(order_ref, residue_ref, seg_count)
    arrange_strain(1, other_ref, psd_ref, spectra_ref, start_ref, residue_ref, seg_count)
    copies[4].wait()
    arrange_strain(0, own_ref, psd_ref, spectra_ref, start_ref, residue_ref, seg_count)
    copies[5].wait()
    copies[6].wait()
    first = lax.axis_index("bank") * tmpl_ref.shape[0]
    group = Group(tmpl_ref, first, edge_ref, series_ref, inv_ref, frac_ref, mask_ref)
    add_up(group, spectra_ref, psd_ref, dft_ref)


def next_kernel(
    tmpl_ref, spectra_ref, dft_ref, psd_ref, old_series_ref, old_inv_ref, old_frac_ref, edge_ref,
    out_ref, series_ref, inv_ref, frac_ref,
    mask_ref,
):
    bank = lax.axis_index("bank")
    count = tmpl_ref.shape[0]
    old = Group(None, bank * count, edge_ref, old_series_ref, old_inv_ref, old_frac_ref)
    group = Group(tmpl_ref, (bank ^ 1) * count, edge_ref, series_ref, inv_ref, frac_ref, mask_ref)
    out_ref[...] = jnp.zeros_like(out_ref)
    add_up(group, spectra_ref, psd_ref, dft_ref, values_of(old, out_ref))


def last_kernel(
    seg_count, tmpl_refs,
    spectra_ref, dft_ref, psd_ref, part_ref, old_series_ref, old_inv_ref, old_frac_ref, edge_ref, order_ref, seg_ref,
    out_refs,
    all_ref, placed_ref, start_ref, residue_ref, held,
):
    bank = lax.axis_index("bank")
    seg_starts(seg_ref, start_ref, seg_count)
    inverse_order(order_ref, residue_ref, seg_count)
    all_ref[...] = part_ref[...]
    placed_ref[...] = jnp.zeros_like(placed_ref)
    count = old_series_ref.shape[0]
    group = Group(None, (bank ^ 1) * count, edge_ref, old_series_ref, old_inv_ref, old_frac_ref)
    for s, tmpl_ref in enumerate(tmpl_refs):
        old, group = group, Group(tmpl_ref, (bank ^ (s + 2)) * count, edge_ref, *held[s])
        add_up(group, spectra_ref, psd_ref, dft_ref, values_of(old, all_ref))
    for write in values_of(group, all_ref):
        write()
    pair_slots = all_ref.shape[0] // seg_count
    seg_here = lax.axis_index("seg")
    core, chip = seg_here % 2, seg_here // 2
    ids = lax.broadcasted_iota(jnp.int32, (pair_slots, LANES), 0)
    for m in range(seg_count // 2):
        for source in range(2):
            side = core ^ source
            start, first = first_slot(start_ref, residue_ref, seg_count, m, side)
            live = (seg_ref[0, chip * 2 + source] - first + seg_count - 1) // seg_count
            values = all_ref[pl.ds((m * 2 + side) * pair_slots, pair_slots), :]
            placed_ref[m, pl.ds((start + first) // seg_count, pair_slots), :] = jnp.where(ids < live, values, 0.0)
        out_refs[m][...] = placed_ref[m, :BLK_DEV]


def add_kernel(part_refs, peak_ref, chi_ref):
    tmpl_total = peak_ref.shape[1]
    rows = functools.reduce(jnp.add, [ref[...] for ref in part_refs])
    peak_ref[...] = rows[:, :tmpl_total]
    chi_ref[...] = rows[:, tmpl_total : 2 * tmpl_total]


def swap(x, axis, step):
    return lax.ppermute(x, axis, [(i, i ^ step) for i in range(lax.axis_size(axis))])


def body(strain, templates, inv_psd, seg_blocks, dest_order, bin_edges):
    seg_count, bank_count = lax.axis_size("seg"), lax.axis_size("bank")
    chip_count = seg_count // 2
    slots, detectors, width = strain.shape
    freq_count = width // 2
    tmpl_total, bins = bin_edges.shape[0], bin_edges.shape[1] - 1
    tmpl_count = templates.shape[0]
    rows = detectors * slots
    tiles = detectors * width // LANES
    f32, i32 = jnp.float32, jnp.int32
    dft = jnp.asarray(dft_chunks(freq_count))
    psd = tile_rows(inv_psd)

    other = tile_rows(swap(strain, "seg", 1))
    remote = [tile_rows(swap(templates, "bank", s)) for s in range(1, bank_count)]

    def shape(*dims, dtype=f32):
        return jax.ShapeDtypeStruct(dims, dtype)

    chunks = freq_count // CHUNK
    sums = [(tmpl_count, chunks + bins - 1, rows, 2 * TIME_LAGS)] + [(tmpl_count, bins + 1, 8, LANES)] * 2
    sum_shapes = tuple(shape(*dims) for dims in sums)
    mask = pltpu.VMEM((tmpl_count, 3, chunks, LANES), f32)
    tables = [pltpu.SMEM((seg_count,), i32), pltpu.SMEM((seg_count,), i32)]

    def call(kernel, name, flops, **kwargs):
        return pl.pallas_call(
            kernel,
            name=name,
            cost_estimate=pl.CostEstimate(flops=flops, bytes_accessed=4 * 10**6, transcendentals=0),
            compiler_params=pltpu.CompilerParams(vmem_limit_bytes=40 * 1024 * 1024),
            **kwargs,
        )

    spectra, dft_held, psd_held, *series = call(
        functools.partial(own_kernel, seg_count),
        "own_templates",
        10**9,
        out_shape=(shape((slots + 1) * tiles, LANES), shape(*dft.shape, dtype=dft.dtype), shape(*psd.shape)) + sum_shapes,
        in_specs=[VMEM] + [pl.BlockSpec(memory_space=pltpu.HBM)] * 7,
        out_specs=(VMEM,) * 6,
        scratch_shapes=[
            pltpu.VMEM((slots, tiles, LANES), strain.dtype),
            pltpu.VMEM((tmpl_count, tiles, LANES), f32),
            pltpu.SMEM(dest_order.shape, i32),
            pltpu.SMEM(seg_blocks.shape, i32),
            pltpu.SMEM(bin_edges.shape, i32),
        ]
        + tables
        + [mask, pltpu.SemaphoreType.DMA((7,))],
    )(
        other,
        *[
            pltpu.with_memory_space_constraint(x, pltpu.HBM)
            for x in (tile_rows(strain), tile_rows(templates), psd, dft, dest_order, seg_blocks, bin_edges)
        ],
    )

    part, *series = call(
        next_kernel,
        "next_templates",
        10**9,
        out_shape=(shape(slots, LANES),) + sum_shapes,
        in_specs=[VMEM] * 7 + [SMEM],
        out_specs=(VMEM,) * 4,
        scratch_shapes=[mask],
    )(remote[0], spectra, dft_held, psd_held, *series, bin_edges)

    left = bank_count - 2

    def last(*refs):
        ins, outs, held = refs[: left + 10], refs[left + 10 : left + 10 + chip_count], refs[left + 10 + chip_count :]
        groups = [held[4 + 4 * s : 8 + 4 * s] for s in range(left)]
        last_kernel(seg_count, ins[:left], *ins[left:], outs, *held[:4], groups)

    parts = call(
        last,
        "last_templates",
        2 * 10**9,
        out_shape=(shape(BLK_DEV, LANES),) * chip_count,
        in_specs=[VMEM] * (left + 7) + [SMEM] * 3,
        out_specs=(VMEM,) * chip_count,
        scratch_shapes=[pltpu.VMEM((slots, LANES), f32), pltpu.VMEM((chip_count, BLK_DEV + 8, LANES), f32)]
        + tables
        + ([pltpu.VMEM(dims, f32) for dims in sums] + [mask]) * left,
    )(*remote[1:], spectra, dft_held, psd_held, part, *series, bin_edges, dest_order, seg_blocks)

    got = [swap(parts[m], "seg", 2 * m) for m in reversed(range(1, chip_count))] + [parts[0]]
    return call(
        lambda *refs: add_kernel(refs[:chip_count], *refs[chip_count:]),
        "add_rows",
        10**5,
        out_shape=(shape(BLK_DEV, tmpl_total),) * 2,
        in_specs=[VMEM] * chip_count,
        out_specs=(VMEM, VMEM),
    )(*got)


def solution(mesh):
    return jax.shard_map(
        body,
        mesh=mesh,
        in_specs=(
            P(("bank", "seg"), None, None),
            P("bank", None, None),
            P(),
            P("bank", None),
            P("bank", None),
            P(),
        ),
        out_specs=(P(("bank", "seg"), None), P(("bank", "seg"), None)),
        check_vma=False,
    )
```

time: 117 us -> 23.6 us (0.20)
  other arithmetic: 43.1 us -> 0 us
  matrix products: 26.5 us -> 0 us
  local copies, waits for them, and re-layouts: 17.8 us -> 0.02 us
  blocking collectives: 11.3 us -> 0 us
  Pallas kernels: 0 us -> 8.82 us
  waiting for transfers between devices: 7.4 us -> 4.84 us
    dot_general x9 -> x0, matrix products: 26.5 us -> none  [the longest x6 24.8 us: filter_core(): lax.dot_general(dft_rows, flattened, (((0,), (1,)), ((), ())), preferred_...]
    another operation x17 -> x0, other arithmetic: 22 us -> none
    all_gather x1 -> x0, blocking collectives: 11.3 us -> none  [filter_all(): piece = lax.all_gather(templates, 'bank', axis=0, tiled=True)]
    ppermute x0 -> x7, starting transfers between devices: none -> 9.09 us  [swap(): lax.ppermute(x, axis, [(i, i ^ step) for i in range(lax.axis_size(axis))])]
    pallas_call x0 -> x4, Pallas kernels: none -> 8.82 us  [the longest x1 3.58 us: body(): call(last, 'last_templates', 2 * 10 ** 9, out_shape=(shape(BLK_DEV, LANES...]
    all_to_all x2 -> x0, starting transfers between devices: 8.22 us -> none  [the longest x1 4.88 us: body(): lax.all_to_all(peak_out, 'seg', split_axis=0, concat_axis=0, tiled=True)]
    mul x7 -> x0, other arithmetic: 7.68 us -> none  [the longest x6 7.17 us: filter_core(): prod_re = (tmpl_re * strain_re + tmpl_im * strain_im) * weights]
    all_to_all x2 -> x0, waiting for transfers between devices: 7.4 us -> none  [the longest x1 4.42 us: body(): lax.all_to_all(chisq_out, 'seg', split_axis=0, concat_axis=0, tiled=True)]
  transfers between devices with their start and end apart: 2 -> 7, of which waited for: 2 -> 4; matrix products, arithmetic and copies ran while one was open for 3% -> 0% of each run, Pallas kernels for 0% -> 19%
where the time goes in v2:
time: 23.6 us; the launch traced here: 23.5 us
  starting transfers between devices  9.09 us (39%)
  Pallas kernels  8.82 us (37%)
  waiting for transfers between devices  4.84 us (21%)
  between operations  0.69 us (3%)
    ppermute x7, starting transfers between devices, swap(): lax.ppermute(x, axis, [(i, i ^ step) for i in range(lax.axis_size(axis))])  9.09 us
    ppermute x7, waiting for transfers between devices, swap(): lax.ppermute(x, axis, [(i, i ^ step) for i in range(lax.axis_size(axis))])  4.84 us
    pallas_call x1, Pallas kernels, body(): call(last, 'last_templates', 2 * 10 ** 9, out_shape=(shape(BLK_DEV, LANES...  3.58 us
    pallas_call x1, Pallas kernels, body(): call(functools.partial(own_kernel, seg_count), 'own_templates', 10 ** 9,...  2.6 us
    pallas_call x1, Pallas kernels, body(): call(next_kernel, 'next_templates', 10 ** 9, out_shape=(shape(slots, LANE...  1.96 us
    pallas_call x1, Pallas kernels, body(): call(lambda *refs: add_kernel(refs[:chip_count], *refs[chip_count:]), 'ad...  0.67 us
  transfers between devices with their start and end apart: 7, of which 4 were waited for; matrix products, arithmetic and copies ran while one was open for 0% of the time, Pallas kernels for 19%

profile of v2, /device:TPU:0, one launch (start us, length us, event | category | flops | bytes accessed | tf_op | source)
XLA Modules:
  0.0 23.5 jit_solution(11474427529592640949)
XLA Ops:
  0.6 0.0 copy-start
  0.6 0.5 %collective-permute-start.2 = (bf16[32,2,4096]{2,1,0:T(2,128)(2,1)}, bf16[32,2,4096]{2,1,0:T(2,128)(2,1)S(1)}, u32[]{:S(2)}, u32[]{:S(2)}) collective-permute-start(bf16[32,2,4096]{2,1,0:T(2,128)(2,1)} %param.7), channel_id=1, source_target_pairs={{0,1},{1,0},{2,3},{3,2},{4,5},{5,4},{6,7},{7,6},{8,9},{9,8},{10,11... | collective-permute-start | bytes 1572872 | tf_op jit(solution)/shard_map/ppermute | solution.py:308
  1.2 2.6 %collective-permute-start.3 = (f32[3,2,4096]{2,1,0:T(2,128)}, f32[3,2,4096]{2,1,0:T(2,128)S(1)}, u32[]{:S(2)}, u32[]{:S(2)}) collective-permute-start(f32[3,2,4096]{2,1,0:T(2,128)} %param.8), channel_id=1, source_target_pairs={{0,8},{8,0},{16,24},{24,16},{1,9},{9,1},{17,25},{25,17},{2,10},{10... | collective-permute-start | bytes 294920 | tf_op jit(solution)/shard_map/ppermute | solution.py:308
  3.7 1.5 %collective-permute-start = (f32[3,2,4096]{2,1,0:T(2,128)}, f32[3,2,4096]{2,1,0:T(2,128)S(1)}, u32[]{:S(2)}, u32[]{:S(2)}) collective-permute-start(f32[3,2,4096]{2,1,0:T(2,128)} %param.8), channel_id=1, source_target_pairs={{0,16},{8,24},{16,0},{24,8},{1,17},{9,25},{17,1},{25,9},{2,18},{10... | collective-permute-start | bytes 294920 | tf_op jit(solution)/shard_map/ppermute | solution.py:308
  5.2 0.0 collective-permute-start.1
  5.3 0.0 collective-permute-done.2
  5.3 2.6 %own_templates.1 = (f32[2112,128]{1,0:T(8,128)S(1)}, bf16[16,256,128]{2,1,0:T(8,128)(2,1)S(1)}, f32[32,128]{1,0:T(8,128)S(1)}, f32[3,23,64,128]{3,2,1,0:T(8,128)...) custom-call(bf16[32,64,128]{2,1,0:T(8,128)(2,1)S(1)} %bitcast.36, bf16[32,64,128]{2,1,0:T(8,128)(2,1)} %bitcast.39, ...), custom_call_target="tpu_custom_call" | custom-call | flops 1000000000 | bytes 4000000 | tf_op jit(solution)/shard_map/own_templates/pallas_call | solution.py:345
  7.9 0.0 collective-permute-done.3
  7.9 0.0 copy-done
  7.9 0.0 copy-start.1
  7.9 0.0 copy-start.2
  7.9 2.0 %next_templates.1 = (f32[32,128]{1,0:T(8,128)S(1)}, f32[3,23,64,128]{3,2,1,0:T(8,128)S(1)}, f32[3,9,8,128]{3,2,1,0:T(8,128)S(1)}, f32[3,9,8,128]{3,2,1,0:T(8,128)S(1)}) custom-call(f32[3,64,128]{2,1,0:T(8,128)S(1)} %bitcast.35, f32[2112,128]{1,0:T(8,128)S(1)} %get-tuple-element.16.spectra_ref.refs_2_, ...), custom_call_target="tpu_custom_call" | custom-call | flops 1000000000 | bytes 4000000 | tf_op jit(solution)/shard_map/next_templates/pallas_call | solution.py:369
  9.9 0.1 collective-permute-done
  10.1 0.9 %collective-permute-done.1 = f32[3,2,4096]{2,1,0:T(2,128)S(1)} collective-permute-done((f32[3,2,4096]{2,1,0:T(2,128)}, f32[3,2,4096]{2,1,0:T(2,128)S(1)}, u32[]{:S(2)}, u32[]{:S(2)}) %collective-permute-start.1) | collective-permute-done | bytes 98336 | tf_op jit(solution)/shard_map/ppermute | solution.py:308
  11.0 0.0 copy-done.1
  11.0 0.0 copy-done.2
  11.0 3.6 %last_templates.1 = (f32[16,128]{1,0:T(8,128)S(1)}, f32[16,128]{1,0:T(8,128)S(1)}, f32[16,128]{1,0:T(8,128)S(1)}, f32[16,128]{1,0:T(8,128)S(1)}) custom-call(f32[3,64,128]{2,1,0:T(8,128)S(1)} %bitcast.37, f32[3,64,128]{2,1,0:T(8,128)S(1)} %bitcast.38, f32[2112,128]{1,0:T(8,128)S(1)} %get-tuple-element.16.spectra_ref.refs_2_, ...), custom_call_target="tpu_custom_call" | custom-call | flops 2000000000 | bytes 4000000 | tf_op jit(solution)/shard_map/last_templates/pallas_call | solution.py:386
  14.6 3.7 %collective-permute-start.4 = (f32[16,128]{1,0:T(8,128)S(1)}, f32[16,128]{1,0:T(8,128)S(1)}, u32[]{:S(2)}, u32[]{:S(2)}) collective-permute-start(f32[16,128]{1,0:T(8,128)S(1)} %get-tuple-element.26), channel_id=1, source_target_pairs={{0,6},{1,7},{2,4},{3,5},{4,2},{5,3},{6,0},{7,1},{8,14},{9,15},{10,... | collective-permute-start | bytes 24584 | tf_op jit(solution)/shard_map/ppermute | solution.py:308
  18.2 0.0 collective-permute-start.5
  18.2 0.8 %collective-permute-start.6 = (f32[16,128]{1,0:T(8,128)S(1)}, f32[16,128]{1,0:T(8,128)S(1)}, u32[]{:S(2)}, u32[]{:S(2)}) collective-permute-start(f32[16,128]{1,0:T(8,128)S(1)} %get-tuple-element.28), channel_id=1, source_target_pairs={{0,2},{1,3},{2,0},{3,1},{4,6},{5,7},{6,4},{7,5},{8,10},{9,11},{10,... | collective-permute-start | bytes 24584 | tf_op jit(solution)/shard_map/ppermute | solution.py:308
  19.0 1.1 %collective-permute-done.4.refs_0_ = f32[16,128]{1,0:T(8,128)S(1)} collective-permute-done((f32[16,128]{1,0:T(8,128)S(1)}, f32[16,128]{1,0:T(8,128)S(1)}, u32[]{:S(2)}, u32[]{:S(2)}) %collective-permute-start.4) | collective-permute-done | bytes 8224 | tf_op jit(solution)/shard_map/ppermute | solution.py:308
  20.1 2.7 %collective-permute-done.5.refs_1_ = f32[16,128]{1,0:T(8,128)S(1)} collective-permute-done((f32[16,128]{1,0:T(8,128)S(1)}, f32[16,128]{1,0:T(8,128)S(1)}, u32[]{:S(2)}, u32[]{:S(2)}) %collective-permute-start.5) | collective-permute-done | bytes 8224 | tf_op jit(solution)/shard_map/ppermute | solution.py:308
  22.8 0.0 collective-permute-done.6.refs_2_
  22.8 0.7 %add_rows.1 = (f32[16,12]{1,0:T(8,128)}, f32[16,12]{1,0:T(8,128)}) custom-call(f32[16,128]{1,0:T(8,128)S(1)} %collective-permute-done.4.refs_0_, f32[16,128]{1,0:T(8,128)S(1)} %collective-permute-done.5.refs_1_, f32[16,128]{1,0:T(8,128)S(1)} %collective-permute-done.6.refs_2_, f32[16,128]{1,0:T(8,128)S(1)} %get-tuple-element.29.refs_3_), custom_call_target="tpu_custom_call" | custom-call | flops 100000 | bytes 4000000 | tf_op jit(solution)/shard_map/add_rows/pallas_call | solution.py:399
Async XLA Ops:
  0.6 7.3 %copy-start = (s32[12,9]{1,0:T(8,128)S(1)}, s32[12,9]{1,0:T(8,128)}, u32[]{:S(2)}) copy-start(s32[12,9]{1,0:T(8,128)} %refs_9_.1) | copy-start | bytes 1300
  0.6 4.6 %collective-permute-start.2 = (bf16[32,2,4096]{2,1,0:T(2,128)(2,1)}, bf16[32,2,4096]{2,1,0:T(2,128)(2,1)S(1)}, u32[]{:S(2)}, u32[]{:S(2)}) collective-permute-start(bf16[32,2,4096]{2,1,0:T(2,128)(2,1)} %param.7), channel_id=1, source_target_pairs={{0,1},{1,0},{2,3},{3,2},{4,5},{5,4},{6,7},{7,6},{8,9},{9,8},{10,11... | collective-permute-start | bytes 1572872 | tf_op jit(solution)/shard_map/ppermute | solution.py:308
  1.2 6.7 %collective-permute-start.3 = (f32[3,2,4096]{2,1,0:T(2,128)}, f32[3,2,4096]{2,1,0:T(2,128)S(1)}, u32[]{:S(2)}, u32[]{:S(2)}) collective-permute-start(f32[3,2,4096]{2,1,0:T(2,128)} %param.8), channel_id=1, source_target_pairs={{0,8},{8,0},{16,24},{24,16},{1,9},{9,1},{17,25},{25,17},{2,10},{10... | collective-permute-start | bytes 294920 | tf_op jit(solution)/shard_map/ppermute | solution.py:308
  3.7 6.3 %collective-permute-start = (f32[3,2,4096]{2,1,0:T(2,128)}, f32[3,2,4096]{2,1,0:T(2,128)S(1)}, u32[]{:S(2)}, u32[]{:S(2)}) collective-permute-start(f32[3,2,4096]{2,1,0:T(2,128)} %param.8), channel_id=1, source_target_pairs={{0,16},{8,24},{16,0},{24,8},{1,17},{9,25},{17,1},{25,9},{2,18},{10... | collective-permute-start | bytes 294920 | tf_op jit(solution)/shard_map/ppermute | solution.py:308
  5.2 5.7 %collective-permute-start.1 = (f32[3,2,4096]{2,1,0:T(2,128)}, f32[3,2,4096]{2,1,0:T(2,128)S(1)}, u32[]{:S(2)}, u32[]{:S(2)}) collective-permute-start(f32[3,2,4096]{2,1,0:T(2,128)} %param.8), channel_id=1, source_target_pairs={{0,24},{8,16},{16,8},{24,0},{1,25},{9,17},{17,9},{25,1},{2,26},{10... | collective-permute-start | bytes 294920 | tf_op jit(solution)/shard_map/ppermute | solution.py:308
  7.9 3.1 %copy-start.1 = (s32[1,8]{1,0:T(1,128)S(1)}, s32[1,8]{1,0:T(1,128)}, u32[]{:S(2)}) copy-start(s32[1,8]{1,0:T(1,128)} %refs_10_.1) | copy-start | bytes 100
  7.9 3.1 %copy-start.2 = (s32[1,8]{1,0:T(1,128)S(1)}, s32[1,8]{1,0:T(1,128)}, u32[]{:S(2)}) copy-start(s32[1,8]{1,0:T(1,128)} %refs_11_.1) | copy-start | bytes 100
  14.6 5.5 %collective-permute-start.4 = (f32[16,128]{1,0:T(8,128)S(1)}, f32[16,128]{1,0:T(8,128)S(1)}, u32[]{:S(2)}, u32[]{:S(2)}) collective-permute-start(f32[16,128]{1,0:T(8,128)S(1)} %get-tuple-element.26), channel_id=1, source_target_pairs={{0,6},{1,7},{2,4},{3,5},{4,2},{5,3},{6,0},{7,1},{8,14},{9,15},{10,... | collective-permute-start | bytes 24584 | tf_op jit(solution)/shard_map/ppermute | solution.py:308
  18.2 4.5 %collective-permute-start.5 = (f32[16,128]{1,0:T(8,128)S(1)}, f32[16,128]{1,0:T(8,128)S(1)}, u32[]{:S(2)}, u32[]{:S(2)}) collective-permute-start(f32[16,128]{1,0:T(8,128)S(1)} %get-tuple-element.27), channel_id=1, source_target_pairs={{0,4},{1,5},{2,6},{3,7},{4,0},{5,1},{6,2},{7,3},{8,12},{9,13},{10,... | collective-permute-start | bytes 24584 | tf_op jit(solution)/shard_map/ppermute | solution.py:308
  18.2 4.5 %collective-permute-start.6 = (f32[16,128]{1,0:T(8,128)S(1)}, f32[16,128]{1,0:T(8,128)S(1)}, u32[]{:S(2)}, u32[]{:S(2)}) collective-permute-start(f32[16,128]{1,0:T(8,128)S(1)} %get-tuple-element.28), channel_id=1, source_target_pairs={{0,2},{1,3},{2,0},{3,1},{4,6},{5,7},{6,4},{7,5},{8,10},{9,11},{10,... | collective-permute-start | bytes 24584 | tf_op jit(solution)/shard_map/ppermute | solution.py:308

commit v3 on v2

--- a/solution.py
+++ b/solution.py
@@ -32,16 +32,21 @@
     return tiles.reshape(lead + (detectors * width // LANES, LANES))
 
 
-def seg_starts(seg_ref, start_ref, seg_count):
+def core_here():
+    return lax.axis_index("seg") % 2
+
+
+def seg_starts(seg_ref, start_ref, seg_count, in_vmem=False):
     total = jnp.int32(0)
     for s in range(seg_count):
         start_ref[s] = total
-        total = total + seg_ref[0, s]
-
-
-def inverse_order(order_ref, residue_ref, seg_count):
+        total = total + seg_ref[:, s : s + 1][0, 0] if in_vmem else total + seg_ref[0, s]
+    start_ref[seg_count] = total
+
+
+def inverse_order(order_ref, residue_ref, seg_count, in_vmem=False):
     for r in range(seg_count):
-        residue_ref[order_ref[0, r]] = jnp.int32(r)
+        residue_ref[order_ref[:, r : r + 1][0, 0] if in_vmem else order_ref[0, r]] = jnp.int32(r)
 
 
 def first_slot(start_ref, residue_ref, seg_count, m, side):
@@ -70,7 +75,7 @@
     starts = lax.broadcasted_iota(jnp.int32, shape, 0) * CHUNK
     for t in range(group.count):
         low = high = jnp.full(shape, CHUNK, jnp.int32)
-        past = [group.edge[group.first + t, p] - starts for p in range(1, group.bins)]
+        past = [group.edge_rows(t, p, shape) - starts for p in range(1, group.bins)]
         here = [(q >= 0) & (q < CHUNK) for q in past]
         for q, inside in zip(past, here):
             high = jnp.where(inside, q, high)
@@ -88,7 +93,7 @@
     power = (tmpl[:half] * tmpl[:half] + tmpl[half:] * tmpl[half:]) * psd_ref[...]
     shape = power.shape
     ids = lax.broadcasted_iota(jnp.int32, shape, 0) // 2 * LANES + lax.broadcasted_iota(jnp.int32, shape, 1)
-    below = [ids < group.edge[group.first + t, p] for p in range(1, bins)]
+    below = [ids < group.edge_rows(t, p, shape) for p in range(1, bins)]
     parts = []
     for p in range(bins):
         if p == 0:
@@ -110,14 +115,20 @@
 
 
 class Group:
-    def __init__(self, tmpl_ref, first, edge_ref, series_ref, inv_ref, frac_ref, mask_ref=None):
-        self.tmpl, self.first, self.edge = tmpl_ref, first, edge_ref
+    def __init__(self, tmpl_ref, first, splat_ref, series_ref, inv_ref, frac_ref, mask_ref=None):
+        self.tmpl, self.first, self.splat = tmpl_ref, first, splat_ref
         self.series, self.inv, self.frac, self.mask = series_ref, inv_ref, frac_ref, mask_ref
-        self.count, self.rows, self.bins = series_ref.shape[0], series_ref.shape[2], edge_ref.shape[1] - 1
+        self.count, self.rows, self.bins = series_ref.shape[0], series_ref.shape[2], splat_ref.shape[0] - 1
         self.chunks = series_ref.shape[1] - (self.bins - 1)
 
+    def edge_rows(self, t, p, shape):
+        return jnp.broadcast_to(self.splat[p, pl.ds(self.first + t, 1), :], shape)
+
+    def edge(self, t, p):
+        return self.splat[p, pl.ds(self.first + t, 1), :][0, 0]
+
     def chunk_of(self, t, p):
-        return lax.shift_right_logical(self.edge[self.first + t, p], CHUNK.bit_length() - 1)
+        return lax.shift_right_logical(self.edge(t, p), CHUNK.bit_length() - 1)
 
     def inside(self, t, p):
         return self.chunk_of(t, p) == self.chunk_of(t, p + 1)
@@ -149,8 +160,7 @@
     for t in range(group.count):
         sigma_rows(group, t, psd_ref)
     rows = group.rows
-    beside = list(beside)
-    gap = group.chunks // (len(beside) + 1)
+    beside = dict(beside)
     running = [jnp.zeros((rows, 2 * TIME_LAGS), jnp.float32) for _ in range(group.count)]
     for c in range(group.chunks):
         stack = []
@@ -164,15 +174,14 @@
             group.series[t, c] = ended
             cross = jnp.broadcast_to(group.mask[t, 2, c : c + 1, :], (rows, LANES)) > 0.5
             running[t] = jnp.where(cross, got[(2 * t + 1) * rows : (2 * t + 2) * rows], ended)
-        if beside and c % gap == gap - 1:
-            beside.pop(0)()
+        for write in beside.get(c, ()):
+            write()
     for t in range(group.count):
         group.series[t, group.chunks] = running[t]
-    for write in beside:
-        write()
-
-    picks = [(t, p) for t in range(group.count) for p in range(1, group.bins - 1)]
-    any_inside = functools.reduce(jnp.logical_or, [group.inside(t, p) for t, p in picks])
+
+    chunk_of = [[group.chunk_of(t, p) for p in range(1, group.bins)] for t in range(group.count)]
+    pairs = [pair for row in chunk_of for pair in zip(row, row[1:])]
+    any_inside = functools.reduce(jnp.logical_or, [a == b for a, b in pairs])
 
     @pl.when(any_inside)
     def _():
@@ -181,15 +190,15 @@
 
             @pl.when(group.inside(t, p))
             def _():
-                c, row = group.chunk_of(t, p), group.first + t
+                c = group.chunk_of(t, p)
                 ids = lax.broadcasted_iota(jnp.int32, (1, LANES), 1) + c * CHUNK
-                member = jnp.where((ids >= group.edge[row, p]) & (ids < group.edge[row, p + 1]), 1.0, 0.0)
+                member = jnp.where((ids >= group.edge(t, p)) & (ids < group.edge(t, p + 1)), 1.0, 0.0)
                 prod = masked(product(group, spectra_ref, t, c), member)
                 group.series[t, group.chunks + p] = jnp.dot(prod, dft_ref[c], preferred_element_type=jnp.float32)
 
             return 0
 
-        lax.fori_loop(0, len(picks), one, 0)
+        lax.fori_loop(0, len(pairs), one, 0)
 
 
 def test_values(group, t, out_ref):
@@ -201,9 +210,10 @@
             [jnp.broadcast_to(ref[t, p, d : d + 1, :], (slots, LANES)) for d in range(2)], axis=0
         )
 
-    series = [group.series[t, group.chunk_of(t, 1)]]
+    chunk_of = [group.chunk_of(t, p) for p in range(1, bins)]
+    series = [group.series[t, chunk_of[0]]]
     for p in range(1, bins - 1):
-        at = jnp.where(group.inside(t, p), group.chunks + p, group.chunk_of(t, p + 1))
+        at = jnp.where(chunk_of[p - 1] == chunk_of[p], group.chunks + p, chunk_of[p])
         series.append(group.series[t, at])
     series.append(group.series[t, group.chunks])
     whole = functools.reduce(jnp.add, series)
@@ -218,7 +228,7 @@
     peak = jnp.sqrt(jnp.max(power, axis=1, keepdims=True))
     out_ids = lax.broadcasted_iota(jnp.int32, (slots, LANES), 1)
     out = jnp.where(out_ids == row, peak, out_ref[...])
-    out_ref[...] = jnp.where(out_ids == row + group.edge.shape[0], chi, out)
+    out_ref[...] = jnp.where(out_ids == row + group.splat.shape[1], chi, out)
 
 
 def values_of(group, out_ref):
@@ -228,72 +238,92 @@
 def own_kernel(
     seg_count,
     other_ref, own_any, tmpl_any, psd_any, dft_any, order_any, seg_any, edge_any,
-    spectra_ref, dft_ref, psd_ref, series_ref, inv_ref, frac_ref,
-    own_ref, tmpl_ref, order_ref, seg_ref, edge_ref, start_ref, residue_ref, mask_ref, sems,
+    spectra_ref, dft_ref, psd_ref, splat_ref, order_lanes_ref, seg_lanes_ref, series_ref, inv_ref, frac_ref,
+    own_ref, tmpl_ref, lanes_ref, order_ref, seg_ref, start_ref, residue_ref, mask_ref, sems,
 ):
     pairs = [
-        (order_any, order_ref), (seg_any, seg_ref), (edge_any, edge_ref), (psd_any, psd_ref),
-        (own_any, own_ref), (tmpl_any, tmpl_ref), (dft_any, dft_ref),
+        (order_any, order_ref), (seg_any, seg_ref), (psd_any, psd_ref), (edge_any, lanes_ref), (tmpl_any, tmpl_ref),
+        (own_any, own_ref), (dft_any, dft_ref), (order_any, order_lanes_ref), (seg_any, seg_lanes_ref),
     ]
     copies = [pltpu.make_async_copy(src, dst, sems.at[i]) for i, (src, dst) in enumerate(pairs)]
     for copy in copies:
         copy.start()
     for copy in copies[:4]:
         copy.wait()
+    for p in range(splat_ref.shape[0]):
+        splat_ref[p] = jnp.broadcast_to(lanes_ref[:, p : p + 1], splat_ref.shape[1:])
     seg_starts(seg_ref, start_ref, seg_count)
     inverse_order(order_ref, residue_ref, seg_count)
     arrange_strain(1, other_ref, psd_ref, spectra_ref, start_ref, residue_ref, seg_count)
     copies[4].wait()
+    copies[5].wait()
     arrange_strain(0, own_ref, psd_ref, spectra_ref, start_ref, residue_ref, seg_count)
-    copies[5].wait()
-    copies[6].wait()
+    for copy in copies[6:]:
+        copy.wait()
     first = lax.axis_index("bank") * tmpl_ref.shape[0]
-    group = Group(tmpl_ref, first, edge_ref, series_ref, inv_ref, frac_ref, mask_ref)
+    group = Group(tmpl_ref, first, splat_ref, series_ref, inv_ref, frac_ref, mask_ref)
     add_up(group, spectra_ref, psd_ref, dft_ref)
 
 
 def next_kernel(
-    tmpl_ref, spectra_ref, dft_ref, psd_ref, old_series_ref, old_inv_ref, old_frac_ref, edge_ref,
-    out_ref, series_ref, inv_ref, frac_ref,
-    mask_ref,
+    tmpl_ref, spectra_ref, dft_ref, psd_ref, splat_ref, old_series_ref, old_inv_ref, old_frac_ref,
+    out_ref, series_ref, inv_ref, frac_ref, mask_ref,
 ):
-    bank = lax.axis_index("bank")
-    count = tmpl_ref.shape[0]
-    old = Group(None, bank * count, edge_ref, old_series_ref, old_inv_ref, old_frac_ref)
-    group = Group(tmpl_ref, (bank ^ 1) * count, edge_ref, series_ref, inv_ref, frac_ref, mask_ref)
+    bank, count = lax.axis_index("bank"), tmpl_ref.shape[0]
     out_ref[...] = jnp.zeros_like(out_ref)
-    add_up(group, spectra_ref, psd_ref, dft_ref, values_of(old, out_ref))
+    old = Group(None, bank * count, splat_ref, old_series_ref, old_inv_ref, old_frac_ref)
+    group = Group(tmpl_ref, (bank ^ (1 + core_here())) * count, splat_ref, series_ref, inv_ref, frac_ref, mask_ref)
+    beside = {4 * n + 3: [write] for n, write in enumerate(values_of(old, out_ref))}
+    add_up(group, spectra_ref, psd_ref, dft_ref, beside)
+    for write in values_of(group, out_ref):
+        write()
+
+
+def mid_kernel(source, old_source, tmpl_ref, spectra_ref, dft_ref, psd_ref, splat_ref, old, out_ref, sums, mask_ref):
+    bank, count = lax.axis_index("bank"), tmpl_ref.shape[0]
+    group = Group(tmpl_ref, (bank ^ source()) * count, splat_ref, *sums, mask_ref)
+    out_ref[...] = old[0][...]
+    beside = {}
+    if old_source is not None:
+        writes = values_of(Group(None, (bank ^ old_source()) * count, splat_ref, *old[1:]), out_ref)
+        beside = {4 * n + 3: [write] for n, write in enumerate(writes)}
+    add_up(group, spectra_ref, psd_ref, dft_ref, beside)
 
 
 def last_kernel(
-    seg_count, tmpl_refs,
-    spectra_ref, dft_ref, psd_ref, part_ref, old_series_ref, old_inv_ref, old_frac_ref, edge_ref, order_ref, seg_ref,
-    out_refs,
-    all_ref, placed_ref, start_ref, residue_ref, held,
+    seg_count, sources, tmpl_ref, spectra_ref, dft_ref, psd_ref, splat_ref, order_ref, seg_ref, old_sums, part_ref,
+    out_refs, sums, mask_ref, all_ref, placed_ref, start_ref, residue_ref, place_ref,
 ):
-    bank = lax.axis_index("bank")
-    seg_starts(seg_ref, start_ref, seg_count)
-    inverse_order(order_ref, residue_ref, seg_count)
-    all_ref[...] = part_ref[...]
-    placed_ref[...] = jnp.zeros_like(placed_ref)
-    count = old_series_ref.shape[0]
-    group = Group(None, (bank ^ 1) * count, edge_ref, old_series_ref, old_inv_ref, old_frac_ref)
-    for s, tmpl_ref in enumerate(tmpl_refs):
-        old, group = group, Group(tmpl_ref, (bank ^ (s + 2)) * count, edge_ref, *held[s])
-        add_up(group, spectra_ref, psd_ref, dft_ref, values_of(old, all_ref))
-    for write in values_of(group, all_ref):
-        write()
     pair_slots = all_ref.shape[0] // seg_count
     seg_here = lax.axis_index("seg")
     core, chip = seg_here % 2, seg_here // 2
+
+    def place():
+        seg_starts(seg_ref, start_ref, seg_count, in_vmem=True)
+        inverse_order(order_ref, residue_ref, seg_count, in_vmem=True)
+        for m in range(seg_count // 2):
+            for source in range(2):
+                start, first = first_slot(start_ref, residue_ref, seg_count, m, core ^ source)
+                stop = start_ref[chip * 2 + source + 1]
+                live = (stop - start - first + seg_count - 1) // seg_count
+                place_ref[4 * m + 2 * source] = (start + first) // seg_count
+                place_ref[4 * m + 2 * source + 1] = live
+
+    bank, count = lax.axis_index("bank"), tmpl_ref.shape[0]
+    all_ref[...] = part_ref[...]
+    placed_ref[...] = jnp.zeros_like(placed_ref)
+    old = Group(None, (bank ^ sources[0]()) * count, splat_ref, *old_sums)
+    group = Group(tmpl_ref, (bank ^ sources[1]()) * count, splat_ref, *sums, mask_ref)
+    writes = values_of(old, all_ref)
+    add_up(group, spectra_ref, psd_ref, dft_ref, {3: writes[:1], 6: writes[1:2], 8: [place], 9: writes[2:]})
+    for write in values_of(group, all_ref):
+        write()
     ids = lax.broadcasted_iota(jnp.int32, (pair_slots, LANES), 0)
     for m in range(seg_count // 2):
         for source in range(2):
-            side = core ^ source
-            start, first = first_slot(start_ref, residue_ref, seg_count, m, side)
-            live = (seg_ref[0, chip * 2 + source] - first + seg_count - 1) // seg_count
-            values = all_ref[pl.ds((m * 2 + side) * pair_slots, pair_slots), :]
-            placed_ref[m, pl.ds((start + first) // seg_count, pair_slots), :] = jnp.where(ids < live, values, 0.0)
+            values = all_ref[pl.ds((m * 2 + (core ^ source)) * pair_slots, pair_slots), :]
+            values = jnp.where(ids < place_ref[4 * m + 2 * source + 1], values, 0.0)
+            placed_ref[m, pl.ds(place_ref[4 * m + 2 * source], pair_slots), :] = values
         out_refs[m][...] = placed_ref[m, :BLK_DEV]
 
 
@@ -322,7 +352,9 @@
     psd = tile_rows(inv_psd)
 
     other = tile_rows(swap(strain, "seg", 1))
-    remote = [tile_rows(swap(templates, "bank", s)) for s in range(1, bank_count)]
+    far = [tile_rows(swap(templates, "bank", s)) for s in range(3, bank_count)]
+    near = [(b * seg_count + s, (b ^ (1 + s % 2)) * seg_count + s) for b in range(bank_count) for s in range(seg_count)]
+    near = lax.ppermute(templates, ("bank", "seg"), near)
 
     def shape(*dims, dtype=f32):
         return jax.ShapeDtypeStruct(dims, dtype)
@@ -331,69 +363,94 @@
     sums = [(tmpl_count, chunks + bins - 1, rows, 2 * TIME_LAGS)] + [(tmpl_count, bins + 1, 8, LANES)] * 2
     sum_shapes = tuple(shape(*dims) for dims in sums)
     mask = pltpu.VMEM((tmpl_count, 3, chunks, LANES), f32)
-    tables = [pltpu.SMEM((seg_count,), i32), pltpu.SMEM((seg_count,), i32)]
-
-    def call(kernel, name, flops, **kwargs):
+    tables = [pltpu.SMEM((seg_count + 1,), i32), pltpu.SMEM((seg_count,), i32)]
+
+    def call(kernel, name, flops, bytes_accessed=4 * 10**6, **kwargs):
         return pl.pallas_call(
             kernel,
             name=name,
-            cost_estimate=pl.CostEstimate(flops=flops, bytes_accessed=4 * 10**6, transcendentals=0),
+            cost_estimate=pl.CostEstimate(flops=flops, bytes_accessed=bytes_accessed, transcendentals=0),
             compiler_params=pltpu.CompilerParams(vmem_limit_bytes=40 * 1024 * 1024),
             **kwargs,
         )
 
-    spectra, dft_held, psd_held, *series = call(
+    hbm = pl.BlockSpec(memory_space=pltpu.HBM)
+
+    def in_hbm(*arrays):
+        return [pltpu.with_memory_space_constraint(x, pltpu.HBM) for x in arrays]
+
+    splat_shape = shape(bins + 1, tmpl_total, LANES, dtype=i32)
+    spectra, dft_held, psd_held, splat, order_held, seg_held, *own_sums = call(
         functools.partial(own_kernel, seg_count),
         "own_templates",
         10**9,
-        out_shape=(shape((slots + 1) * tiles, LANES), shape(*dft.shape, dtype=dft.dtype), shape(*psd.shape)) + sum_shapes,
-        in_specs=[VMEM] + [pl.BlockSpec(memory_space=pltpu.HBM)] * 7,
-        out_specs=(VMEM,) * 6,
+        out_shape=(shape((slots + 1) * tiles, LANES), shape(*dft.shape, dtype=dft.dtype), shape(*psd.shape), splat_shape)
+        + (shape(*dest_order.shape, dtype=i32), shape(*seg_blocks.shape, dtype=i32))
+        + sum_shapes,
+        in_specs=[VMEM] + [hbm] * 7,
+        out_specs=(VMEM,) * 9,
         scratch_shapes=[
             pltpu.VMEM((slots, tiles, LANES), strain.dtype),
             pltpu.VMEM((tmpl_count, tiles, LANES), f32),
+            pltpu.VMEM(bin_edges.shape, i32),
             pltpu.SMEM(dest_order.shape, i32),
             pltpu.SMEM(seg_blocks.shape, i32),
-            pltpu.SMEM(bin_edges.shape, i32),
         ]
         + tables
-        + [mask, pltpu.SemaphoreType.DMA((7,))],
-    )(
-        other,
-        *[
-            pltpu.with_memory_space_constraint(x, pltpu.HBM)
-            for x in (tile_rows(strain), tile_rows(templates), psd, dft, dest_order, seg_blocks, bin_edges)
-        ],
-    )
-
-    part, *series = call(
+        + [mask, pltpu.SemaphoreType.DMA((9,))],
+    )(other, *in_hbm(tile_rows(strain), tile_rows(templates), psd, dft, dest_order, seg_blocks, bin_edges))
+
+    near, spectra = lax.optimization_barrier((near, spectra))
+    held = (spectra, dft_held, psd_held, splat)
+    out = call(
         next_kernel,
         "next_templates",
-        10**9,
-        out_shape=(shape(slots, LANES),) + sum_shapes,
-        in_specs=[VMEM] * 7 + [SMEM],
-        out_specs=(VMEM,) * 4,
-        scratch_shapes=[mask],
-    )(remote[0], spectra, dft_held, psd_held, *series, bin_edges)
-
-    left = bank_count - 2
+        1,
+        1,
+        out_shape=shape(slots, LANES),
+        in_specs=[VMEM] * 8,
+        out_specs=VMEM,
+        scratch_shapes=[pltpu.VMEM(dims, f32) for dims in sums] + [mask],
+    )(tile_rows(near), *held, *own_sums)
+
+    sources = [functools.partial(int, s) for s in range(3, bank_count)] + [lambda: 2 - core_here()]
+    remote = far + [tile_rows(swap(near, "seg", 1))]
+    old = [out]
+    for n, tmpl in enumerate(remote[:-1]):
+
+        def mid(*refs, n=n, count=len(old)):
+            ins, olds, (out_ref, *sums_out, mask_ref) = refs[:5], refs[5 : 5 + count], refs[5 + count :]
+            mid_kernel(sources[n], sources[n - 1] if n else None, *ins, olds, out_ref, sums_out, mask_ref)
+
+        old = call(
+            mid,
+            "mid_templates",
+            1,
+            1,
+            out_shape=(shape(slots, LANES),) + sum_shapes,
+            in_specs=[VMEM] * (5 + len(old)),
+            out_specs=(VMEM,) * 4,
+            scratch_shapes=[mask],
+        )(tmpl, *held, *old)
 
     def last(*refs):
-        ins, outs, held = refs[: left + 10], refs[left + 10 : left + 10 + chip_count], refs[left + 10 + chip_count :]
-        groups = [held[4 + 4 * s : 8 + 4 * s] for s in range(left)]
-        last_kernel(seg_count, ins[:left], *ins[left:], outs, *held[:4], groups)
+        ins, part_ref, sums_in, refs = refs[:7], refs[7], refs[8:11], refs[11:]
+        outs, refs = refs[:chip_count], refs[chip_count:]
+        last_kernel(seg_count, sources[-2:], *ins, sums_in, part_ref, outs, refs[:3], *refs[3:])
 
     parts = call(
         last,
         "last_templates",
-        2 * 10**9,
+        10**9,
         out_shape=(shape(BLK_DEV, LANES),) * chip_count,
-        in_specs=[VMEM] * (left + 7) + [SMEM] * 3,
+        in_specs=[VMEM] * 11,
         out_specs=(VMEM,) * chip_count,
-        scratch_shapes=[pltpu.VMEM((slots, LANES), f32), pltpu.VMEM((chip_count, BLK_DEV + 8, LANES), f32)]
+        scratch_shapes=[pltpu.VMEM(dims, f32) for dims in sums]
+        + [mask]
+        + [pltpu.VMEM((slots, LANES), f32), pltpu.VMEM((chip_count, BLK_DEV + 8, LANES), f32)]
         + tables
-        + ([pltpu.VMEM(dims, f32) for dims in sums] + [mask]) * left,
-    )(*remote[1:], spectra, dft_held, psd_held, part, *series, bin_edges, dest_order, seg_blocks)
+        + [pltpu.SMEM((4 * chip_count,), i32)],
+    )(remote[-1], *held, order_held, seg_held, *old)
 
     got = [swap(parts[m], "seg", 2 * m) for m in reversed(range(1, chip_count))] + [parts[0]]
     return call(

time: 23.6 us -> 22 us (0.932)
  Pallas kernels: 8.82 us -> 7.86 us
  waiting for transfers between devices: 4.84 us -> 4.24 us
    ppermute x7 -> x6, starting transfers between devices: 9.09 us -> 6.52 us  [swap(): lax.ppermute(x, axis, [(i, i ^ step) for i in range(lax.axis_size(axis))])]
    ppermute x0 -> x1, starting transfers between devices: none -> 2.56 us  [body(): near = lax.ppermute(templates, ('bank', 'seg'), near)]
    pallas_call x2 -> x3, Pallas kernels: 5.55 us -> 4.51 us  [the longest x1 1.73 us: body(): call(last, 'last_templates', 10 ** 9, out_shape=(shape(BLK_DEV, LANES),)...]
    ppermute x7 -> x6, waiting for transfers between devices: 4.84 us -> 4.24 us  [swap(): lax.ppermute(x, axis, [(i, i ^ step) for i in range(lax.axis_size(axis))])]
  transfers between devices with their start and end apart: 7 -> 7, of which waited for: 4 -> 3; matrix products, arithmetic and copies ran while one was open for 0% -> 0% of each run, Pallas kernels for 19% -> 25%
where the time goes in v3:
time: 22 us; the launch traced here: 21.9 us
  starting transfers between devices  9.08 us (41%)
  Pallas kernels  7.86 us (36%)
  waiting for transfers between devices  4.24 us (19%)
  between operations  0.68 us (3%)
    ppermute x6, starting transfers between devices, swap(): lax.ppermute(x, axis, [(i, i ^ step) for i in range(lax.axis_size(axis))])  6.52 us
    ppermute x6, waiting for transfers between devices, swap(): lax.ppermute(x, axis, [(i, i ^ step) for i in range(lax.axis_size(axis))])  4.24 us
    pallas_call x1, Pallas kernels, body(): call(functools.partial(own_kernel, seg_count), 'own_templates', 10 ** 9,...  2.67 us
    ppermute x1, starting transfers between devices, body(): near = lax.ppermute(templates, ('bank', 'seg'), near)  2.56 us
    pallas_call x1, Pallas kernels, body(): call(last, 'last_templates', 10 ** 9, out_shape=(shape(BLK_DEV, LANES),)...  1.73 us
    pallas_call x1, Pallas kernels, body(): call(next_kernel, 'next_templates', 1, 1, out_shape=shape(slots, LANES),...  1.67 us
    pallas_call x1, Pallas kernels, body(): call(mid, 'mid_templates', 1, 1, out_shape=(shape(slots, LANES),) + sum_s...  1.12 us
    pallas_call x1, Pallas kernels, body(): call(lambda *refs: add_kernel(refs[:chip_count], *refs[chip_count:]), 'ad...  0.67 us
  transfers between devices with their start and end apart: 7, of which 3 were waited for; matrix products, arithmetic and copies ran while one was open for 0% of the time, Pallas kernels for 25%

profile of v3, /device:TPU:0, one launch (start us, length us, event | category | flops | bytes accessed | tf_op | source)
XLA Modules:
  0.0 21.9 jit_solution(10789747170151474114)
XLA Ops:
  0.6 0.5 %collective-permute-start.1 = (bf16[32,2,4096]{2,1,0:T(2,128)(2,1)}, bf16[32,2,4096]{2,1,0:T(2,128)(2,1)S(1)}, u32[]{:S(2)}, u32[]{:S(2)}) collective-permute-start(bf16[32,2,4096]{2,1,0:T(2,128)(2,1)} %param.7), channel_id=1, source_target_pairs={{0,1},{1,0},{2,3},{3,2},{4,5},{5,4},{6,7},{7,6},{8,9},{9,8},{10,11... | collective-permute-start | bytes 1572872 | tf_op jit(solution)/shard_map/ppermute | solution.py:338
  1.1 2.6 %collective-permute-start = (f32[3,2,4096]{2,1,0:T(2,128)}, f32[3,2,4096]{2,1,0:T(2,128)S(1)}, u32[]{:S(2)}, u32[]{:S(2)}) collective-permute-start(f32[3,2,4096]{2,1,0:T(2,128)} %param.8), channel_id=1, source_target_pairs={{0,8},{1,17},{2,10},{3,19},{4,12},{5,21},{6,14},{7,23},{8,0},{9,25... | collective-permute-start | bytes 294920 | tf_op jit(solution)/shard_map/ppermute | solution.py:357
  3.7 1.5 %collective-permute-start.3 = (f32[3,2,4096]{2,1,0:T(2,128)}, f32[3,2,4096]{2,1,0:T(2,128)S(1)}, u32[]{:S(2)}, u32[]{:S(2)}) collective-permute-start(f32[3,2,4096]{2,1,0:T(2,128)} %param.8), channel_id=1, source_target_pairs={{0,24},{8,16},{16,8},{24,0},{1,25},{9,17},{17,9},{25,1},{2,26},{10... | collective-permute-start | bytes 294920 | tf_op jit(solution)/shard_map/ppermute | solution.py:338
  5.2 0.0 collective-permute-done.1
  5.2 2.7 %own_templates.1 = (f32[2112,128]{1,0:T(8,128)S(1)}, bf16[16,256,128]{2,1,0:T(8,128)(2,1)S(1)}, f32[32,128]{1,0:T(8,128)S(1)}, s32[9,12,128]{2,1,0:T(8,128)S(1)}...) custom-call(bf16[32,64,128]{2,1,0:T(8,128)(2,1)S(1)} %bitcast.38, ...), custom_call_target="tpu_custom_call" | custom-call | flops 1000000000 | bytes 4000000 | tf_op jit(solution)/shard_map/own_templates/pallas_call | solution.py:383
  7.9 0.0 collective-permute-done
  7.9 0.1 collective-permute-start.2
  8.0 1.7 %next_templates.1.refs_5_ = f32[32,128]{1,0:T(8,128)S(1)} custom-call(f32[3,64,128]{2,1,0:T(8,128)S(1)} %bitcast.36, f32[2112,128]{1,0:T(8,128)S(1)} %get-tuple-element.23.spectra_ref.refs_1_, bf16[16,256,128]{2,1,0:T(8,128)(2,1)S(1)} %get-tuple-element.24.dft_ref.refs_2_, f32[32,128]{1,0:T(8,128)S(1)} %get-tuple-element.25.psd_ref.refs_3_, ...), custom_call_target="tpu_custom_call" | custom-call | flops 1 | bytes 1 | tf_op jit(solution)/shard_map/next_templates/pallas_call | solution.py:405
  9.6 0.5 %collective-permute-done.3 = f32[3,2,4096]{2,1,0:T(2,128)S(1)} collective-permute-done((f32[3,2,4096]{2,1,0:T(2,128)}, f32[3,2,4096]{2,1,0:T(2,128)S(1)}, u32[]{:S(2)}, u32[]{:S(2)}) %collective-permute-start.3) | collective-permute-done | bytes 98336 | tf_op jit(solution)/shard_map/ppermute | solution.py:338
  10.1 1.1 %mid_templates.1 = (f32[32,128]{1,0:T(8,128)S(1)}, f32[3,23,64,128]{3,2,1,0:T(8,128)S(1)}, f32[3,9,8,128]{3,2,1,0:T(8,128)S(1)}, f32[3,9,8,128]{3,2,1,0:T(8,128)S(1)}) custom-call(f32[3,64,128]{2,1,0:T(8,128)S(1)} %bitcast.35, f32[2112,128]{1,0:T(8,128)S(1)} %get-tuple-element.23.spectra_ref.refs_1_, ...), custom_call_target="tpu_custom_call" | custom-call | flops 1 | bytes 1 | tf_op jit(solution)/shard_map/mid_templates/pallas_call | solution.py:425
  11.2 0.0 collective-permute-done.2
  11.2 1.7 %last_templates.1 = (f32[16,128]{1,0:T(8,128)S(1)}, f32[16,128]{1,0:T(8,128)S(1)}, f32[16,128]{1,0:T(8,128)S(1)}, f32[16,128]{1,0:T(8,128)S(1)}) custom-call(f32[3,64,128]{2,1,0:T(8,128)S(1)} %bitcast.37, f32[2112,128]{1,0:T(8,128)S(1)} %get-tuple-element.23.spectra_ref.refs_1_, bf16[16,256,128]{2,1,0:T(8,128)(2,1)S(1)} %get-tuple-element.24.dft_ref.refs_2_, ...), custom_call_target="tpu_custom_call" | custom-call | flops 1000000000 | bytes 4000000 | tf_op jit(solution)/shard_map/last_templates/pallas_call | solution.py:441
  13.0 3.7 %collective-permute-start.4 = (f32[16,128]{1,0:T(8,128)S(1)}, f32[16,128]{1,0:T(8,128)S(1)}, u32[]{:S(2)}, u32[]{:S(2)}) collective-permute-start(f32[16,128]{1,0:T(8,128)S(1)} %get-tuple-element.36), channel_id=1, source_target_pairs={{0,6},{1,7},{2,4},{3,5},{4,2},{5,3},{6,0},{7,1},{8,14},{9,15},{10,... | collective-permute-start | bytes 24584 | tf_op jit(solution)/shard_map/ppermute | solution.py:338
  16.6 0.0 collective-permute-start.5
  16.6 0.8 %collective-permute-start.6 = (f32[16,128]{1,0:T(8,128)S(1)}, f32[16,128]{1,0:T(8,128)S(1)}, u32[]{:S(2)}, u32[]{:S(2)}) collective-permute-start(f32[16,128]{1,0:T(8,128)S(1)} %get-tuple-element.38), channel_id=1, source_target_pairs={{0,2},{1,3},{2,0},{3,1},{4,6},{5,7},{6,4},{7,5},{8,10},{9,11},{10,... | collective-permute-start | bytes 24584 | tf_op jit(solution)/shard_map/ppermute | solution.py:338
  17.4 1.1 %collective-permute-done.4.refs_0_ = f32[16,128]{1,0:T(8,128)S(1)} collective-permute-done((f32[16,128]{1,0:T(8,128)S(1)}, f32[16,128]{1,0:T(8,128)S(1)}, u32[]{:S(2)}, u32[]{:S(2)}) %collective-permute-start.4) | collective-permute-done | bytes 8224 | tf_op jit(solution)/shard_map/ppermute | solution.py:338
  18.5 2.7 %collective-permute-done.5.refs_1_ = f32[16,128]{1,0:T(8,128)S(1)} collective-permute-done((f32[16,128]{1,0:T(8,128)S(1)}, f32[16,128]{1,0:T(8,128)S(1)}, u32[]{:S(2)}, u32[]{:S(2)}) %collective-permute-start.5) | collective-permute-done | bytes 8224 | tf_op jit(solution)/shard_map/ppermute | solution.py:338
  21.2 0.0 collective-permute-done.6.refs_2_
  21.2 0.7 %add_rows.1 = (f32[16,12]{1,0:T(8,128)}, f32[16,12]{1,0:T(8,128)}) custom-call(f32[16,128]{1,0:T(8,128)S(1)} %collective-permute-done.4.refs_0_, f32[16,128]{1,0:T(8,128)S(1)} %collective-permute-done.5.refs_1_, f32[16,128]{1,0:T(8,128)S(1)} %collective-permute-done.6.refs_2_, f32[16,128]{1,0:T(8,128)S(1)} %get-tuple-element.39.refs_3_), custom_call_target="tpu_custom_call" | custom-call | flops 100000 | bytes 4000000 | tf_op jit(solution)/shard_map/add_rows/pallas_call | solution.py:456
Async XLA Ops:
  0.6 4.6 %collective-permute-start.1 = (bf16[32,2,4096]{2,1,0:T(2,128)(2,1)}, bf16[32,2,4096]{2,1,0:T(2,128)(2,1)S(1)}, u32[]{:S(2)}, u32[]{:S(2)}) collective-permute-start(bf16[32,2,4096]{2,1,0:T(2,128)(2,1)} %param.7), channel_id=1, source_target_pairs={{0,1},{1,0},{2,3},{3,2},{4,5},{5,4},{6,7},{7,6},{8,9},{9,8},{10,11... | collective-permute-start | bytes 1572872 | tf_op jit(solution)/shard_map/ppermute | solution.py:338
  1.1 6.7 %collective-permute-start = (f32[3,2,4096]{2,1,0:T(2,128)}, f32[3,2,4096]{2,1,0:T(2,128)S(1)}, u32[]{:S(2)}, u32[]{:S(2)}) collective-permute-start(f32[3,2,4096]{2,1,0:T(2,128)} %param.8), channel_id=1, source_target_pairs={{0,8},{1,17},{2,10},{3,19},{4,12},{5,21},{6,14},{7,23},{8,0},{9,25... | collective-permute-start | bytes 294920 | tf_op jit(solution)/shard_map/ppermute | solution.py:357
  3.7 6.4 %collective-permute-start.3 = (f32[3,2,4096]{2,1,0:T(2,128)}, f32[3,2,4096]{2,1,0:T(2,128)S(1)}, u32[]{:S(2)}, u32[]{:S(2)}) collective-permute-start(f32[3,2,4096]{2,1,0:T(2,128)} %param.8), channel_id=1, source_target_pairs={{0,24},{8,16},{16,8},{24,0},{1,25},{9,17},{17,9},{25,1},{2,26},{10... | collective-permute-start | bytes 294920 | tf_op jit(solution)/shard_map/ppermute | solution.py:338
  7.9 3.3 %collective-permute-start.2 = (f32[3,2,4096]{2,1,0:T(2,128)S(1)}, f32[3,2,4096]{2,1,0:T(2,128)S(1)}, u32[]{:S(2)}, u32[]{:S(2)}) collective-permute-start(f32[3,2,4096]{2,1,0:T(2,128)S(1)} %collective-permute-done), channel_id=1, source_target_pairs={{0,1},{1,0},{2,3},{3,2},{4,5},{5,4},{6,7},{7,6},{8,9},{9,8},{10,11... | collective-permute-start | bytes 294920 | tf_op jit(solution)/shard_map/ppermute | solution.py:338
  13.0 5.5 %collective-permute-start.4 = (f32[16,128]{1,0:T(8,128)S(1)}, f32[16,128]{1,0:T(8,128)S(1)}, u32[]{:S(2)}, u32[]{:S(2)}) collective-permute-start(f32[16,128]{1,0:T(8,128)S(1)} %get-tuple-element.36), channel_id=1, source_target_pairs={{0,6},{1,7},{2,4},{3,5},{4,2},{5,3},{6,0},{7,1},{8,14},{9,15},{10,... | collective-permute-start | bytes 24584 | tf_op jit(solution)/shard_map/ppermute | solution.py:338
  16.6 4.5 %collective-permute-start.5 = (f32[16,128]{1,0:T(8,128)S(1)}, f32[16,128]{1,0:T(8,128)S(1)}, u32[]{:S(2)}, u32[]{:S(2)}) collective-permute-start(f32[16,128]{1,0:T(8,128)S(1)} %get-tuple-element.37), channel_id=1, source_target_pairs={{0,4},{1,5},{2,6},{3,7},{4,0},{5,1},{6,2},{7,3},{8,12},{9,13},{10,... | collective-permute-start | bytes 24584 | tf_op jit(solution)/shard_map/ppermute | solution.py:338
  16.6 4.5 %collective-permute-start.6 = (f32[16,128]{1,0:T(8,128)S(1)}, f32[16,128]{1,0:T(8,128)S(1)}, u32[]{:S(2)}, u32[]{:S(2)}) collective-permute-start(f32[16,128]{1,0:T(8,128)S(1)} %get-tuple-element.38), channel_id=1, source_target_pairs={{0,2},{1,3},{2,0},{3,1},{4,6},{5,7},{6,4},{7,5},{8,10},{9,11},{10,... | collective-permute-start | bytes 24584 | tf_op jit(solution)/shard_map/ppermute | solution.py:338

commit v4 on v3

--- a/solution.py
+++ b/solution.py
@@ -36,17 +36,17 @@
     return lax.axis_index("seg") % 2
 
 
-def seg_starts(seg_ref, start_ref, seg_count, in_vmem=False):
+def seg_starts(seg_ref, start_ref, seg_count):
     total = jnp.int32(0)
     for s in range(seg_count):
         start_ref[s] = total
-        total = total + seg_ref[:, s : s + 1][0, 0] if in_vmem else total + seg_ref[0, s]
+        total = total + seg_ref[:, s : s + 1][0, 0]
     start_ref[seg_count] = total
 
 
-def inverse_order(order_ref, residue_ref, seg_count, in_vmem=False):
+def inverse_order(order_ref, residue_ref, seg_count):
     for r in range(seg_count):
-        residue_ref[order_ref[:, r : r + 1][0, 0] if in_vmem else order_ref[0, r]] = jnp.int32(r)
+        residue_ref[order_ref[:, r : r + 1][0, 0]] = jnp.int32(r)
 
 
 def first_slot(start_ref, residue_ref, seg_count, m, side):
@@ -235,57 +235,37 @@
     return [functools.partial(test_values, group, t, out_ref) for t in range(group.count)]
 
 
+def begin_kernel(out_ref):
+    out_ref[...] = jnp.zeros_like(out_ref)
+
+
 def own_kernel(
     seg_count,
-    other_ref, own_any, tmpl_any, psd_any, dft_any, order_any, seg_any, edge_any,
-    spectra_ref, dft_ref, psd_ref, splat_ref, order_lanes_ref, seg_lanes_ref, series_ref, inv_ref, frac_ref,
-    own_ref, tmpl_ref, lanes_ref, order_ref, seg_ref, start_ref, residue_ref, mask_ref, sems,
+    _, other_ref, own_ref, tmpl_ref, psd_ref, dft_ref, order_ref, seg_ref, edge_ref,
+    spectra_ref, splat_ref, out_ref,
+    start_ref, residue_ref, mask_ref, series_ref, inv_ref, frac_ref,
 ):
-    pairs = [
-        (order_any, order_ref), (seg_any, seg_ref), (psd_any, psd_ref), (edge_any, lanes_ref), (tmpl_any, tmpl_ref),
-        (own_any, own_ref), (dft_any, dft_ref), (order_any, order_lanes_ref), (seg_any, seg_lanes_ref),
-    ]
-    copies = [pltpu.make_async_copy(src, dst, sems.at[i]) for i, (src, dst) in enumerate(pairs)]
-    for copy in copies:
-        copy.start()
-    for copy in copies[:4]:
-        copy.wait()
     for p in range(splat_ref.shape[0]):
-        splat_ref[p] = jnp.broadcast_to(lanes_ref[:, p : p + 1], splat_ref.shape[1:])
+        splat_ref[p] = jnp.broadcast_to(edge_ref[:, p : p + 1], splat_ref.shape[1:])
     seg_starts(seg_ref, start_ref, seg_count)
     inverse_order(order_ref, residue_ref, seg_count)
+    arrange_strain(0, own_ref, psd_ref, spectra_ref, start_ref, residue_ref, seg_count)
     arrange_strain(1, other_ref, psd_ref, spectra_ref, start_ref, residue_ref, seg_count)
-    copies[4].wait()
-    copies[5].wait()
-    arrange_strain(0, own_ref, psd_ref, spectra_ref, start_ref, residue_ref, seg_count)
-    for copy in copies[6:]:
-        copy.wait()
     first = lax.axis_index("bank") * tmpl_ref.shape[0]
     group = Group(tmpl_ref, first, splat_ref, series_ref, inv_ref, frac_ref, mask_ref)
     add_up(group, spectra_ref, psd_ref, dft_ref)
-
-
-def next_kernel(
-    tmpl_ref, spectra_ref, dft_ref, psd_ref, splat_ref, old_series_ref, old_inv_ref, old_frac_ref,
-    out_ref, series_ref, inv_ref, frac_ref, mask_ref,
-):
-    bank, count = lax.axis_index("bank"), tmpl_ref.shape[0]
     out_ref[...] = jnp.zeros_like(out_ref)
-    old = Group(None, bank * count, splat_ref, old_series_ref, old_inv_ref, old_frac_ref)
-    group = Group(tmpl_ref, (bank ^ (1 + core_here())) * count, splat_ref, series_ref, inv_ref, frac_ref, mask_ref)
-    beside = {4 * n + 3: [write] for n, write in enumerate(values_of(old, out_ref))}
-    add_up(group, spectra_ref, psd_ref, dft_ref, beside)
     for write in values_of(group, out_ref):
         write()
 
 
-def mid_kernel(source, old_source, tmpl_ref, spectra_ref, dft_ref, psd_ref, splat_ref, old, out_ref, sums, mask_ref):
+def mid_kernel(source, old_source, tmpl_ref, spectra_ref, dft_ref, psd_ref, splat_ref, old, sums, out_ref, mask_ref):
     bank, count = lax.axis_index("bank"), tmpl_ref.shape[0]
     group = Group(tmpl_ref, (bank ^ source()) * count, splat_ref, *sums, mask_ref)
-    out_ref[...] = old[0][...]
     beside = {}
-    if old_source is not None:
-        writes = values_of(Group(None, (bank ^ old_source()) * count, splat_ref, *old[1:]), out_ref)
+    if old:
+        out_ref[...] = old[3][...]
+        writes = values_of(Group(None, (bank ^ old_source()) * count, splat_ref, *old[:3]), out_ref)
         beside = {4 * n + 3: [write] for n, write in enumerate(writes)}
     add_up(group, spectra_ref, psd_ref, dft_ref, beside)
 
@@ -299,8 +279,8 @@
     core, chip = seg_here % 2, seg_here // 2
 
     def place():
-        seg_starts(seg_ref, start_ref, seg_count, in_vmem=True)
-        inverse_order(order_ref, residue_ref, seg_count, in_vmem=True)
+        seg_starts(seg_ref, start_ref, seg_count)
+        inverse_order(order_ref, residue_ref, seg_count)
         for m in range(seg_count // 2):
             for source in range(2):
                 start, first = first_slot(start_ref, residue_ref, seg_count, m, core ^ source)
@@ -351,11 +331,6 @@
     dft = jnp.asarray(dft_chunks(freq_count))
     psd = tile_rows(inv_psd)
 
-    other = tile_rows(swap(strain, "seg", 1))
-    far = [tile_rows(swap(templates, "bank", s)) for s in range(3, bank_count)]
-    near = [(b * seg_count + s, (b ^ (1 + s % 2)) * seg_count + s) for b in range(bank_count) for s in range(seg_count)]
-    near = lax.ppermute(templates, ("bank", "seg"), near)
-
     def shape(*dims, dtype=f32):
         return jax.ShapeDtypeStruct(dims, dtype)
 
@@ -374,67 +349,60 @@
             **kwargs,
         )
 
-    hbm = pl.BlockSpec(memory_space=pltpu.HBM)
-
-    def in_hbm(*arrays):
-        return [pltpu.with_memory_space_constraint(x, pltpu.HBM) for x in arrays]
+    begin = call(begin_kernel, "begin", 2 * 10**9, 1, out_shape=shape(8, LANES), out_specs=VMEM)()
+    other = tile_rows(swap(strain, "seg", 1))
+    far = [tile_rows(swap(templates, "bank", s)) for s in range(3, bank_count)]
+    near = [(b * seg_count + s, (b ^ (1 + s % 2)) * seg_count + s) for b in range(bank_count) for s in range(seg_count)]
+    near = lax.ppermute(templates, ("bank", "seg"), near)
 
     splat_shape = shape(bins + 1, tmpl_total, LANES, dtype=i32)
-    spectra, dft_held, psd_held, splat, order_held, seg_held, *own_sums = call(
+    spectra, splat, out = call(
         functools.partial(own_kernel, seg_count),
         "own_templates",
         10**9,
-        out_shape=(shape((slots + 1) * tiles, LANES), shape(*dft.shape, dtype=dft.dtype), shape(*psd.shape), splat_shape)
-        + (shape(*dest_order.shape, dtype=i32), shape(*seg_blocks.shape, dtype=i32))
-        + sum_shapes,
-        in_specs=[VMEM] + [hbm] * 7,
-        out_specs=(VMEM,) * 9,
-        scratch_shapes=[
-            pltpu.VMEM((slots, tiles, LANES), strain.dtype),
-            pltpu.VMEM((tmpl_count, tiles, LANES), f32),
-            pltpu.VMEM(bin_edges.shape, i32),
-            pltpu.SMEM(dest_order.shape, i32),
-            pltpu.SMEM(seg_blocks.shape, i32),
-        ]
-        + tables
-        + [mask, pltpu.SemaphoreType.DMA((9,))],
-    )(other, *in_hbm(tile_rows(strain), tile_rows(templates), psd, dft, dest_order, seg_blocks, bin_edges))
+        out_shape=(shape((slots + 1) * tiles, LANES), splat_shape, shape(slots, LANES)),
+        in_specs=[VMEM] * 9,
+        out_specs=(VMEM,) * 3,
+        scratch_shapes=tables + [mask] + [pltpu.VMEM(dims, f32) for dims in sums],
+    )(begin, other, tile_rows(strain), tile_rows(templates), psd, dft, dest_order, seg_blocks, bin_edges)
 
     near, spectra = lax.optimization_barrier((near, spectra))
-    held = (spectra, dft_held, psd_held, splat)
-    out = call(
-        next_kernel,
-        "next_templates",
-        1,
-        1,
-        out_shape=shape(slots, LANES),
-        in_specs=[VMEM] * 8,
-        out_specs=VMEM,
-        scratch_shapes=[pltpu.VMEM(dims, f32) for dims in sums] + [mask],
-    )(tile_rows(near), *held, *own_sums)
-
-    sources = [functools.partial(int, s) for s in range(3, bank_count)] + [lambda: 2 - core_here()]
-    remote = far + [tile_rows(swap(near, "seg", 1))]
-    old = [out]
-    for n, tmpl in enumerate(remote[:-1]):
-
-        def mid(*refs, n=n, count=len(old)):
-            ins, olds, (out_ref, *sums_out, mask_ref) = refs[:5], refs[5 : 5 + count], refs[5 + count :]
-            mid_kernel(sources[n], sources[n - 1] if n else None, *ins, olds, out_ref, sums_out, mask_ref)
-
-        old = call(
+    held = (spectra, dft, psd, splat)
+    sources = [lambda: 1 + core_here(), lambda: 2 - core_here()]
+    sources += [functools.partial(int, s) for s in range(3, bank_count)]
+    remote = [[tile_rows(near)], [tile_rows(swap(part, "seg", 1)) for part in (near[:2], near[2:])]]
+    remote += [[x] for x in far]
+    old = []
+    for n, parts in enumerate(remote[:-1]):
+
+        def mid(*refs, n=n, count=len(old), split=len(parts)):
+            parts, refs = refs[:split], refs[split:]
+            ins, olds, (*outs, mask_ref, tmpl_ref) = refs[:4], refs[4 : 4 + count], refs[4 + count :]
+            if split > 1:
+                row = 0
+                for ref in parts:
+                    tmpl_ref[row : row + ref.shape[0]] = ref[...]
+                    row += ref.shape[0]
+            else:
+                (tmpl_ref,) = parts
+            out_ref = outs[3] if olds else None
+            mid_kernel(sources[n], sources[n - 1], tmpl_ref, *ins, olds, outs[:3], out_ref, mask_ref)
+
+        outs = sum_shapes + ((shape(slots, LANES),) if old else ())
+        new = call(
             mid,
-            "mid_templates",
+            "mid_templates" if old else "next_templates",
             1,
             1,
-            out_shape=(shape(slots, LANES),) + sum_shapes,
-            in_specs=[VMEM] * (5 + len(old)),
-            out_specs=(VMEM,) * 4,
-            scratch_shapes=[mask],
-        )(tmpl, *held, *old)
+            out_shape=outs,
+            in_specs=[VMEM] * (4 + len(parts) + len(old)),
+            out_specs=(VMEM,) * len(outs),
+            scratch_shapes=[mask, pltpu.VMEM((tmpl_count, tiles, LANES), f32)],
+        )(*parts, *held, *old)
+        old = list(new) if old else [*new, out]
 
     def last(*refs):
-        ins, part_ref, sums_in, refs = refs[:7], refs[7], refs[8:11], refs[11:]
+        ins, sums_in, part_ref, refs = refs[:7], refs[7:10], refs[10], refs[11:]
         outs, refs = refs[:chip_count], refs[chip_count:]
         last_kernel(seg_count, sources[-2:], *ins, sums_in, part_ref, outs, refs[:3], *refs[3:])
 
@@ -450,7 +418,7 @@
         + [pltpu.VMEM((slots, LANES), f32), pltpu.VMEM((chip_count, BLK_DEV + 8, LANES), f32)]
         + tables
         + [pltpu.SMEM((4 * chip_count,), i32)],
-    )(remote[-1], *held, order_held, seg_held, *old)
+    )(*remote[-1], *held, dest_order, seg_blocks, *old)
 
     got = [swap(parts[m], "seg", 2 * m) for m in reversed(range(1, chip_count))] + [parts[0]]
     return call(

time: 22 us -> 21.4 us (0.973)
  Pallas kernels: 7.86 us -> 6.64 us
  starting transfers between devices: 9.08 us -> 9.9 us
  waiting for transfers between devices: 4.24 us -> 3.92 us
    pallas_call x1, Pallas kernels: 2.67 us -> 1.68 us  [body(): call(functools.partial(own_kernel, seg_count), 'own_templates', 10 ** 9,...]
    ppermute x6 -> x7, starting transfers between devices: 6.52 us -> 7.34 us  [swap(): lax.ppermute(x, axis, [(i, i ^ step) for i in range(lax.axis_size(axis))])]
    ppermute x6 -> x7, waiting for transfers between devices: 4.24 us -> 3.92 us  [swap(): lax.ppermute(x, axis, [(i, i ^ step) for i in range(lax.axis_size(axis))])]
    pallas_call x2 -> x3, Pallas kernels: 2.79 us -> 2.53 us  [the longest x2 2.53 us: body(): call(mid, 'mid_templates' if old else 'next_templates', 1, 1, out_shape=o...]
  transfers between devices with their start and end apart: 7 -> 8, of which waited for: 3 -> 2; matrix products, arithmetic and copies ran while one was open for 0% -> 0% of each run, Pallas kernels for 25% -> 20%
where the time goes in v4:
time: 21.4 us; the launch traced here: 21.3 us
  starting transfers between devices  9.9 us (46%)
  Pallas kernels  6.64 us (31%)
  waiting for transfers between devices  3.92 us (18%)
  between operations  0.8 us (4%)
    ppermute x7, starting transfers between devices, swap(): lax.ppermute(x, axis, [(i, i ^ step) for i in range(lax.axis_size(axis))])  7.34 us
    ppermute x7, waiting for transfers between devices, swap(): lax.ppermute(x, axis, [(i, i ^ step) for i in range(lax.axis_size(axis))])  3.92 us
    ppermute x1, starting transfers between devices, body(): near = lax.ppermute(templates, ('bank', 'seg'), near)  2.56 us
    pallas_call x2, Pallas kernels, body(): call(mid, 'mid_templates' if old else 'next_templates', 1, 1, out_shape=o...  2.53 us
    pallas_call x1, Pallas kernels, body(): call(last, 'last_templates', 10 ** 9, out_shape=(shape(BLK_DEV, LANES),)...  1.75 us
    pallas_call x1, Pallas kernels, body(): call(functools.partial(own_kernel, seg_count), 'own_templates', 10 ** 9,...  1.68 us
    pallas_call x1, Pallas kernels, body(): call(lambda *refs: add_kernel(refs[:chip_count], *refs[chip_count:]), 'ad...  0.67 us
  transfers between devices with their start and end apart: 8, of which 2 were waited for; matrix products, arithmetic and copies ran while one was open for 0% of the time, Pallas kernels for 20%

profile of v4, /device:TPU:0, one launch (start us, length us, event | category | flops | bytes accessed | tf_op | source)
XLA Modules:
  0.0 21.3 jit_solution(1261078873334991958)
XLA Ops:
  0.6 0.0 copy-start
  0.6 0.0 copy-start.4
  0.7 0.0 copy-start.5
  0.7 0.0 copy-start.1
  0.7 0.0 copy-start.3
  0.7 0.0 copy-start.2
  0.7 0.0 copy-start.6
  0.7 0.5 %collective-permute-start.2 = (bf16[32,2,4096]{2,1,0:T(2,128)(2,1)}, bf16[32,2,4096]{2,1,0:T(2,128)(2,1)S(1)}, u32[]{:S(2)}, u32[]{:S(2)}) collective-permute-start(bf16[32,2,4096]{2,1,0:T(2,128)(2,1)} %param.7), channel_id=1, source_target_pairs={{0,1},{1,0},{2,3},{3,2},{4,5},{5,4},{6,7},{7,6},{8,9},{9,8},{10,11... | collective-permute-start | bytes 1572872 | tf_op jit(solution)/shard_map/ppermute | solution.py:318
  1.2 2.6 %collective-permute-start.1 = (f32[3,2,4096]{2,1,0:T(2,128)}, f32[3,2,4096]{2,1,0:T(2,128)S(1)}, u32[]{:S(2)}, u32[]{:S(2)}) collective-permute-start(f32[3,2,4096]{2,1,0:T(2,128)} %param.8), channel_id=1, source_target_pairs={{0,8},{1,17},{2,10},{3,19},{4,12},{5,21},{6,14},{7,23},{8,0},{9,25... | collective-permute-start | bytes 294920 | tf_op jit(solution)/shard_map/ppermute | solution.py:356
  3.8 1.5 %collective-permute-start = (f32[3,2,4096]{2,1,0:T(2,128)}, f32[3,2,4096]{2,1,0:T(2,128)S(1)}, u32[]{:S(2)}, u32[]{:S(2)}) collective-permute-start(f32[3,2,4096]{2,1,0:T(2,128)} %param.8), channel_id=1, source_target_pairs={{0,24},{8,16},{16,8},{24,0},{1,25},{9,17},{17,9},{25,1},{2,26},{10... | collective-permute-start | bytes 294920 | tf_op jit(solution)/shard_map/ppermute | solution.py:318
  5.3 0.0 collective-permute-done.2
  5.3 0.0 copy-done
  5.3 0.0 copy-done.4
  5.3 0.0 copy-done.5
  5.3 0.0 copy-done.1
  5.3 0.0 copy-done.3
  5.3 0.0 copy-done.2
  5.3 0.0 copy-done.6
  5.3 1.7 %own_templates.1 = (f32[2112,128]{1,0:T(8,128)S(1)}, s32[9,12,128]{2,1,0:T(8,128)S(1)}, f32[32,128]{1,0:T(8,128)S(1)}) custom-call(f32[8,128]{1,0:T(8,128)S(1)} %begin.1._, bf16[32,64,128]{2,1,0:T(8,128)(2,1)S(1)} %bitcast.49, bf16[32,64,128]{2,1,0:T(8,128)(2,1)S(1)} %bitcast.48, f32[3,64,128]{2,1,0:T(8,128)S(1)} %bitcast.50, f32[32,128]{1,0:T(8,128)S(1)} %bitcast.41, ...), custom_call_target="tpu_custom_call" | custom-call | flops 1000000000 | bytes 4000000 | tf_op jit(solution)/shard_map/own_templates/pallas_call | solution.py:359
  7.0 0.0 collective-permute-done.1
  7.0 0.1 collective-permute-start.3
  7.1 0.5 %collective-permute-start.4 = (f32[1,2,4096]{2,1,0:T(2,128)S(1)}, f32[1,2,4096]{2,1,0:T(2,128)S(1)}, u32[]{:S(2)}, u32[]{:S(2)}) collective-permute-start(f32[1,2,4096]{2,1,0:T(2,128)S(1)} %slice.7), channel_id=1, source_target_pairs={{0,1},{1,0},{2,3},{3,2},{4,5},{5,4},{6,7},{7,6},{8,9},{9,8},{10,11... | collective-permute-start | bytes 98312 | tf_op jit(solution)/shard_map/ppermute | solution.py:318
  7.6 1.1 %next_templates.1 = (f32[3,23,64,128]{3,2,1,0:T(8,128)S(1)}, f32[3,9,8,128]{3,2,1,0:T(8,128)S(1)}, f32[3,9,8,128]{3,2,1,0:T(8,128)S(1)}) custom-call(f32[3,64,128]{2,1,0:T(8,128)S(1)} %bitcast.40, f32[2112,128]{1,0:T(8,128)S(1)} %get-tuple-element.19.refs_1_.refs_2_, bf16[16,256,128]{2,1,0:T(8,128)(2,1)S(1)} %copy-done, f32[32,128]{1,0:T(8,128)S(1)} %bitcast.42, ...), custom_call_target="tpu_custom_call" | custom-call | flops 1 | bytes 1 | tf_op jit(solution)/shard_map/next_templates/pallas_call | solution.py:392
  8.8 0.0 collective-permute-done.4
  8.8 0.0 collective-permute-done.3
  8.8 1.4 %mid_templates.1 = (f32[3,23,64,128]{3,2,1,0:T(8,128)S(1)}, f32[3,9,8,128]{3,2,1,0:T(8,128)S(1)}, f32[3,9,8,128]{3,2,1,0:T(8,128)S(1)}, f32[32,128]{1,0:T(8,128)S(1)}) custom-call(f32[2,64,128]{2,1,0:T(8,128)S(1)} %bitcast.46, f32[1,64,128]{2,1,0:T(8,128)S(1)} %bitcast.47, f32[2112,128]{1,0:T(8,128)S(1)} %get-tuple-element.19.refs_1_.refs_2_, ...), custom_call_target="tpu_custom_call" | custom-call | flops 1 | bytes 1 | tf_op jit(solution)/shard_map/mid_templates/pallas_call | solution.py:392
  10.2 0.0 collective-permute-done
  10.2 1.7 %last_templates.1 = (f32[16,128]{1,0:T(8,128)S(1)}, f32[16,128]{1,0:T(8,128)S(1)}, f32[16,128]{1,0:T(8,128)S(1)}, f32[16,128]{1,0:T(8,128)S(1)}) custom-call(f32[3,64,128]{2,1,0:T(8,128)S(1)} %bitcast.45, f32[2112,128]{1,0:T(8,128)S(1)} %get-tuple-element.19.refs_1_.refs_2_, bf16[16,256,128]{2,1,0:T(8,128)(2,1)S(1)} %copy-done, f32[32,128]{1,0:T(8,128)S(1)} %bitcast.44, ...), custom_call_target="tpu_custom_call" | custom-call | flops 1000000000 | bytes 4000000 | tf_op jit(solution)/shard_map/last_templates/pallas_call | solution.py:409
  11.9 4.1 %collective-permute-start.5 = (f32[16,128]{1,0:T(8,128)S(1)}, f32[16,128]{1,0:T(8,128)S(1)}, u32[]{:S(2)}, u32[]{:S(2)}) collective-permute-start(f32[16,128]{1,0:T(8,128)S(1)} %get-tuple-element.30), channel_id=1, source_target_pairs={{0,6},{1,7},{2,4},{3,5},{4,2},{5,3},{6,0},{7,1},{8,14},{9,15},{10,... | collective-permute-start | bytes 24584 | tf_op jit(solution)/shard_map/ppermute | solution.py:318
  16.1 0.0 collective-permute-start.6
  16.1 0.6 %collective-permute-start.7 = (f32[16,128]{1,0:T(8,128)S(1)}, f32[16,128]{1,0:T(8,128)S(1)}, u32[]{:S(2)}, u32[]{:S(2)}) collective-permute-start(f32[16,128]{1,0:T(8,128)S(1)} %get-tuple-element.32), channel_id=1, source_target_pairs={{0,2},{1,3},{2,0},{3,1},{4,6},{5,7},{6,4},{7,5},{8,10},{9,11},{10,... | collective-permute-start | bytes 24584 | tf_op jit(solution)/shard_map/ppermute | solution.py:318
  16.7 1.0 %collective-permute-done.5.refs_0_ = f32[16,128]{1,0:T(8,128)S(1)} collective-permute-done((f32[16,128]{1,0:T(8,128)S(1)}, f32[16,128]{1,0:T(8,128)S(1)}, u32[]{:S(2)}, u32[]{:S(2)}) %collective-permute-start.5) | collective-permute-done | bytes 8224 | tf_op jit(solution)/shard_map/ppermute | solution.py:318
  17.7 2.9 %collective-permute-done.6.refs_1_ = f32[16,128]{1,0:T(8,128)S(1)} collective-permute-done((f32[16,128]{1,0:T(8,128)S(1)}, f32[16,128]{1,0:T(8,128)S(1)}, u32[]{:S(2)}, u32[]{:S(2)}) %collective-permute-start.6) | collective-permute-done | bytes 8224 | tf_op jit(solution)/shard_map/ppermute | solution.py:318
  20.6 0.0 collective-permute-done.7.refs_2_
  20.6 0.7 %add_rows.1 = (f32[16,12]{1,0:T(8,128)}, f32[16,12]{1,0:T(8,128)}) custom-call(f32[16,128]{1,0:T(8,128)S(1)} %collective-permute-done.5.refs_0_, f32[16,128]{1,0:T(8,128)S(1)} %collective-permute-done.6.refs_1_, f32[16,128]{1,0:T(8,128)S(1)} %collective-permute-done.7.refs_2_, f32[16,128]{1,0:T(8,128)S(1)} %get-tuple-element.33.refs_3_), custom_call_target="tpu_custom_call" | custom-call | flops 100000 | bytes 4000000 | tf_op jit(solution)/shard_map/add_rows/pallas_call | solution.py:424
  (3 shorter events, 0.0 us)
Async XLA Ops:
  0.6 4.7 %copy-start = (bf16[16,256,128]{2,1,0:T(8,128)(2,1)S(1)}, bf16[16,256,128]{2,1,0:T(8,128)(2,1)}, u32[]{:S(2)}) copy-start(bf16[16,256,128]{2,1,0:T(8,128)(2,1)} %constant.2.clone.dft_ref.refs_2_.refs_3_) | copy-start | bytes 3145732
  0.6 4.6 %copy-start.4 = (bf16[32,2,4096]{2,1,0:T(2,128)(2,1)S(1)}, bf16[32,2,4096]{2,1,0:T(2,128)(2,1)}, u32[]{:S(2)}) copy-start(bf16[32,2,4096]{2,1,0:T(2,128)(2,1)} %param.7) | copy-start | bytes 1572868
  0.7 4.6 %copy-start.5 = (f32[3,2,4096]{2,1,0:T(2,128)S(1)}, f32[3,2,4096]{2,1,0:T(2,128)}, u32[]{:S(2)}) copy-start(f32[3,2,4096]{2,1,0:T(2,128)} %param.8) | copy-start | bytes 294916
  0.7 4.6 %copy-start.1 = (f32[2,2048]{1,0:T(2,128)S(1)}, f32[2,2048]{1,0:T(2,128)}, u32[]{:S(2)}) copy-start(f32[2,2048]{1,0:T(2,128)} %param.9) | copy-start | bytes 49156
  0.7 4.6 %copy-start.3 = (s32[1,8]{1,0:T(1,128)S(1)}, s32[1,8]{1,0:T(1,128)}, u32[]{:S(2)}) copy-start(s32[1,8]{1,0:T(1,128)} %refs_6_.1) | copy-start | bytes 100
  0.7 4.6 %copy-start.2 = (s32[1,8]{1,0:T(1,128)S(1)}, s32[1,8]{1,0:T(1,128)}, u32[]{:S(2)}) copy-start(s32[1,8]{1,0:T(1,128)} %refs_5_.1) | copy-start | bytes 100
  0.7 4.6 %copy-start.6 = (s32[12,9]{1,0:T(8,128)S(1)}, s32[12,9]{1,0:T(8,128)}, u32[]{:S(2)}) copy-start(s32[12,9]{1,0:T(8,128)} %edge_ref.1) | copy-start | bytes 1300
  0.7 4.6 %collective-permute-start.2 = (bf16[32,2,4096]{2,1,0:T(2,128)(2,1)}, bf16[32,2,4096]{2,1,0:T(2,128)(2,1)S(1)}, u32[]{:S(2)}, u32[]{:S(2)}) collective-permute-start(bf16[32,2,4096]{2,1,0:T(2,128)(2,1)} %param.7), channel_id=1, source_target_pairs={{0,1},{1,0},{2,3},{3,2},{4,5},{5,4},{6,7},{7,6},{8,9},{9,8},{10,11... | collective-permute-start | bytes 1572872 | tf_op jit(solution)/shard_map/ppermute | solution.py:318
  1.2 5.8 %collective-permute-start.1 = (f32[3,2,4096]{2,1,0:T(2,128)}, f32[3,2,4096]{2,1,0:T(2,128)S(1)}, u32[]{:S(2)}, u32[]{:S(2)}) collective-permute-start(f32[3,2,4096]{2,1,0:T(2,128)} %param.8), channel_id=1, source_target_pairs={{0,8},{1,17},{2,10},{3,19},{4,12},{5,21},{6,14},{7,23},{8,0},{9,25... | collective-permute-start | bytes 294920 | tf_op jit(solution)/shard_map/ppermute | solution.py:356
  3.8 6.4 %collective-permute-start = (f32[3,2,4096]{2,1,0:T(2,128)}, f32[3,2,4096]{2,1,0:T(2,128)S(1)}, u32[]{:S(2)}, u32[]{:S(2)}) collective-permute-start(f32[3,2,4096]{2,1,0:T(2,128)} %param.8), channel_id=1, source_target_pairs={{0,24},{8,16},{16,8},{24,0},{1,25},{9,17},{17,9},{25,1},{2,26},{10... | collective-permute-start | bytes 294920 | tf_op jit(solution)/shard_map/ppermute | solution.py:318
  7.0 1.7 %collective-permute-start.3 = (f32[2,2,4096]{2,1,0:T(2,128)S(1)}, f32[2,2,4096]{2,1,0:T(2,128)S(1)}, u32[]{:S(2)}, u32[]{:S(2)}) collective-permute-start(f32[2,2,4096]{2,1,0:T(2,128)S(1)} %slice.6), channel_id=1, source_target_pairs={{0,1},{1,0},{2,3},{3,2},{4,5},{5,4},{6,7},{7,6},{8,9},{9,8},{10,11... | collective-permute-start | bytes 196616 | tf_op jit(solution)/shard_map/ppermute | solution.py:318
  7.1 1.6 %collective-permute-start.4 = (f32[1,2,4096]{2,1,0:T(2,128)S(1)}, f32[1,2,4096]{2,1,0:T(2,128)S(1)}, u32[]{:S(2)}, u32[]{:S(2)}) collective-permute-start(f32[1,2,4096]{2,1,0:T(2,128)S(1)} %slice.7), channel_id=1, source_target_pairs={{0,1},{1,0},{2,3},{3,2},{4,5},{5,4},{6,7},{7,6},{8,9},{9,8},{10,11... | collective-permute-start | bytes 98312 | tf_op jit(solution)/shard_map/ppermute | solution.py:318
  11.9 5.8 %collective-permute-start.5 = (f32[16,128]{1,0:T(8,128)S(1)}, f32[16,128]{1,0:T(8,128)S(1)}, u32[]{:S(2)}, u32[]{:S(2)}) collective-permute-start(f32[16,128]{1,0:T(8,128)S(1)} %get-tuple-element.30), channel_id=1, source_target_pairs={{0,6},{1,7},{2,4},{3,5},{4,2},{5,3},{6,0},{7,1},{8,14},{9,15},{10,... | collective-permute-start | bytes 24584 | tf_op jit(solution)/shard_map/ppermute | solution.py:318
  16.1 4.5 %collective-permute-start.6 = (f32[16,128]{1,0:T(8,128)S(1)}, f32[16,128]{1,0:T(8,128)S(1)}, u32[]{:S(2)}, u32[]{:S(2)}) collective-permute-start(f32[16,128]{1,0:T(8,128)S(1)} %get-tuple-element.31), channel_id=1, source_target_pairs={{0,4},{1,5},{2,6},{3,7},{4,0},{5,1},{6,2},{7,3},{8,12},{9,13},{10,... | collective-permute-start | bytes 24584 | tf_op jit(solution)/shard_map/ppermute | solution.py:318
  16.1 4.5 %collective-permute-start.7 = (f32[16,128]{1,0:T(8,128)S(1)}, f32[16,128]{1,0:T(8,128)S(1)}, u32[]{:S(2)}, u32[]{:S(2)}) collective-permute-start(f32[16,128]{1,0:T(8,128)S(1)} %get-tuple-element.32), channel_id=1, source_target_pairs={{0,2},{1,3},{2,0},{3,1},{4,6},{5,7},{6,4},{7,5},{8,10},{9,11},{10,... | collective-permute-start | bytes 24584 | tf_op jit(solution)/shard_map/ppermute | solution.py:318

commit v5 on v4

--- a/solution.py
+++ b/solution.py
@@ -53,7 +53,7 @@
     seg_here = lax.axis_index("seg")
     core, chip = seg_here % 2, seg_here // 2
     start = start_ref[chip * 2 + (core ^ side)]
-    residue = residue_ref[(chip ^ m) * 2 + core]
+    residue = residue_ref[(chip ^ m) * 2 + (core ^ (m > 0))]
     return start, (residue - start % seg_count + seg_count) % seg_count
 
 
@@ -69,21 +69,21 @@
             spectra_ref[pl.ds(row, tiles, stride=slots + 1), :] = src_ref[first + j * seg_count].astype(jnp.float32) * both
 
 
-def chunk_masks(group):
-    shape = (group.chunks, LANES)
+def chunk_masks(splat_ref, mask_ref):
+    shape = mask_ref.shape[2:]
     lanes = lax.broadcasted_iota(jnp.int32, shape, 1)
     starts = lax.broadcasted_iota(jnp.int32, shape, 0) * CHUNK
-    for t in range(group.count):
+    for t in range(mask_ref.shape[0]):
         low = high = jnp.full(shape, CHUNK, jnp.int32)
-        past = [group.edge_rows(t, p, shape) - starts for p in range(1, group.bins)]
+        past = [jnp.broadcast_to(splat_ref[p, t : t + 1, :], shape) - starts for p in range(1, splat_ref.shape[0] - 1)]
         here = [(q >= 0) & (q < CHUNK) for q in past]
         for q, inside in zip(past, here):
             high = jnp.where(inside, q, high)
         for q, inside in zip(reversed(past), reversed(here)):
             low = jnp.where(inside, q, low)
-        group.mask[t, 0] = jnp.where(lanes < low, 1.0, 0.0)
-        group.mask[t, 1] = jnp.where(lanes >= high, 1.0, 0.0)
-        group.mask[t, 2] = jnp.where(high < CHUNK, 1.0, 0.0)
+        mask_ref[t, 0] = jnp.where(lanes < low, 1.0, 0.0)
+        mask_ref[t, 1] = jnp.where(lanes >= high, 1.0, 0.0)
+        mask_ref[t, 2] = jnp.where(high < CHUNK, 1.0, 0.0)
 
 
 def sigma_rows(group, t, psd_ref):
@@ -94,7 +94,8 @@
     shape = power.shape
     ids = lax.broadcasted_iota(jnp.int32, shape, 0) // 2 * LANES + lax.broadcasted_iota(jnp.int32, shape, 1)
     below = [ids < group.edge_rows(t, p, shape) for p in range(1, bins)]
-    parts = []
+    row_pair = lax.broadcasted_iota(jnp.int32, (8, LANES), 0) // 2
+    packs = []
     for p in range(bins):
         if p == 0:
             member = below[0]
@@ -106,12 +107,18 @@
         part = functools.reduce(jnp.add, [part[i : i + 8] for i in range(0, half, 8)])
         part = part + pltpu.roll(part, 4, 0)
         part = part + pltpu.roll(part, 2, 0)
-        parts.append(jnp.broadcast_to(jnp.sum(part, axis=1, keepdims=True), (8, LANES)))
-    total = functools.reduce(jnp.add, parts)
-    for p in range(bins):
-        group.inv[t, p] = 1.0 / parts[p]
-        group.frac[t, p] = parts[p] / total
-    group.inv[t, bins] = 1.0 / total
+        if p % 4 == 0:
+            packs.append(part)
+        else:
+            packs[-1] = jnp.where(row_pair == p % 4, part, packs[-1])
+    packs = [jnp.broadcast_to(jnp.sum(x, axis=1, keepdims=True), (8, LANES)) for x in packs]
+    total = functools.reduce(jnp.add, packs)
+    total = total + pltpu.roll(total, 4, 0)
+    total = 1.0 / (total + pltpu.roll(total, 2, 0))
+    for i, pack in enumerate(packs):
+        group.inv[t, 8 * i : 8 * i + 8] = 1.0 / pack
+        group.frac[t, 8 * i : 8 * i + 8] = pack * total
+    group.inv[t, 2 * bins : 2 * bins + 8] = total
 
 
 class Group:
@@ -124,6 +131,9 @@
     def edge_rows(self, t, p, shape):
         return jnp.broadcast_to(self.splat[p, pl.ds(self.first + t, 1), :], shape)
 
+    def mask_row(self, t, kind, c):
+        return self.mask[self.first + t, kind, c : c + 1, :]
+
     def edge(self, t, p):
         return self.splat[p, pl.ds(self.first + t, 1), :][0, 0]
 
@@ -156,7 +166,6 @@
 
 
 def add_up(group, spectra_ref, psd_ref, dft_ref, beside=()):
-    chunk_masks(group)
     for t in range(group.count):
         sigma_rows(group, t, psd_ref)
     rows = group.rows
@@ -166,13 +175,13 @@
         stack = []
         for t in range(group.count):
             prod = product(group, spectra_ref, t, c)
-            stack.append(masked(prod, group.mask[t, 0, c : c + 1, :]))
-            stack.append(masked(prod, group.mask[t, 1, c : c + 1, :]))
+            stack.append(masked(prod, group.mask_row(t, 0, c)))
+            stack.append(masked(prod, group.mask_row(t, 1, c)))
         got = jnp.dot(jnp.concatenate(stack, axis=0), dft_ref[c], preferred_element_type=jnp.float32)
         for t in range(group.count):
             ended = running[t] + got[2 * t * rows : (2 * t + 1) * rows]
             group.series[t, c] = ended
-            cross = jnp.broadcast_to(group.mask[t, 2, c : c + 1, :], (rows, LANES)) > 0.5
+            cross = jnp.broadcast_to(group.mask_row(t, 2, c), (rows, LANES)) > 0.5
             running[t] = jnp.where(cross, got[(2 * t + 1) * rows : (2 * t + 2) * rows], ended)
         for write in beside.get(c, ()):
             write()
@@ -201,38 +210,48 @@
         lax.fori_loop(0, len(pairs), one, 0)
 
 
-def test_values(group, t, out_ref):
+def sums_at(group, t):
+    chunk_of = [group.chunk_of(t, p) for p in range(1, group.bins)]
+    places = [chunk_of[0]]
+    for p in range(1, group.bins - 1):
+        places.append(jnp.where(chunk_of[p - 1] == chunk_of[p], group.chunks + p, chunk_of[p]))
+    return places + [group.chunks]
+
+
+def test_values(group, t, places, start, out_ref):
     slots, bins = group.rows // 2, group.bins
     row = group.first + t
-
-    def spread(ref, p):
-        return jnp.concatenate(
-            [jnp.broadcast_to(ref[t, p, d : d + 1, :], (slots, LANES)) for d in range(2)], axis=0
-        )
-
-    chunk_of = [group.chunk_of(t, p) for p in range(1, bins)]
-    series = [group.series[t, chunk_of[0]]]
-    for p in range(1, bins - 1):
-        at = jnp.where(chunk_of[p - 1] == chunk_of[p], group.chunks + p, chunk_of[p])
-        series.append(group.series[t, at])
-    series.append(group.series[t, group.chunks])
-    whole = functools.reduce(jnp.add, series)
-    chi = jnp.zeros((group.rows, LANES), jnp.float32)
-    for p in range(bins):
-        dev = series[p] - spread(group.frac, p) * whole
-        chi = chi + dev * dev * spread(group.inv, p)
-    chi = jnp.sum(chi[:slots] + chi[slots:], axis=1, keepdims=True) / (TIME_LAGS * 2.0 * 2 * (bins - 1))
-    power = whole * whole * spread(group.inv, bins)
-    power = power[:slots] + power[slots:]
+    chi = power = None
+    for d in range(2):
+
+        def spread(ref, p, d=d):
+            return jnp.broadcast_to(ref[t, 2 * p + d : 2 * p + d + 1, :], (8, LANES))
+
+        rows = pl.ds(d * slots + start, 8)
+        series = [group.series[t, place, rows, :] for place in places]
+        whole = functools.reduce(jnp.add, series)
+        for p in range(bins):
+            dev = series[p] - spread(group.frac, p) * whole
+            term = dev * dev * spread(group.inv, p)
+            chi = term if chi is None else chi + term
+        term = whole * whole * spread(group.inv, bins)
+        power = term if power is None else power + term
+    chi = jnp.sum(chi, axis=1, keepdims=True)
     power = power + pltpu.roll(power, TIME_LAGS, 1)
-    peak = jnp.sqrt(jnp.max(power, axis=1, keepdims=True))
-    out_ids = lax.broadcasted_iota(jnp.int32, (slots, LANES), 1)
-    out = jnp.where(out_ids == row, peak, out_ref[...])
-    out_ref[...] = jnp.where(out_ids == row + group.splat.shape[1], chi, out)
+    peak = jnp.max(power, axis=1, keepdims=True)
+    out_ids = lax.broadcasted_iota(jnp.int32, (8, LANES), 1)
+    out = jnp.where(out_ids == row, peak, out_ref[start : start + 8, :])
+    out_ref[start : start + 8, :] = jnp.where(out_ids == row + group.splat.shape[1], chi, out)
 
 
 def values_of(group, out_ref):
-    return [functools.partial(test_values, group, t, out_ref) for t in range(group.count)]
+    writes = []
+    for t in range(group.count):
+        places = sums_at(group, t)
+        writes += [
+            functools.partial(test_values, group, t, places, start, out_ref) for start in range(0, group.rows // 2, 8)
+        ]
+    return writes
 
 
 def begin_kernel(out_ref):
@@ -242,11 +261,12 @@
 def own_kernel(
     seg_count,
     _, other_ref, own_ref, tmpl_ref, psd_ref, dft_ref, order_ref, seg_ref, edge_ref,
-    spectra_ref, splat_ref, out_ref,
-    start_ref, residue_ref, mask_ref, series_ref, inv_ref, frac_ref,
+    spectra_ref, splat_ref, mask_ref, out_ref,
+    start_ref, residue_ref, series_ref, inv_ref, frac_ref,
 ):
     for p in range(splat_ref.shape[0]):
         splat_ref[p] = jnp.broadcast_to(edge_ref[:, p : p + 1], splat_ref.shape[1:])
+    chunk_masks(splat_ref, mask_ref)
     seg_starts(seg_ref, start_ref, seg_count)
     inverse_order(order_ref, residue_ref, seg_count)
     arrange_strain(0, own_ref, psd_ref, spectra_ref, start_ref, residue_ref, seg_count)
@@ -259,20 +279,20 @@
         write()
 
 
-def mid_kernel(source, old_source, tmpl_ref, spectra_ref, dft_ref, psd_ref, splat_ref, old, sums, out_ref, mask_ref):
+def mid_kernel(source, old_source, tmpl_ref, spectra_ref, dft_ref, psd_ref, splat_ref, mask_ref, old, sums, out_ref):
     bank, count = lax.axis_index("bank"), tmpl_ref.shape[0]
     group = Group(tmpl_ref, (bank ^ source()) * count, splat_ref, *sums, mask_ref)
     beside = {}
     if old:
         out_ref[...] = old[3][...]
         writes = values_of(Group(None, (bank ^ old_source()) * count, splat_ref, *old[:3]), out_ref)
-        beside = {4 * n + 3: [write] for n, write in enumerate(writes)}
+        beside = {n + 1: [write] for n, write in enumerate(writes)}
     add_up(group, spectra_ref, psd_ref, dft_ref, beside)
 
 
 def last_kernel(
-    seg_count, sources, tmpl_ref, spectra_ref, dft_ref, psd_ref, splat_ref, order_ref, seg_ref, old_sums, part_ref,
-    out_refs, sums, mask_ref, all_ref, placed_ref, start_ref, residue_ref, place_ref,
+    seg_count, sources, tmpl_ref, spectra_ref, dft_ref, psd_ref, splat_ref, mask_ref, order_ref, seg_ref, old_sums,
+    part_ref, out_refs, sums, all_ref, placed_ref, start_ref, residue_ref, place_ref,
 ):
     pair_slots = all_ref.shape[0] // seg_count
     seg_here = lax.axis_index("seg")
@@ -295,9 +315,12 @@
     old = Group(None, (bank ^ sources[0]()) * count, splat_ref, *old_sums)
     group = Group(tmpl_ref, (bank ^ sources[1]()) * count, splat_ref, *sums, mask_ref)
     writes = values_of(old, all_ref)
-    add_up(group, spectra_ref, psd_ref, dft_ref, {3: writes[:1], 6: writes[1:2], 8: [place], 9: writes[2:]})
+    add_up(group, spectra_ref, psd_ref, dft_ref, {n + 1: [write] for n, write in enumerate([place] + writes)})
     for write in values_of(group, all_ref):
         write()
+    lanes = lax.broadcasted_iota(jnp.int32, all_ref.shape, 1)
+    scale = 1.0 / (TIME_LAGS * 2.0 * 2 * (group.bins - 1))
+    all_ref[...] = jnp.where(lanes < splat_ref.shape[1], jnp.sqrt(all_ref[...]), all_ref[...] * scale)
     ids = lax.broadcasted_iota(jnp.int32, (pair_slots, LANES), 0)
     for m in range(seg_count // 2):
         for source in range(2):
@@ -335,9 +358,8 @@
         return jax.ShapeDtypeStruct(dims, dtype)
 
     chunks = freq_count // CHUNK
-    sums = [(tmpl_count, chunks + bins - 1, rows, 2 * TIME_LAGS)] + [(tmpl_count, bins + 1, 8, LANES)] * 2
+    sums = [(tmpl_count, chunks + bins - 1, rows, 2 * TIME_LAGS)] + [(tmpl_count, 2 * bins + 8, LANES)] * 2
     sum_shapes = tuple(shape(*dims) for dims in sums)
-    mask = pltpu.VMEM((tmpl_count, 3, chunks, LANES), f32)
     tables = [pltpu.SMEM((seg_count + 1,), i32), pltpu.SMEM((seg_count,), i32)]
 
     def call(kernel, name, flops, bytes_accessed=4 * 10**6, **kwargs):
@@ -351,24 +373,28 @@
 
     begin = call(begin_kernel, "begin", 2 * 10**9, 1, out_shape=shape(8, LANES), out_specs=VMEM)()
     other = tile_rows(swap(strain, "seg", 1))
-    far = [tile_rows(swap(templates, "bank", s)) for s in range(3, bank_count)]
-    near = [(b * seg_count + s, (b ^ (1 + s % 2)) * seg_count + s) for b in range(bank_count) for s in range(seg_count)]
-    near = lax.ppermute(templates, ("bank", "seg"), near)
+    def fetch(x, step):
+        here = [(b, s) for b in range(bank_count) for s in range(seg_count)]
+        return lax.ppermute(x, ("bank", "seg"), [((b ^ step(s)) * seg_count + (s ^ 1), b * seg_count + s) for b, s in here])
+
+    far = [tile_rows(fetch(templates, lambda _, n=n: n)) for n in range(3, bank_count)]
+    near = fetch(templates, lambda s: 2 - s % 2)
 
     splat_shape = shape(bins + 1, tmpl_total, LANES, dtype=i32)
-    spectra, splat, out = call(
+    spectra, splat, mask, out = call(
         functools.partial(own_kernel, seg_count),
         "own_templates",
         10**9,
-        out_shape=(shape((slots + 1) * tiles, LANES), splat_shape, shape(slots, LANES)),
+        out_shape=(shape((slots + 1) * tiles, LANES), splat_shape)
+        + (shape(tmpl_total, 3, chunks, LANES), shape(slots, LANES)),
         in_specs=[VMEM] * 9,
-        out_specs=(VMEM,) * 3,
-        scratch_shapes=tables + [mask] + [pltpu.VMEM(dims, f32) for dims in sums],
+        out_specs=(VMEM,) * 4,
+        scratch_shapes=tables + [pltpu.VMEM(dims, f32) for dims in sums],
     )(begin, other, tile_rows(strain), tile_rows(templates), psd, dft, dest_order, seg_blocks, bin_edges)
 
     near, spectra = lax.optimization_barrier((near, spectra))
-    held = (spectra, dft, psd, splat)
-    sources = [lambda: 1 + core_here(), lambda: 2 - core_here()]
+    held = (spectra, dft, psd, splat, mask)
+    sources = [lambda: 2 - core_here(), lambda: 1 + core_here()]
     sources += [functools.partial(int, s) for s in range(3, bank_count)]
     remote = [[tile_rows(near)], [tile_rows(swap(part, "seg", 1)) for part in (near[:2], near[2:])]]
     remote += [[x] for x in far]
@@ -377,7 +403,7 @@
 
         def mid(*refs, n=n, count=len(old), split=len(parts)):
             parts, refs = refs[:split], refs[split:]
-            ins, olds, (*outs, mask_ref, tmpl_ref) = refs[:4], refs[4 : 4 + count], refs[4 + count :]
+            ins, olds, (*outs, tmpl_ref) = refs[:5], refs[5 : 5 + count], refs[5 + count :]
             if split > 1:
                 row = 0
                 for ref in parts:
@@ -386,7 +412,7 @@
             else:
                 (tmpl_ref,) = parts
             out_ref = outs[3] if olds else None
-            mid_kernel(sources[n], sources[n - 1], tmpl_ref, *ins, olds, outs[:3], out_ref, mask_ref)
+            mid_kernel(sources[n], sources[n - 1], tmpl_ref, *ins, olds, outs[:3], out_ref)
 
         outs = sum_shapes + ((shape(slots, LANES),) if old else ())
         new = call(
@@ -395,14 +421,14 @@
             1,
             1,
             out_shape=outs,
-            in_specs=[VMEM] * (4 + len(parts) + len(old)),
+            in_specs=[VMEM] * (5 + len(parts) + len(old)),
             out_specs=(VMEM,) * len(outs),
-            scratch_shapes=[mask, pltpu.VMEM((tmpl_count, tiles, LANES), f32)],
+            scratch_shapes=[pltpu.VMEM((tmpl_count, tiles, LANES), f32)],
         )(*parts, *held, *old)
         old = list(new) if old else [*new, out]
 
     def last(*refs):
-        ins, sums_in, part_ref, refs = refs[:7], refs[7:10], refs[10], refs[11:]
+        ins, sums_in, part_ref, refs = refs[:8], refs[8:11], refs[11], refs[12:]
         outs, refs = refs[:chip_count], refs[chip_count:]
         last_kernel(seg_count, sources[-2:], *ins, sums_in, part_ref, outs, refs[:3], *refs[3:])
 
@@ -411,16 +437,15 @@
         "last_templates",
         10**9,
         out_shape=(shape(BLK_DEV, LANES),) * chip_count,
-        in_specs=[VMEM] * 11,
+        in_specs=[VMEM] * 12,
         out_specs=(VMEM,) * chip_count,
         scratch_shapes=[pltpu.VMEM(dims, f32) for dims in sums]
-        + [mask]
         + [pltpu.VMEM((slots, LANES), f32), pltpu.VMEM((chip_count, BLK_DEV + 8, LANES), f32)]
         + tables
         + [pltpu.SMEM((4 * chip_count,), i32)],
     )(*remote[-1], *held, dest_order, seg_blocks, *old)
 
-    got = [swap(parts[m], "seg", 2 * m) for m in reversed(range(1, chip_count))] + [parts[0]]
+    got = [swap(parts[m], "seg", 2 * m + 1) for m in reversed(range(1, chip_count))] + [parts[0]]
     return call(
         lambda *refs: add_kernel(refs[:chip_count], *refs[chip_count:]),
         "add_rows",

time: 21.4 us -> 20.3 us (0.949)
  starting transfers between devices: 9.9 us -> 9.07 us
  waiting for transfers between devices: 3.92 us -> 3.5 us
    ppermute x7 -> x6, starting transfers between devices: 7.34 us -> 5.34 us  [swap(): lax.ppermute(x, axis, [(i, i ^ step) for i in range(lax.axis_size(axis))])]
    ppermute x1 -> x2, starting transfers between devices: 2.56 us -> 3.73 us  [fetch(): lax.ppermute(x, ('bank', 'seg'), [((b ^ step(s)) * seg_count + (s ^ 1), b...]
    ppermute x7 -> x6, waiting for transfers between devices: 3.92 us -> 3.5 us  [swap(): lax.ppermute(x, axis, [(i, i ^ step) for i in range(lax.axis_size(axis))])]
  transfers between devices with their start and end apart: 8 -> 8, of which waited for: 2 -> 2; matrix products, arithmetic and copies ran while one was open for 0% -> 0% of each run, Pallas kernels for 20% -> 21%
where the time goes in v5:
time: 20.3 us; the launch traced here: 20.1 us
  starting transfers between devices  9.07 us (45%)
  Pallas kernels  6.71 us (33%)
  waiting for transfers between devices  3.5 us (17%)
  between operations  0.78 us (4%)
    ppermute x6, starting transfers between devices, swap(): lax.ppermute(x, axis, [(i, i ^ step) for i in range(lax.axis_size(axis))])  5.34 us
    ppermute x2, starting transfers between devices, fetch(): lax.ppermute(x, ('bank', 'seg'), [((b ^ step(s)) * seg_count + (s ^ 1), b...  3.73 us
    ppermute x6, waiting for transfers between devices, swap(): lax.ppermute(x, axis, [(i, i ^ step) for i in range(lax.axis_size(axis))])  3.5 us
    pallas_call x2, Pallas kernels, body(): call(mid, 'mid_templates' if old else 'next_templates', 1, 1, out_shape=o...  2.47 us
    pallas_call x1, Pallas kernels, body(): call(functools.partial(own_kernel, seg_count), 'own_templates', 10 ** 9,...  1.84 us
    pallas_call x1, Pallas kernels, body(): call(last, 'last_templates', 10 ** 9, out_shape=(shape(BLK_DEV, LANES),)...  1.73 us
    pallas_call x1, Pallas kernels, body(): call(lambda *refs: add_kernel(refs[:chip_count], *refs[chip_count:]), 'ad...  0.67 us
  transfers between devices with their start and end apart: 8, of which 2 were waited for; matrix products, arithmetic and copies ran while one was open for 0% of the time, Pallas kernels for 21%

profile of v5, /device:TPU:0, one launch (start us, length us, event | category | flops | bytes accessed | tf_op | source)
XLA Modules:
  0.0 20.1 jit_solution(2729497716954047701)
XLA Ops:
  0.6 0.0 copy-start
  0.6 0.0 copy-start.4
  0.7 0.0 copy-start.5
  0.7 0.0 copy-start.1
  0.7 0.0 copy-start.3
  0.7 0.0 copy-start.2
  0.7 0.0 copy-start.6
  0.7 0.5 %collective-permute-start.2 = (bf16[32,2,4096]{2,1,0:T(2,128)(2,1)}, bf16[32,2,4096]{2,1,0:T(2,128)(2,1)S(1)}, u32[]{:S(2)}, u32[]{:S(2)}) collective-permute-start(bf16[32,2,4096]{2,1,0:T(2,128)(2,1)} %param.7), channel_id=1, source_target_pairs={{0,1},{1,0},{2,3},{3,2},{4,5},{5,4},{6,7},{7,6},{8,9},{9,8},{10,11... | collective-permute-start | bytes 1572872 | tf_op jit(solution)/shard_map/ppermute | solution.py:341
  1.2 2.6 %collective-permute-start.1 = (f32[3,2,4096]{2,1,0:T(2,128)}, f32[3,2,4096]{2,1,0:T(2,128)S(1)}, u32[]{:S(2)}, u32[]{:S(2)}) collective-permute-start(f32[3,2,4096]{2,1,0:T(2,128)} %param.8), channel_id=1, source_target_pairs={{17,0},{8,1},{19,2},{10,3},{21,4},{12,5},{23,6},{14,7},{25,8},{0,9... | collective-permute-start | bytes 294920 | tf_op jit(solution)/shard_map/ppermute | solution.py:378
  3.8 1.1 %collective-permute-start = (f32[3,2,4096]{2,1,0:T(2,128)}, f32[3,2,4096]{2,1,0:T(2,128)S(1)}, u32[]{:S(2)}, u32[]{:S(2)}) collective-permute-start(f32[3,2,4096]{2,1,0:T(2,128)} %param.8), channel_id=1, source_target_pairs={{25,0},{24,1},{27,2},{26,3},{29,4},{28,5},{31,6},{30,7},{17,8},{16... | collective-permute-start | bytes 294920 | tf_op jit(solution)/shard_map/ppermute | solution.py:378
  5.0 0.0 collective-permute-done.2
  5.0 0.0 copy-done
  5.0 0.0 copy-done.4
  5.0 0.0 copy-done.5
  5.0 0.0 copy-done.1
  5.0 0.0 copy-done.3
  5.0 0.0 copy-done.2
  5.0 0.0 copy-done.6
  5.0 1.8 %own_templates.1 = (f32[2112,128]{1,0:T(8,128)S(1)}, s32[9,12,128]{2,1,0:T(8,128)S(1)}, f32[12,3,16,128]{3,2,1,0:T(8,128)S(1)}, f32[32,128]{1,0:T(8,128)S(1)}) custom-call(f32[8,128]{1,0:T(8,128)S(1)} %begin.1._, bf16[32,64,128]{2,1,0:T(8,128)(2,1)S(1)} %bitcast.49, bf16[32,64,128]{2,1,0:T(8,128)(2,1)S(1)} %bitcast.48, f32[3,64,128]{2,1,0:T(8,128)S(1)} %bitcast.50, ...), custom_call_target="tpu_custom_call" | custom-call | flops 1000000000 | bytes 4000000 | tf_op jit(solution)/shard_map/own_templates/pallas_call | solution.py:384
  6.9 0.0 collective-permute-done.1
  6.9 0.5 %collective-permute-start.3 = (f32[2,2,4096]{2,1,0:T(2,128)S(1)}, f32[2,2,4096]{2,1,0:T(2,128)S(1)}, u32[]{:S(2)}, u32[]{:S(2)}) collective-permute-start(f32[2,2,4096]{2,1,0:T(2,128)S(1)} %slice.6), channel_id=1, source_target_pairs={{0,1},{1,0},{2,3},{3,2},{4,5},{5,4},{6,7},{7,6},{8,9},{9,8},{10,11... | collective-permute-start | bytes 196616 | tf_op jit(solution)/shard_map/ppermute | solution.py:341
  7.4 0.1 collective-permute-start.4
  7.5 1.1 %next_templates.1 = (f32[3,23,64,128]{3,2,1,0:T(8,128)S(1)}, f32[3,24,128]{2,1,0:T(8,128)S(1)}, f32[3,24,128]{2,1,0:T(8,128)S(1)}) custom-call(f32[3,64,128]{2,1,0:T(8,128)S(1)} %bitcast.40, f32[2112,128]{1,0:T(8,128)S(1)} %get-tuple-element.20.refs_1_.refs_2_, bf16[16,256,128]{2,1,0:T(8,128)(2,1)S(1)} %copy-done, f32[32,128]{1,0:T(8,128)S(1)} %bitcast.42, ...), custom_call_target="tpu_custom_call" | custom-call | flops 1 | bytes 1 | tf_op jit(solution)/shard_map/next_templates/pallas_call | solution.py:418
  8.6 0.0 collective-permute-done.4
  8.6 0.0 collective-permute-done.3
  8.6 1.4 %mid_templates.1 = (f32[3,23,64,128]{3,2,1,0:T(8,128)S(1)}, f32[3,24,128]{2,1,0:T(8,128)S(1)}, f32[3,24,128]{2,1,0:T(8,128)S(1)}, f32[32,128]{1,0:T(8,128)S(1)}) custom-call(f32[2,64,128]{2,1,0:T(8,128)S(1)} %bitcast.46, f32[1,64,128]{2,1,0:T(8,128)S(1)} %bitcast.47, f32[2112,128]{1,0:T(8,128)S(1)} %get-tuple-element.20.refs_1_.refs_2_, ...), custom_call_target="tpu_custom_call" | custom-call | flops 1 | bytes 1 | tf_op jit(solution)/shard_map/mid_templates/pallas_call | solution.py:418
  10.0 0.0 collective-permute-done
  10.0 1.7 %last_templates.1 = (f32[16,128]{1,0:T(8,128)S(1)}, f32[16,128]{1,0:T(8,128)S(1)}, f32[16,128]{1,0:T(8,128)S(1)}, f32[16,128]{1,0:T(8,128)S(1)}) custom-call(f32[3,64,128]{2,1,0:T(8,128)S(1)} %bitcast.45, f32[2112,128]{1,0:T(8,128)S(1)} %get-tuple-element.20.refs_1_.refs_2_, bf16[16,256,128]{2,1,0:T(8,128)(2,1)S(1)} %copy-done, f32[32,128]{1,0:T(8,128)S(1)} %bitcast.44, ...), custom_call_target="tpu_custom_call" | custom-call | flops 1000000000 | bytes 4000000 | tf_op jit(solution)/shard_map/last_templates/pallas_call | solution.py:435
  11.8 3.7 %collective-permute-start.5 = (f32[16,128]{1,0:T(8,128)S(1)}, f32[16,128]{1,0:T(8,128)S(1)}, u32[]{:S(2)}, u32[]{:S(2)}) collective-permute-start(f32[16,128]{1,0:T(8,128)S(1)} %get-tuple-element.32), channel_id=1, source_target_pairs={{0,7},{1,6},{2,5},{3,4},{4,3},{5,2},{6,1},{7,0},{8,15},{9,14},{10,... | collective-permute-start | bytes 24584 | tf_op jit(solution)/shard_map/ppermute | solution.py:341
  15.5 0.0 collective-permute-start.6
  15.5 0.5 %collective-permute-start.7 = (f32[16,128]{1,0:T(8,128)S(1)}, f32[16,128]{1,0:T(8,128)S(1)}, u32[]{:S(2)}, u32[]{:S(2)}) collective-permute-start(f32[16,128]{1,0:T(8,128)S(1)} %get-tuple-element.34), channel_id=1, source_target_pairs={{0,3},{1,2},{2,1},{3,0},{4,7},{5,6},{6,5},{7,4},{8,11},{9,10},{10,... | collective-permute-start | bytes 24584 | tf_op jit(solution)/shard_map/ppermute | solution.py:341
  16.0 0.9 %collective-permute-done.5.refs_0_ = f32[16,128]{1,0:T(8,128)S(1)} collective-permute-done((f32[16,128]{1,0:T(8,128)S(1)}, f32[16,128]{1,0:T(8,128)S(1)}, u32[]{:S(2)}, u32[]{:S(2)}) %collective-permute-start.5) | collective-permute-done | bytes 8224 | tf_op jit(solution)/shard_map/ppermute | solution.py:341
  16.8 2.6 %collective-permute-done.6.refs_1_ = f32[16,128]{1,0:T(8,128)S(1)} collective-permute-done((f32[16,128]{1,0:T(8,128)S(1)}, f32[16,128]{1,0:T(8,128)S(1)}, u32[]{:S(2)}, u32[]{:S(2)}) %collective-permute-start.6) | collective-permute-done | bytes 8224 | tf_op jit(solution)/shard_map/ppermute | solution.py:341
  19.4 0.0 collective-permute-done.7.refs_2_
  19.4 0.7 %add_rows.1 = (f32[16,12]{1,0:T(8,128)}, f32[16,12]{1,0:T(8,128)}) custom-call(f32[16,128]{1,0:T(8,128)S(1)} %collective-permute-done.5.refs_0_, f32[16,128]{1,0:T(8,128)S(1)} %collective-permute-done.6.refs_1_, f32[16,128]{1,0:T(8,128)S(1)} %collective-permute-done.7.refs_2_, f32[16,128]{1,0:T(8,128)S(1)} %get-tuple-element.35.refs_3_), custom_call_target="tpu_custom_call" | custom-call | flops 100000 | bytes 4000000 | tf_op jit(solution)/shard_map/add_rows/pallas_call | solution.py:449
  (3 shorter events, 0.0 us)
Async XLA Ops:
  0.6 4.3 %copy-start = (bf16[16,256,128]{2,1,0:T(8,128)(2,1)S(1)}, bf16[16,256,128]{2,1,0:T(8,128)(2,1)}, u32[]{:S(2)}) copy-start(bf16[16,256,128]{2,1,0:T(8,128)(2,1)} %constant.2.clone.dft_ref.refs_2_.refs_3_) | copy-start | bytes 3145732
  0.6 4.3 %copy-start.4 = (bf16[32,2,4096]{2,1,0:T(2,128)(2,1)S(1)}, bf16[32,2,4096]{2,1,0:T(2,128)(2,1)}, u32[]{:S(2)}) copy-start(bf16[32,2,4096]{2,1,0:T(2,128)(2,1)} %param.7) | copy-start | bytes 1572868
  0.7 4.3 %copy-start.5 = (f32[3,2,4096]{2,1,0:T(2,128)S(1)}, f32[3,2,4096]{2,1,0:T(2,128)}, u32[]{:S(2)}) copy-start(f32[3,2,4096]{2,1,0:T(2,128)} %param.8) | copy-start | bytes 294916
  0.7 4.3 %copy-start.1 = (f32[2,2048]{1,0:T(2,128)S(1)}, f32[2,2048]{1,0:T(2,128)}, u32[]{:S(2)}) copy-start(f32[2,2048]{1,0:T(2,128)} %param.9) | copy-start | bytes 49156
  0.7 4.3 %copy-start.3 = (s32[1,8]{1,0:T(1,128)S(1)}, s32[1,8]{1,0:T(1,128)}, u32[]{:S(2)}) copy-start(s32[1,8]{1,0:T(1,128)} %refs_7_.1) | copy-start | bytes 100
  0.7 4.3 %copy-start.2 = (s32[1,8]{1,0:T(1,128)S(1)}, s32[1,8]{1,0:T(1,128)}, u32[]{:S(2)}) copy-start(s32[1,8]{1,0:T(1,128)} %refs_6_.1) | copy-start | bytes 100
  0.7 4.3 %copy-start.6 = (s32[12,9]{1,0:T(8,128)S(1)}, s32[12,9]{1,0:T(8,128)}, u32[]{:S(2)}) copy-start(s32[12,9]{1,0:T(8,128)} %edge_ref.1) | copy-start | bytes 1300
  0.7 4.3 %collective-permute-start.2 = (bf16[32,2,4096]{2,1,0:T(2,128)(2,1)}, bf16[32,2,4096]{2,1,0:T(2,128)(2,1)S(1)}, u32[]{:S(2)}, u32[]{:S(2)}) collective-permute-start(bf16[32,2,4096]{2,1,0:T(2,128)(2,1)} %param.7), channel_id=1, source_target_pairs={{0,1},{1,0},{2,3},{3,2},{4,5},{5,4},{6,7},{7,6},{8,9},{9,8},{10,11... | collective-permute-start | bytes 1572872 | tf_op jit(solution)/shard_map/ppermute | solution.py:341
  1.2 5.6 %collective-permute-start.1 = (f32[3,2,4096]{2,1,0:T(2,128)}, f32[3,2,4096]{2,1,0:T(2,128)S(1)}, u32[]{:S(2)}, u32[]{:S(2)}) collective-permute-start(f32[3,2,4096]{2,1,0:T(2,128)} %param.8), channel_id=1, source_target_pairs={{17,0},{8,1},{19,2},{10,3},{21,4},{12,5},{23,6},{14,7},{25,8},{0,9... | collective-permute-start | bytes 294920 | tf_op jit(solution)/shard_map/ppermute | solution.py:378
  3.8 6.2 %collective-permute-start = (f32[3,2,4096]{2,1,0:T(2,128)}, f32[3,2,4096]{2,1,0:T(2,128)S(1)}, u32[]{:S(2)}, u32[]{:S(2)}) collective-permute-start(f32[3,2,4096]{2,1,0:T(2,128)} %param.8), channel_id=1, source_target_pairs={{25,0},{24,1},{27,2},{26,3},{29,4},{28,5},{31,6},{30,7},{17,8},{16... | collective-permute-start | bytes 294920 | tf_op jit(solution)/shard_map/ppermute | solution.py:378
  6.9 1.8 %collective-permute-start.3 = (f32[2,2,4096]{2,1,0:T(2,128)S(1)}, f32[2,2,4096]{2,1,0:T(2,128)S(1)}, u32[]{:S(2)}, u32[]{:S(2)}) collective-permute-start(f32[2,2,4096]{2,1,0:T(2,128)S(1)} %slice.6), channel_id=1, source_target_pairs={{0,1},{1,0},{2,3},{3,2},{4,5},{5,4},{6,7},{7,6},{8,9},{9,8},{10,11... | collective-permute-start | bytes 196616 | tf_op jit(solution)/shard_map/ppermute | solution.py:341
  7.4 1.2 %collective-permute-start.4 = (f32[1,2,4096]{2,1,0:T(2,128)S(1)}, f32[1,2,4096]{2,1,0:T(2,128)S(1)}, u32[]{:S(2)}, u32[]{:S(2)}) collective-permute-start(f32[1,2,4096]{2,1,0:T(2,128)S(1)} %slice.7), channel_id=1, source_target_pairs={{0,1},{1,0},{2,3},{3,2},{4,5},{5,4},{6,7},{7,6},{8,9},{9,8},{10,11... | collective-permute-start | bytes 98312 | tf_op jit(solution)/shard_map/ppermute | solution.py:341
  11.8 5.1 %collective-permute-start.5 = (f32[16,128]{1,0:T(8,128)S(1)}, f32[16,128]{1,0:T(8,128)S(1)}, u32[]{:S(2)}, u32[]{:S(2)}) collective-permute-start(f32[16,128]{1,0:T(8,128)S(1)} %get-tuple-element.32), channel_id=1, source_target_pairs={{0,7},{1,6},{2,5},{3,4},{4,3},{5,2},{6,1},{7,0},{8,15},{9,14},{10,... | collective-permute-start | bytes 24584 | tf_op jit(solution)/shard_map/ppermute | solution.py:341
  15.5 4.0 %collective-permute-start.6 = (f32[16,128]{1,0:T(8,128)S(1)}, f32[16,128]{1,0:T(8,128)S(1)}, u32[]{:S(2)}, u32[]{:S(2)}) collective-permute-start(f32[16,128]{1,0:T(8,128)S(1)} %get-tuple-element.33), channel_id=1, source_target_pairs={{0,5},{1,4},{2,7},{3,6},{4,1},{5,0},{6,3},{7,2},{8,13},{9,12},{10,... | collective-permute-start | bytes 24584 | tf_op jit(solution)/shard_map/ppermute | solution.py:341
  15.5 4.0 %collective-permute-start.7 = (f32[16,128]{1,0:T(8,128)S(1)}, f32[16,128]{1,0:T(8,128)S(1)}, u32[]{:S(2)}, u32[]{:S(2)}) collective-permute-start(f32[16,128]{1,0:T(8,128)S(1)} %get-tuple-element.34), channel_id=1, source_target_pairs={{0,3},{1,2},{2,1},{3,0},{4,7},{5,6},{6,5},{7,4},{8,11},{9,10},{10,... | collective-permute-start | bytes 24584 | tf_op jit(solution)/shard_map/ppermute | solution.py:341

commit v6 on v5

--- a/solution.py
+++ b/solution.py
@@ -445,7 +445,8 @@
         + [pltpu.SMEM((4 * chip_count,), i32)],
     )(*remote[-1], *held, dest_order, seg_blocks, *old)
 
-    got = [swap(parts[m], "seg", 2 * m + 1) for m in reversed(range(1, chip_count))] + [parts[0]]
+    order = [*range(2, chip_count), 1]
+    got = [swap(parts[m], "seg", 2 * m + 1) for m in order] + [parts[0]]
     return call(
         lambda *refs: add_kernel(refs[:chip_count], *refs[chip_count:]),
         "add_rows",

time: 20.3 us -> 20.1 us (level)
  starting transfers between devices: 9.07 us -> 8.82 us
    ppermute x6, starting transfers between devices: 5.34 us -> 5.09 us  [swap(): lax.ppermute(x, axis, [(i, i ^ step) for i in range(lax.axis_size(axis))])]
  transfers between devices with their start and end apart: 8 -> 8, of which waited for: 2 -> 2; matrix products, arithmetic and copies ran while one was open for 0% -> 0% of each run, Pallas kernels for 21% -> 22%
where the time goes in v6:
time: 20.1 us; the launch traced here: 20 us
  starting transfers between devices  8.82 us (44%)
  Pallas kernels  6.71 us (33%)
  waiting for transfers between devices  3.65 us (18%)
  between operations  0.78 us (4%)
    ppermute x6, starting transfers between devices, swap(): lax.ppermute(x, axis, [(i, i ^ step) for i in range(lax.axis_size(axis))])  5.09 us
    ppermute x2, starting transfers between devices, fetch(): lax.ppermute(x, ('bank', 'seg'), [((b ^ step(s)) * seg_count + (s ^ 1), b...  3.73 us
    ppermute x6, waiting for transfers between devices, swap(): lax.ppermute(x, axis, [(i, i ^ step) for i in range(lax.axis_size(axis))])  3.64 us
    pallas_call x2, Pallas kernels, body(): call(mid, 'mid_templates' if old else 'next_templates', 1, 1, out_shape=o...  2.47 us
    pallas_call x1, Pallas kernels, body(): call(functools.partial(own_kernel, seg_count), 'own_templates', 10 ** 9,...  1.84 us
    pallas_call x1, Pallas kernels, body(): call(last, 'last_templates', 10 ** 9, out_shape=(shape(BLK_DEV, LANES),)...  1.73 us
    pallas_call x1, Pallas kernels, body(): call(lambda *refs: add_kernel(refs[:chip_count], *refs[chip_count:]), 'ad...  0.67 us
  transfers between devices with their start and end apart: 8, of which 2 were waited for; matrix products, arithmetic and copies ran while one was open for 0% of the time, Pallas kernels for 22%

profile of v6, /device:TPU:0, one launch (start us, length us, event | category | flops | bytes accessed | tf_op | source)
XLA Modules:
  0.0 20.0 jit_solution(4741520065472198375)
XLA Ops:
  0.6 0.0 copy-start
  0.6 0.0 copy-start.4
  0.7 0.0 copy-start.5
  0.7 0.0 copy-start.1
  0.7 0.0 copy-start.3
  0.7 0.0 copy-start.2
  0.7 0.0 copy-start.6
  0.7 0.5 %collective-permute-start.2 = (bf16[32,2,4096]{2,1,0:T(2,128)(2,1)}, bf16[32,2,4096]{2,1,0:T(2,128)(2,1)S(1)}, u32[]{:S(2)}, u32[]{:S(2)}) collective-permute-start(bf16[32,2,4096]{2,1,0:T(2,128)(2,1)} %param.7), channel_id=1, source_target_pairs={{0,1},{1,0},{2,3},{3,2},{4,5},{5,4},{6,7},{7,6},{8,9},{9,8},{10,11... | collective-permute-start | bytes 1572872 | tf_op jit(solution)/shard_map/ppermute | solution.py:341
  1.2 2.6 %collective-permute-start.1 = (f32[3,2,4096]{2,1,0:T(2,128)}, f32[3,2,4096]{2,1,0:T(2,128)S(1)}, u32[]{:S(2)}, u32[]{:S(2)}) collective-permute-start(f32[3,2,4096]{2,1,0:T(2,128)} %param.8), channel_id=1, source_target_pairs={{17,0},{8,1},{19,2},{10,3},{21,4},{12,5},{23,6},{14,7},{25,8},{0,9... | collective-permute-start | bytes 294920 | tf_op jit(solution)/shard_map/ppermute | solution.py:378
  3.8 1.1 %collective-permute-start = (f32[3,2,4096]{2,1,0:T(2,128)}, f32[3,2,4096]{2,1,0:T(2,128)S(1)}, u32[]{:S(2)}, u32[]{:S(2)}) collective-permute-start(f32[3,2,4096]{2,1,0:T(2,128)} %param.8), channel_id=1, source_target_pairs={{25,0},{24,1},{27,2},{26,3},{29,4},{28,5},{31,6},{30,7},{17,8},{16... | collective-permute-start | bytes 294920 | tf_op jit(solution)/shard_map/ppermute | solution.py:378
  5.0 0.0 collective-permute-done.2
  5.0 0.0 copy-done
  5.0 0.0 copy-done.4
  5.0 0.0 copy-done.5
  5.0 0.0 copy-done.1
  5.0 0.0 copy-done.3
  5.0 0.0 copy-done.2
  5.0 0.0 copy-done.6
  5.0 1.8 %own_templates.1 = (f32[2112,128]{1,0:T(8,128)S(1)}, s32[9,12,128]{2,1,0:T(8,128)S(1)}, f32[12,3,16,128]{3,2,1,0:T(8,128)S(1)}, f32[32,128]{1,0:T(8,128)S(1)}) custom-call(f32[8,128]{1,0:T(8,128)S(1)} %begin.1._, bf16[32,64,128]{2,1,0:T(8,128)(2,1)S(1)} %bitcast.49, bf16[32,64,128]{2,1,0:T(8,128)(2,1)S(1)} %bitcast.48, f32[3,64,128]{2,1,0:T(8,128)S(1)} %bitcast.50, ...), custom_call_target="tpu_custom_call" | custom-call | flops 1000000000 | bytes 4000000 | tf_op jit(solution)/shard_map/own_templates/pallas_call | solution.py:384
  6.9 0.0 collective-permute-done.1
  6.9 0.5 %collective-permute-start.3 = (f32[2,2,4096]{2,1,0:T(2,128)S(1)}, f32[2,2,4096]{2,1,0:T(2,128)S(1)}, u32[]{:S(2)}, u32[]{:S(2)}) collective-permute-start(f32[2,2,4096]{2,1,0:T(2,128)S(1)} %slice.6), channel_id=1, source_target_pairs={{0,1},{1,0},{2,3},{3,2},{4,5},{5,4},{6,7},{7,6},{8,9},{9,8},{10,11... | collective-permute-start | bytes 196616 | tf_op jit(solution)/shard_map/ppermute | solution.py:341
  7.4 0.1 collective-permute-start.4
  7.5 1.1 %next_templates.1 = (f32[3,23,64,128]{3,2,1,0:T(8,128)S(1)}, f32[3,24,128]{2,1,0:T(8,128)S(1)}, f32[3,24,128]{2,1,0:T(8,128)S(1)}) custom-call(f32[3,64,128]{2,1,0:T(8,128)S(1)} %bitcast.40, f32[2112,128]{1,0:T(8,128)S(1)} %get-tuple-element.20.refs_1_.refs_2_, bf16[16,256,128]{2,1,0:T(8,128)(2,1)S(1)} %copy-done, f32[32,128]{1,0:T(8,128)S(1)} %bitcast.42, ...), custom_call_target="tpu_custom_call" | custom-call | flops 1 | bytes 1 | tf_op jit(solution)/shard_map/next_templates/pallas_call | solution.py:418
  8.6 0.0 collective-permute-done.4
  8.6 0.0 collective-permute-done.3
  8.6 1.4 %mid_templates.1 = (f32[3,23,64,128]{3,2,1,0:T(8,128)S(1)}, f32[3,24,128]{2,1,0:T(8,128)S(1)}, f32[3,24,128]{2,1,0:T(8,128)S(1)}, f32[32,128]{1,0:T(8,128)S(1)}) custom-call(f32[2,64,128]{2,1,0:T(8,128)S(1)} %bitcast.46, f32[1,64,128]{2,1,0:T(8,128)S(1)} %bitcast.47, f32[2112,128]{1,0:T(8,128)S(1)} %get-tuple-element.20.refs_1_.refs_2_, ...), custom_call_target="tpu_custom_call" | custom-call | flops 1 | bytes 1 | tf_op jit(solution)/shard_map/mid_templates/pallas_call | solution.py:418
  10.0 0.0 collective-permute-done
  10.0 1.7 %last_templates.1 = (f32[16,128]{1,0:T(8,128)S(1)}, f32[16,128]{1,0:T(8,128)S(1)}, f32[16,128]{1,0:T(8,128)S(1)}, f32[16,128]{1,0:T(8,128)S(1)}) custom-call(f32[3,64,128]{2,1,0:T(8,128)S(1)} %bitcast.45, f32[2112,128]{1,0:T(8,128)S(1)} %get-tuple-element.20.refs_1_.refs_2_, bf16[16,256,128]{2,1,0:T(8,128)(2,1)S(1)} %copy-done, f32[32,128]{1,0:T(8,128)S(1)} %bitcast.44, ...), custom_call_target="tpu_custom_call" | custom-call | flops 1000000000 | bytes 4000000 | tf_op jit(solution)/shard_map/last_templates/pallas_call | solution.py:435
  11.8 2.7 %collective-permute-start.5 = (f32[16,128]{1,0:T(8,128)S(1)}, f32[16,128]{1,0:T(8,128)S(1)}, u32[]{:S(2)}, u32[]{:S(2)}) collective-permute-start(f32[16,128]{1,0:T(8,128)S(1)} %get-tuple-element.32), channel_id=1, source_target_pairs={{0,5},{1,4},{2,7},{3,6},{4,1},{5,0},{6,3},{7,2},{8,13},{9,12},{10,... | collective-permute-start | bytes 24584 | tf_op jit(solution)/shard_map/ppermute | solution.py:341
  14.4 1.1 %collective-permute-start.6 = (f32[16,128]{1,0:T(8,128)S(1)}, f32[16,128]{1,0:T(8,128)S(1)}, u32[]{:S(2)}, u32[]{:S(2)}) collective-permute-start(f32[16,128]{1,0:T(8,128)S(1)} %get-tuple-element.33), channel_id=1, source_target_pairs={{0,7},{1,6},{2,5},{3,4},{4,3},{5,2},{6,1},{7,0},{8,15},{9,14},{10,... | collective-permute-start | bytes 24584 | tf_op jit(solution)/shard_map/ppermute | solution.py:341
  15.5 0.2 collective-permute-start.7
  15.7 0.1 collective-permute-done.5.refs_0_
  15.8 3.5 %collective-permute-done.6.refs_1_ = f32[16,128]{1,0:T(8,128)S(1)} collective-permute-done((f32[16,128]{1,0:T(8,128)S(1)}, f32[16,128]{1,0:T(8,128)S(1)}, u32[]{:S(2)}, u32[]{:S(2)}) %collective-permute-start.6) | collective-permute-done | bytes 8224 | tf_op jit(solution)/shard_map/ppermute | solution.py:341
  19.3 0.0 collective-permute-done.7.refs_2_
  19.3 0.7 %add_rows.1 = (f32[16,12]{1,0:T(8,128)}, f32[16,12]{1,0:T(8,128)}) custom-call(f32[16,128]{1,0:T(8,128)S(1)} %collective-permute-done.5.refs_0_, f32[16,128]{1,0:T(8,128)S(1)} %collective-permute-done.6.refs_1_, f32[16,128]{1,0:T(8,128)S(1)} %collective-permute-done.7.refs_2_, f32[16,128]{1,0:T(8,128)S(1)} %get-tuple-element.35.refs_3_), custom_call_target="tpu_custom_call" | custom-call | flops 100000 | bytes 4000000 | tf_op jit(solution)/shard_map/add_rows/pallas_call | solution.py:450
  (3 shorter events, 0.0 us)
Async XLA Ops:
  0.6 4.3 %copy-start = (bf16[16,256,128]{2,1,0:T(8,128)(2,1)S(1)}, bf16[16,256,128]{2,1,0:T(8,128)(2,1)}, u32[]{:S(2)}) copy-start(bf16[16,256,128]{2,1,0:T(8,128)(2,1)} %constant.2.clone.dft_ref.refs_2_.refs_3_) | copy-start | bytes 3145732
  0.6 4.3 %copy-start.4 = (bf16[32,2,4096]{2,1,0:T(2,128)(2,1)S(1)}, bf16[32,2,4096]{2,1,0:T(2,128)(2,1)}, u32[]{:S(2)}) copy-start(bf16[32,2,4096]{2,1,0:T(2,128)(2,1)} %param.7) | copy-start | bytes 1572868
  0.7 4.3 %copy-start.5 = (f32[3,2,4096]{2,1,0:T(2,128)S(1)}, f32[3,2,4096]{2,1,0:T(2,128)}, u32[]{:S(2)}) copy-start(f32[3,2,4096]{2,1,0:T(2,128)} %param.8) | copy-start | bytes 294916
  0.7 4.3 %copy-start.1 = (f32[2,2048]{1,0:T(2,128)S(1)}, f32[2,2048]{1,0:T(2,128)}, u32[]{:S(2)}) copy-start(f32[2,2048]{1,0:T(2,128)} %param.9) | copy-start | bytes 49156
  0.7 4.3 %copy-start.3 = (s32[1,8]{1,0:T(1,128)S(1)}, s32[1,8]{1,0:T(1,128)}, u32[]{:S(2)}) copy-start(s32[1,8]{1,0:T(1,128)} %refs_7_.1) | copy-start | bytes 100
  0.7 4.3 %copy-start.2 = (s32[1,8]{1,0:T(1,128)S(1)}, s32[1,8]{1,0:T(1,128)}, u32[]{:S(2)}) copy-start(s32[1,8]{1,0:T(1,128)} %refs_6_.1) | copy-start | bytes 100
  0.7 4.3 %copy-start.6 = (s32[12,9]{1,0:T(8,128)S(1)}, s32[12,9]{1,0:T(8,128)}, u32[]{:S(2)}) copy-start(s32[12,9]{1,0:T(8,128)} %edge_ref.1) | copy-start | bytes 1300
  0.7 4.3 %collective-permute-start.2 = (bf16[32,2,4096]{2,1,0:T(2,128)(2,1)}, bf16[32,2,4096]{2,1,0:T(2,128)(2,1)S(1)}, u32[]{:S(2)}, u32[]{:S(2)}) collective-permute-start(bf16[32,2,4096]{2,1,0:T(2,128)(2,1)} %param.7), channel_id=1, source_target_pairs={{0,1},{1,0},{2,3},{3,2},{4,5},{5,4},{6,7},{7,6},{8,9},{9,8},{10,11... | collective-permute-start | bytes 1572872 | tf_op jit(solution)/shard_map/ppermute | solution.py:341
  1.2 5.6 %collective-permute-start.1 = (f32[3,2,4096]{2,1,0:T(2,128)}, f32[3,2,4096]{2,1,0:T(2,128)S(1)}, u32[]{:S(2)}, u32[]{:S(2)}) collective-permute-start(f32[3,2,4096]{2,1,0:T(2,128)} %param.8), channel_id=1, source_target_pairs={{17,0},{8,1},{19,2},{10,3},{21,4},{12,5},{23,6},{14,7},{25,8},{0,9... | collective-permute-start | bytes 294920 | tf_op jit(solution)/shard_map/ppermute | solution.py:378
  3.8 6.2 %collective-permute-start = (f32[3,2,4096]{2,1,0:T(2,128)}, f32[3,2,4096]{2,1,0:T(2,128)S(1)}, u32[]{:S(2)}, u32[]{:S(2)}) collective-permute-start(f32[3,2,4096]{2,1,0:T(2,128)} %param.8), channel_id=1, source_target_pairs={{25,0},{24,1},{27,2},{26,3},{29,4},{28,5},{31,6},{30,7},{17,8},{16... | collective-permute-start | bytes 294920 | tf_op jit(solution)/shard_map/ppermute | solution.py:378
  6.9 1.8 %collective-permute-start.3 = (f32[2,2,4096]{2,1,0:T(2,128)S(1)}, f32[2,2,4096]{2,1,0:T(2,128)S(1)}, u32[]{:S(2)}, u32[]{:S(2)}) collective-permute-start(f32[2,2,4096]{2,1,0:T(2,128)S(1)} %slice.6), channel_id=1, source_target_pairs={{0,1},{1,0},{2,3},{3,2},{4,5},{5,4},{6,7},{7,6},{8,9},{9,8},{10,11... | collective-permute-start | bytes 196616 | tf_op jit(solution)/shard_map/ppermute | solution.py:341
  7.4 1.2 %collective-permute-start.4 = (f32[1,2,4096]{2,1,0:T(2,128)S(1)}, f32[1,2,4096]{2,1,0:T(2,128)S(1)}, u32[]{:S(2)}, u32[]{:S(2)}) collective-permute-start(f32[1,2,4096]{2,1,0:T(2,128)S(1)} %slice.7), channel_id=1, source_target_pairs={{0,1},{1,0},{2,3},{3,2},{4,5},{5,4},{6,7},{7,6},{8,9},{9,8},{10,11... | collective-permute-start | bytes 98312 | tf_op jit(solution)/shard_map/ppermute | solution.py:341
  11.8 4.0 %collective-permute-start.5 = (f32[16,128]{1,0:T(8,128)S(1)}, f32[16,128]{1,0:T(8,128)S(1)}, u32[]{:S(2)}, u32[]{:S(2)}) collective-permute-start(f32[16,128]{1,0:T(8,128)S(1)} %get-tuple-element.32), channel_id=1, source_target_pairs={{0,5},{1,4},{2,7},{3,6},{4,1},{5,0},{6,3},{7,2},{8,13},{9,12},{10,... | collective-permute-start | bytes 24584 | tf_op jit(solution)/shard_map/ppermute | solution.py:341
  14.4 4.9 %collective-permute-start.6 = (f32[16,128]{1,0:T(8,128)S(1)}, f32[16,128]{1,0:T(8,128)S(1)}, u32[]{:S(2)}, u32[]{:S(2)}) collective-permute-start(f32[16,128]{1,0:T(8,128)S(1)} %get-tuple-element.33), channel_id=1, source_target_pairs={{0,7},{1,6},{2,5},{3,4},{4,3},{5,2},{6,1},{7,0},{8,15},{9,14},{10,... | collective-permute-start | bytes 24584 | tf_op jit(solution)/shard_map/ppermute | solution.py:341
  15.5 3.8 %collective-permute-start.7 = (f32[16,128]{1,0:T(8,128)S(1)}, f32[16,128]{1,0:T(8,128)S(1)}, u32[]{:S(2)}, u32[]{:S(2)}) collective-permute-start(f32[16,128]{1,0:T(8,128)S(1)} %get-tuple-element.34), channel_id=1, source_target_pairs={{0,3},{1,2},{2,1},{3,0},{4,7},{5,6},{6,5},{7,4},{8,11},{9,10},{10,... | collective-permute-start | bytes 24584 | tf_op jit(solution)/shard_map/ppermute | solution.py:341
